TPU v7x, 32 devices: a whole 2x2x4 slice. The times are simulated.
32 devices in a mesh: tm: 8 (over z, y), pix: 2 (over x), pb: 2 (over core).
Axes of the slice: x: 2, y: 2, z: 4, core: 2. Of those that a mesh axis runs over, the one named last changes fastest.
Arguments:
- frames: bfloat16 [2, 512, 65536], P('pb', 'tm', 'pix'), may hold values from 0.05 to 15, as said below
- annulus_label: int32 [2, 65536], P('pb', 'pix'), may hold values from 0 to 3, as said below
- lag_width: int32 [2, 4], P('pb'), may hold values from 32 to 128, as said below
Outputs:
- correlation: float32 [2, 4, 512, 128], P('pb', None, 'tm', 'pix')
Inputs may be any that keep to these rules, and one draw needn't show every extreme that they name: `frames`: intensities are positive. `annulus_label`: each annulus label is held by exactly 16384 pixels of every band. `lag_width`: some entry equals 128 in every draw.
All inputs are finite; a program needn't handle non-finite values.
Results may differ from a plain program's by a relative error of at most 0.0003.
Values may be sent and summed in bfloat16 or wider, within the bound.
No kernel may reach another device: no remote copies, remote signals or barrier semaphores. Data moves between devices by JAX's collectives and lax.ppermute only.
A program may use at most 64 MiB of HBM per device.

v0:
```python
import jax
import jax.numpy as jnp
from jax import lax
from jax.sharding import PartitionSpec as P

DELAYS_STORED = 128
PIX = 65536
RADII_IN_GROUP = 4


def from_behind(block, axis, distance):
    devices = range(lax.axis_size(axis))
    route = [(i - distance, i) for i in devices if i - distance in devices]
    return lax.ppermute(block, axis, route)


def skewed(block, lag_count):
    lead = block.shape[:-2]
    rows, width = (block.shape[-2], block.shape[-1])
    flat = block.reshape(lead + (rows * width,))
    flat = jnp.pad(flat, [(0, 0)] * len(lead) + [(0, rows)])
    return flat.reshape(lead + (rows, width + 1))[..., :lag_count]


def shards(frames, annulus_label, lag_width):
    band_count, frame_count, pixel_count = frames.shape
    block_reach = (DELAYS_STORED + frame_count - 2) // frame_count
    labels = lax.broadcasted_iota(jnp.int32, (1, RADII_IN_GROUP, 1), 1)
    onehot = (annulus_label[:, None, :] == labels).astype(jnp.bfloat16)
    masked = frames[:, None, :, :] * onehot[:, :, None, :]

    def gram_tile(neighbour):
        return jnp.einsum("brtp,bsp->brts", masked, neighbour, preferred_element_type=jnp.float32)

    def annulus_sums(neighbour):
        return jnp.einsum("brp,bsp->brs", onehot, neighbour, preferred_element_type=jnp.float32)

    tile_list = [gram_tile(frames)]
    sum_list = [annulus_sums(frames)]
    for offset in range(1, block_reach + 1):
        neighbour = from_behind(frames, "tm", -offset)
        tile_list.append(gram_tile(neighbour))
        sum_list.append(annulus_sums(neighbour))
    joined = jnp.concatenate(tile_list, axis=3)
    sums_part = jnp.concatenate(sum_list, axis=2)
    banded = skewed(joined, DELAYS_STORED)
    half_lags = DELAYS_STORED // lax.axis_size("pix")
    lag_start = lax.axis_index("pix") * half_lags
    band_part = lax.psum_scatter(banded, "pix", scatter_dimension=3, tiled=True)
    sums_total = lax.psum(sums_part, "pix")
    window_width = sums_total.shape[2]
    spread_sums = jnp.broadcast_to(
        sums_total[:, :, None, :], (band_count, RADII_IN_GROUP, frame_count, window_width)
    )
    far_all = skewed(spread_sums, DELAYS_STORED)
    far_sums = lax.dynamic_slice_in_dim(far_all, lag_start, half_lags, 3)
    own_sums = sums_total[:, :, :frame_count][..., None]
    row_ids = lax.broadcasted_iota(jnp.int32, (frame_count, half_lags), 0)
    lag_ids = lag_start + lax.broadcasted_iota(jnp.int32, (frame_count, half_lags), 1)
    global_rows = lax.axis_index("tm") * frame_count + row_ids
    frame_total = frame_count * lax.axis_size("tm")
    valid = (lag_ids[None, None] < lag_width[:, :, None, None]) & (
        global_rows + lag_ids < frame_total
    )[None, None]
    denominator = jnp.where(valid, own_sums * far_sums, 1.0)
    annulus_size = PIX // RADII_IN_GROUP
    return jnp.where(valid, annulus_size * band_part / denominator, 0.0)


def solution(mesh):
    return jax.shard_map(
        shards,
        mesh=mesh,
        in_specs=(P("pb", "tm", "pix"), P("pb", "pix"), P("pb", None)),
        out_specs=P("pb", None, "tm", "pix"),
        check_vma=False,
    )
```

profile of v0, /device:TPU:0, one launch (start us, length us, event | category | flops | bytes accessed | tf_op | source)
XLA Modules:
  0.0 220.2 jit_solution(16541784850528195049)
XLA Ops:
  6.5 0.0 reduce-scatter.4.cloned.1.call-start
  6.5 1.3 collective-permute-start.1
  7.8 1.3 collective-permute-start
  9.1 1.0 fusion.40
  10.2 0.0 copy-start
  10.2 0.1 add_compare_fusion
  10.3 3.6 %convolution_bitcast_fusion = f32[1,4,64]{2,1,0:T(4,128)S(1)} fusion(s32[32768]{0:T(1024)} %bitcast.53, bf16[1,64,32768]{2,1,0:T(8,128)(2,1)} %param.3), kind=kOutput, calls=%fused_computation.24 | convolution fusion | flops 16908288 | bytes 4326400 | tf_op jit(solution)/shard_map/brp,bsp->brs/dot_general | solution.py:36
  13.8 0.0 copy-done
  13.8 4.5 %fusion.19 = f32[1,4,64,64]{3,2,1,0:T(8,128)S(1)} fusion(bf16[1,64,32768]{2,1,0:T(8,128)(2,1)S(1)} %copy-done, bf16[4,32768]{1,0:T(4,128)(2,1)S(1)} %fusion.40, bf16[64,32768]{1,0:T(8,128)(2,1)S(1)} %bitcast.49), kind=kOutput, calls=%fused_computation.19 | convolution fusion | flops 1082130432 | bytes 8716288 | tf_op jit(solution)/shard_map/brtp,bsp->brts/dot_general | solution.py:33
  18.3 84.8 %collective-permute-done.1 = bf16[1,64,32768]{2,1,0:T(8,128)(2,1)} collective-permute-done((bf16[1,64,32768]{2,1,0:T(8,128)(2,1)}, bf16[1,64,32768]{2,1,0:T(8,128)(2,1)}, u32[]{:S(2)}, u32[]{:S(2)}) %collective-permute-start.1) | collective-permute-done | bytes 4194336 | tf_op jit(solution)/shard_map/ppermute | solution.py:14
  103.2 6.6 %fusion.29 = f32[1,4,64,64]{3,2,1,0:T(8,128)S(1)} fusion(bf16[1,64,32768]{2,1,0:T(8,128)(2,1)} %collective-permute-done.1, bf16[4,32768]{1,0:T(4,128)(2,1)S(1)} %fusion.40, bf16[64,32768]{1,0:T(8,128)(2,1)S(1)} %bitcast.50), kind=kOutput, calls=%fused_computation.21 | convolution fusion | flops 1082130432 | bytes 8716288 | tf_op jit(solution)/shard_map/brtp,bsp->brts/dot_general | solution.py:33
  109.8 0.0 copy-start.1
  109.8 0.0 collective-permute-done
  109.8 6.7 %fusion.24 = f32[1,4,64,64]{3,2,1,0:T(8,128)S(1)} fusion(bf16[1,64,32768]{2,1,0:T(8,128)(2,1)} %collective-permute-done, bf16[4,32768]{1,0:T(4,128)(2,1)S(1)} %fusion.40, bf16[64,32768]{1,0:T(8,128)(2,1)S(1)} %bitcast.51), kind=kOutput, calls=%fused_computation.20 | convolution fusion | flops 1082130432 | bytes 8716288 | tf_op jit(solution)/shard_map/brtp,bsp->brts/dot_general | solution.py:33
  116.5 0.1 pad_maximum_fusion
  116.7 0.2 reshape.149
  116.9 0.5 reshape.150
  117.4 0.2 copy.4
  117.5 0.9 reshape.155
  118.4 0.0 reduce-scatter.4.cloned.1.call-update
  118.4 0.0 copy-done.1
  118.4 3.4 %fusion.37 = f32[1,4,64]{2,1,0:T(4,128)S(1)} fusion(bf16[1,64,32768]{2,1,0:T(8,128)(2,1)} %collective-permute-done.1, s32[32768]{0:T(1024)S(1)} %bitcast.54), kind=kOutput, calls=%fused_computation.23 | convolution fusion | flops 16908288 | bytes 4326400 | tf_op jit(solution)/shard_map/brp,bsp->brs/dot_general | solution.py:36
  121.8 3.4 %fusion.34 = f32[1,4,64]{2,1,0:T(4,128)S(1)} fusion(bf16[1,64,32768]{2,1,0:T(8,128)(2,1)} %collective-permute-done, s32[32768]{0:T(1024)S(1)} %bitcast.55), kind=kOutput, calls=%fused_computation.22 | convolution fusion | flops 16908288 | bytes 4326400 | tf_op jit(solution)/shard_map/brp,bsp->brs/dot_general | solution.py:36
  125.2 0.1 pad_maximum_fusion.1
  125.3 4.9 %psum.7 = f32[1,4,192]{2,1,0:T(4,128)S(1)} all-reduce(f32[1,4,192]{2,1,0:T(4,128)S(1)} %pad_maximum_fusion.1), channel_id=1, replica_groups=mesh['tm'=8,'pix'=2,'pb'=2] {'pix'}, use_global_device_ids=true, to_apply=%region_1.2 | all-reduce | flops 768 | bytes 6144 | tf_op jit(solution)/shard_map/psum | solution.py:50
  130.2 0.2 broadcast_in_dim.26
  130.4 0.3 reshape.151
  130.8 80.7 %reduce-scatter.4.cloned.1.call-done = f32[64,256]{1,0:T(8,128)} async-done(((f32[128,256]{1,0:T(8,128)}), f32[64,256]{1,0:T(8,128)}) %reduce-scatter.4.cloned.1.call-update) | async-done | bytes 65552
  211.5 0.9 reshape.156
  212.4 0.1 copy.5
  212.6 0.0 copy-done.2
  212.6 0.8 divide_select_fusion
  (8 shorter events, 0.1 us)
Async XLA Ops:
  6.5 205.0 %reduce-scatter.4.cloned.1.call-start = ((), (), s32[]{:S(2)}) async-start(), calls=%async_computation.1 | async-start | bytes 196608
  6.5 96.6 %collective-permute-start.1 = (bf16[1,64,32768]{2,1,0:T(8,128)(2,1)}, bf16[1,64,32768]{2,1,0:T(8,128)(2,1)}, u32[]{:S(2)}, u32[]{:S(2)}) collective-permute-start(bf16[1,64,32768]{2,1,0:T(8,128)(2,1)} %param.3), channel_id=1, source_target_pairs={{8,0},{12,4},{16,8},{20,12},{24,16},{28,20},{9,1},{13,5},{17,9},{2... | collective-permute-start | bytes 12582920 | tf_op jit(solution)/shard_map/ppermute | solution.py:14
  7.8 102.0 %collective-permute-start = (bf16[1,64,32768]{2,1,0:T(8,128)(2,1)}, bf16[1,64,32768]{2,1,0:T(8,128)(2,1)}, u32[]{:S(2)}, u32[]{:S(2)}) collective-permute-start(bf16[1,64,32768]{2,1,0:T(8,128)(2,1)} %param.3), channel_id=1, source_target_pairs={{4,0},{8,4},{12,8},{16,12},{20,16},{24,20},{28,24},{5,1},{9,5},{13... | collective-permute-start | bytes 12582920 | tf_op jit(solution)/shard_map/ppermute | solution.py:14
  10.2 3.7 %copy-start = (bf16[1,64,32768]{2,1,0:T(8,128)(2,1)S(1)}, bf16[1,64,32768]{2,1,0:T(8,128)(2,1)}, u32[]{:S(2)}) copy-start(bf16[1,64,32768]{2,1,0:T(8,128)(2,1)} %param.3) | copy-start | bytes 12582916
  109.8 8.6 %copy-start.1 = (s32[1,32768]{1,0:T(1,128)S(1)}, s32[1,32768]{1,0:T(1,128)}, u32[]{:S(2)}) copy-start(s32[1,32768]{1,0:T(1,128)} %param.4) | copy-start | bytes 393220
  121.8 90.8 %copy-start.2 = (s32[1,4]{1,0:T(1,128)S(1)}, s32[1,4]{1,0:T(1,128)}, u32[]{:S(2)}) copy-start(s32[1,4]{1,0:T(1,128)} %param.5) | copy-start | bytes 52
Sparse Core Ops, SparseCore 0:
  118.5 92.9 reduce-scatter.3
where the time goes:
time: 221 us; the launch traced here: 220 us
  waiting for transfers between devices  166 us (75%)
  matrix products  28.1 us (13%)
  between operations  13.6 us (6%)
  blocking collectives  4.93 us (2%)
  local copies, waits for them, and re-layouts  3.27 us (1%)
  starting transfers between devices  2.57 us (1%)
    ppermute x2, waiting for transfers between devices, from_behind(): return lax.ppermute(block, axis, route)  84.8 us
    unnamed x2, waiting for transfers between devices  80.8 us
    dot_general x3, matrix products, gram_tile(): jnp.einsum('brtp,bsp->brts', masked, neighbour, preferred_element_type=jn...  17.8 us
    dot_general x3, matrix products, annulus_sums(): jnp.einsum('brp,bsp->brs', onehot, neighbour, preferred_element_type=jnp....  10.3 us
    psum x1, blocking collectives, shards(): sums_total = lax.psum(sums_part, 'pix')  4.93 us
  transfers between devices with their start and end apart: 3, of which 2 were waited for; matrix products, arithmetic and copies ran while one was open for 11% of the time, Pallas kernels for 0%

commit v1 on v0

v1 whole, which is shorter than its diff:
```python
import functools

import jax
import jax.numpy as jnp
from jax import lax
from jax.experimental import pallas as pl
from jax.experimental.pallas import tpu as pltpu
from jax.sharding import PartitionSpec as P

DELAYS_STORED = 128
PIX = 65536
RADII = 4
ROWS = 64
UNITS = 16
PIECES = ((0, 8), (8, 6), (14, 2))
NT = (((1,), (1,)), ((), ()))


def packed(tile):
    half = tile.shape[0] // 2
    return jnp.concatenate([tile[:half], tile[half:]], axis=1)


def masked_by_annulus(block, label):
    return [block * (label == a).astype(block.dtype) for a in range(RADII)]


def sums_of(label, columns):
    ids = lax.broadcasted_iota(jnp.int32, (8, label.shape[1]), 0)
    onehot = (label == ids).astype(jnp.float32).astype(columns.dtype)
    return lax.dot_general(onehot, columns, NT, preferred_element_type=jnp.float32)


def own_kernel(steps, frames_ref, label_ref, out_ref, acc, acc_sums):
    step = pl.program_id(0)

    @pl.when(step == 0)
    def _():
        acc[...] = jnp.zeros_like(acc)
        acc_sums[...] = jnp.zeros_like(acc_sums)

    block = frames_ref[0]
    label = label_ref[...]
    rows = jnp.concatenate(masked_by_annulus(block, label), axis=0)
    acc[...] += lax.dot_general(rows, block, NT, preferred_element_type=jnp.float32)
    acc_sums[...] += sums_of(label, block)

    @pl.when(step == steps - 1)
    def _():
        tile = acc[...]
        t = lax.rem(lax.broadcasted_iota(jnp.int32, tile.shape, 0), ROWS)
        below = lax.broadcasted_iota(jnp.int32, tile.shape, 1) < t
        out_ref[: 2 * ROWS] = packed(jnp.where(below, 0.0, tile))
        sums = acc_sums[...]
        out_ref[2 * ROWS :] = jnp.concatenate([sums, sums], axis=1)


def cost(pixels, rows, columns):
    return pl.CostEstimate(
        flops=2 * rows * columns * pixels, bytes_accessed=2 * columns * pixels, transcendentals=0
    )


def own_part(frames, label):
    pixels = frames.shape[2]
    width = pixels // 8
    steps = pixels // width
    shape = (2 * ROWS + 8, 128)
    return pl.pallas_call(
        functools.partial(own_kernel, steps),
        grid=(steps,),
        in_specs=[
            pl.BlockSpec((1, ROWS, width), lambda k: (0, 0, k)),
            pl.BlockSpec((1, width), lambda k: (0, k)),
        ],
        out_specs=pl.BlockSpec(shape, lambda k: (0, 0)),
        out_shape=jax.ShapeDtypeStruct(shape, jnp.float32),
        scratch_shapes=[
            pltpu.VMEM((RADII * ROWS, ROWS), jnp.float32),
            pltpu.VMEM((8, ROWS), jnp.float32),
        ],
        compiler_params=pltpu.CompilerParams(vmem_limit_bytes=16 << 20),
        cost_estimate=cost(pixels, 512, 256),
        name="own_tile_and_sums",
    )(frames, label)


def chunk_kernel(steps, first, last, place_ref, own_ref, label_ref, near_ref, far_ref, *refs):
    if not first:
        before_ref, before_sums_ref, *refs = refs
    *out_refs, acc, acc_sums = refs
    step = pl.program_id(0)

    @pl.when(step == 0)
    def _():
        acc[...] = jnp.zeros_like(acc) if first else before_ref[...]
        acc_sums[...] = jnp.zeros_like(acc_sums) if first else before_sums_ref[...]

    later = place_ref[0] == 1
    own, near, far = own_ref[0], near_ref[0], far_ref[0]
    earliest = jnp.where(later, far, own)
    latest = jnp.where(later, own, far)
    label = label_ref[...]
    rows = jnp.concatenate(masked_by_annulus(earliest, label) + masked_by_annulus(near, label), axis=0)
    columns = jnp.concatenate([near, latest], axis=0)
    acc[...] += lax.dot_general(rows, columns, NT, preferred_element_type=jnp.float32)
    acc_sums[...] += sums_of(label, columns)

    @pl.when(step == steps - 1)
    def _():
        if not last:
            out_refs[0][...] = acc[...]
            out_refs[1][...] = acc_sums[...]
            return
        half = RADII * ROWS
        shape = (half, ROWS)
        t = lax.rem(lax.broadcasted_iota(jnp.int32, shape, 0), ROWS)
        below = lax.broadcasted_iota(jnp.int32, shape, 1) < t
        near_tile = acc[:half, :ROWS]
        far_tile = acc[:half, ROWS:]
        next_tile = acc[half:, ROWS:]
        second = place_ref[1] == 1
        here = (jnp.where(below, near_tile, 0.0), jnp.where(below, far_tile, near_tile))
        after = (jnp.where(below, next_tile, 0.0), jnp.where(below, 0.0, next_tile))
        sums = acc_sums[...]
        lane = lax.broadcasted_iota(jnp.int32, sums.shape, 1)
        after_sums = jnp.where(lane < ROWS, pltpu.roll(sums, ROWS, 1), 0.0)
        for k, ((low, high), row) in enumerate(((here, sums), (after, after_sums))):
            out_refs[2 * k][: 2 * ROWS] = packed(jnp.where(second, high, low))
            out_refs[2 * k + 1][: 2 * ROWS] = packed(jnp.where(second, low, high))
            out_refs[2 * k][2 * ROWS :] = row
            out_refs[2 * k + 1][2 * ROWS :] = row


def chunk_part(place, piece, label, start, near, far, before, last):
    size = near.shape[2]
    width = size // max(1, size // (label.shape[1] // 8))
    steps, offset = size // width, start // width
    acc_shape, sums_shape = (2 * RADII * ROWS, 2 * ROWS), (8, 2 * ROWS)
    message = (2 * ROWS + 8, 2 * ROWS)

    def whole(shape):
        return pl.BlockSpec(shape, lambda k: (0, 0))

    block = pl.BlockSpec((1, ROWS, width), lambda k: (0, 0, k))
    in_specs = [
        pl.BlockSpec(memory_space=pltpu.SMEM),
        block,
        pl.BlockSpec((1, width), lambda k: (0, k + offset)),
        block,
        block,
    ]
    operands = [place, piece, label, near, far]
    if before is not None:
        in_specs += [whole(acc_shape), whole(sums_shape)]
        operands += before
    shapes = [message] * 4 if last else [acc_shape, sums_shape]
    return pl.pallas_call(
        functools.partial(chunk_kernel, steps, before is None, last),
        grid=(steps,),
        in_specs=in_specs,
        out_specs=[whole(shape) for shape in shapes],
        out_shape=[jax.ShapeDtypeStruct(shape, jnp.float32) for shape in shapes],
        scratch_shapes=[pltpu.VMEM(acc_shape, jnp.float32), pltpu.VMEM(sums_shape, jnp.float32)],
        compiler_params=pltpu.CompilerParams(vmem_limit_bytes=16 << 20),
        cost_estimate=cost(size, 1024, 256),
        name="chunk_tiles",
    )(*operands)


def final_kernel(place_ref, factor_ref, own_ref, kept_ref, *refs):
    *message_refs, out_ref = refs
    total = jnp.where(place_ref[0] == 0, kept_ref[...], 0.0)
    for ref in message_refs:
        total = total + ref[...]
    own = own_ref[...]
    first = place_ref[1] == 0
    tile = total[: 2 * ROWS] + jnp.where(first, own[: 2 * ROWS], 0.0)
    ahead, present = total[2 * ROWS :], own[2 * ROWS :]
    lane = lax.broadcasted_iota(jnp.int32, ahead.shape, 1)
    moved = pltpu.roll(ahead, ROWS, 1)
    same = jnp.where(first, present, jnp.where(lane < ROWS, ahead, moved))
    beyond = jnp.where(first == (lane < ROWS), ahead, moved)
    t = lax.rem(lax.broadcasted_iota(jnp.int32, tile.shape, 0), ROWS)
    s = lax.rem(lax.broadcasted_iota(jnp.int32, tile.shape, 1), ROWS)

    def spread(row):
        pairs = [jnp.where(lane[:1] < ROWS, row[a : a + 1], row[2 + a : 3 + a]) for a in range(2)]
        return jnp.concatenate([jnp.broadcast_to(pair, (ROWS, 2 * ROWS)) for pair in pairs], axis=0)

    far = jnp.where(s < t, spread(beyond), spread(same))
    factor = factor_ref[...]
    tile = jnp.where(factor > 0.0, tile * factor / far, 0.0)
    for group in range(2):
        part = tile[:, group * ROWS : (group + 1) * ROWS]
        twice = jnp.concatenate([part, part], axis=1)
        for bit in range(6):
            turned = pltpu.roll(twice, 128 - (1 << bit), 1)
            twice = jnp.where((t >> bit) & 1 == 1, turned, twice)
        for a in range(2):
            out_ref[0, 2 * group + a] = twice[a * ROWS : (a + 1) * ROWS, :ROWS]


def final_part(place, factor, own, kept, messages):
    vmem = pl.BlockSpec(memory_space=pltpu.VMEM)
    return pl.pallas_call(
        final_kernel,
        in_specs=[pl.BlockSpec(memory_space=pltpu.SMEM)] + [vmem] * (3 + len(messages)),
        out_specs=vmem,
        out_shape=jax.ShapeDtypeStruct((1, RADII, ROWS, ROWS), jnp.float32),
        compiler_params=pltpu.CompilerParams(vmem_limit_bytes=16 << 20),
        name="normalise_and_skew",
    )(place, factor, own, kept, *messages)


def factors(own, lag_width):
    tm, pix = lax.axis_index("tm"), lax.axis_index("pix")
    devices = lax.axis_size("tm")
    t = lax.broadcasted_iota(jnp.int32, (RADII, ROWS, ROWS), 1)
    s = lax.broadcasted_iota(jnp.int32, (RADII, ROWS, ROWS), 2)
    lag = jnp.where(s >= t, s - t, s - t + ROWS) + pix * ROWS
    valid = (lag < lag_width[0][:, None, None]) & (tm * ROWS + t + lag < devices * ROWS)
    annulus_size = PIX // RADII
    result = jnp.where(valid, annulus_size / own[:, :, None], 0.0)
    return packed(result.reshape(RADII * ROWS, ROWS))


def shards(frames, annulus_label, lag_width):
    devices = lax.axis_size("tm")
    pixels = frames.shape[2]
    pb, pix = lax.axis_index("pb"), lax.axis_index("pix")
    place = jnp.stack([pb, pix]).astype(jnp.int32)

    def far_pairs():
        for i in range(devices):
            for band, target in ((0, i - 2), (1, i + 2)):
                if 0 <= target < devices:
                    yield 2 * i + band, 2 * target + band

    def near_pairs():
        for i in range(devices):
            band, target = (0, i - 1) if i % 2 else (1, i + 1)
            if target < devices:
                yield 2 * i + band, 2 * target + band

    tm_pb = ("tm", "pb")

    def sent(piece):
        far = lax.ppermute(piece, tm_pb, list(far_pairs()))
        near = lax.ppermute(piece, tm_pb, list(near_pairs()))
        return near, far

    unit = pixels // UNITS
    pieces = [
        lax.slice_in_dim(frames, begin * unit, (begin + count) * unit, axis=2) for begin, count in PIECES
    ]
    received = []
    for index, piece in enumerate(pieces):
        if index >= 2:
            piece, _ = lax.optimization_barrier((piece, received[index - 2]))
        received.append(sent(piece))

    own = own_part(frames, annulus_label)
    own = own + lax.ppermute(own, "pix", [(0, 1), (1, 0)])
    factor = factors(own[2 * ROWS : 2 * ROWS + RADII, :ROWS], lag_width)

    state = None
    for index, ((begin, _), piece, (near, far)) in enumerate(zip(PIECES, pieces, received)):
        last = index == len(pieces) - 1
        state = chunk_part(place, piece, annulus_label, begin * unit, near, far, state, last)
    here_same, here_other, after_same, after_other = state

    def message_pairs(step, flip):
        for i in range(devices):
            for band in range(2):
                target = i + step if band == 0 else i - 2 + step
                has_near = i % 2 == band
                if not 0 <= target < devices:
                    continue
                if (step and not has_near) or (not step and not flip and band == 0):
                    continue
                for x in range(2):
                    yield (i * 2 + x) * 2 + band, (target * 2 + (x ^ flip)) * 2 + band

    everywhere = ("tm", "pix", "pb")
    messages = [
        lax.ppermute(message, everywhere, list(message_pairs(step, flip)))
        for message, step, flip in (
            (here_same, 0, 0),
            (here_other, 0, 1),
            (after_same, 1, 0),
            (after_other, 1, 1),
        )
    ]
    return final_part(place, factor, own, here_same, messages)


def solution(mesh):
    return jax.shard_map(
        shards,
        mesh=mesh,
        in_specs=(P("pb", "tm", "pix"), P("pb", "pix"), P("pb", None)),
        out_specs=P("pb", None, "tm", "pix"),
        check_vma=False,
    )
```

time: 221 us -> 73.6 us (0.33)
  waiting for transfers between devices: 166 us -> 21.5 us
  matrix products: 28.1 us -> 0 us
  Pallas kernels: 0 us -> 24.3 us
  starting transfers between devices: 2.57 us -> 22.7 us
  between operations: 13.6 us -> 0.22 us
  blocking collectives: 4.93 us -> 0 us
    unnamed x2 -> x0, waiting for transfers between devices: 80.8 us -> none
    ppermute x2 -> x11, waiting for transfers between devices: 84.8 us -> 21.5 us  [the longest x3 14.1 us: sent(): near = lax.ppermute(piece, tm_pb, list(near_pairs()))]
    dot_general x6 -> x0, matrix products: 28.1 us -> none  [the longest x3 17.8 us: gram_tile(): jnp.einsum('brtp,bsp->brts', masked, neighbour, preferred_element_type=jn...]
    pallas_call x0 -> x5, Pallas kernels: none -> 24.3 us  [the longest x3 15.5 us: chunk_part(): pl.pallas_call(functools.partial(chunk_kernel, steps, before is None, las...]
    ppermute x2 -> x11, starting transfers between devices: 2.57 us -> 22.7 us  [the longest x4 11.7 us: shards(): lax.ppermute(message, everywhere, list(message_pairs(step, flip)))]
    psum x1 -> x0, blocking collectives: 4.93 us -> none  [shards(): sums_total = lax.psum(sums_part, 'pix')]
    slice x2 -> x4, local copies, waits for them, and re-layouts: 0.02 us -> 4.26 us  [the longest x3 4.25 us: shards(): lax.slice_in_dim(frames, begin * unit, (begin + count) * unit, axis=2)]
  transfers between devices with their start and end apart: 3 -> 11, of which waited for: 2 -> 6; matrix products, arithmetic and copies ran while one was open for 11% -> 4% of each run, Pallas kernels for 0% -> 28%
where the time goes in v1:
time: 73.6 us; the launch traced here: 73.2 us
  Pallas kernels  24.3 us (33%)
  starting transfers between devices  22.7 us (31%)
  waiting for transfers between devices  21.5 us (29%)
  local copies, waits for them, and re-layouts  4.27 us (6%)
    pallas_call x3, Pallas kernels, chunk_part(): pl.pallas_call(functools.partial(chunk_kernel, steps, before is None, las...  15.5 us
    ppermute x3, waiting for transfers between devices, sent(): near = lax.ppermute(piece, tm_pb, list(near_pairs()))  14.1 us
    ppermute x4, starting transfers between devices, shards(): lax.ppermute(message, everywhere, list(message_pairs(step, flip)))  11.7 us
    pallas_call x1, Pallas kernels, own_part(): pl.pallas_call(functools.partial(own_kernel, steps), grid=(steps,), in_sp...  7.02 us
    slice x3, local copies, waits for them, and re-layouts, shards(): lax.slice_in_dim(frames, begin * unit, (begin + count) * unit, axis=2)  4.25 us
    ppermute x3, starting transfers between devices, sent(): near = lax.ppermute(piece, tm_pb, list(near_pairs()))  4.12 us
    ppermute x3, waiting for transfers between devices, sent(): far = lax.ppermute(piece, tm_pb, list(far_pairs()))  3.97 us
    ppermute x3, starting transfers between devices, sent(): far = lax.ppermute(piece, tm_pb, list(far_pairs()))  3.88 us
  transfers between devices with their start and end apart: 11, of which 6 were waited for; matrix products, arithmetic and copies ran while one was open for 4% of the time, Pallas kernels for 28%

profile of v1, /device:TPU:0, one launch (start us, length us, event | category | flops | bytes accessed | tf_op | source)
XLA Modules:
  0.0 73.2 jit_solution(7819402969382547125)
XLA Ops:
  0.0 1.9 %slice.30.own_ref = bf16[1,64,16384]{2,1,0:T(8,128)(2,1)S(1)} slice(bf16[1,64,32768]{2,1,0:T(8,128)(2,1)} %frames_ref.1), slice={[0:1], [0:64], [0:16384]} | slice | bytes 4194304 | tf_op jit(solution)/shard_map/slice | solution.py:255
  1.9 0.0 copy-start.1
  1.9 1.4 %collective-permute-start.1 = (bf16[1,64,16384]{2,1,0:T(8,128)(2,1)S(1)}, bf16[1,64,16384]{2,1,0:T(8,128)(2,1)}, u32[]{:S(2)}, u32[]{:S(2)}) collective-permute-start(bf16[1,64,16384]{2,1,0:T(8,128)(2,1)S(1)} %slice.30.own_ref), channel_id=1, source_target_pairs={{1,5},{4,0},{9,13},{12,8},{17,21},{20,16},{25,29},{28,24},{3,7},{6... | collective-permute-start | bytes 6291464 | tf_op jit(solution)/shard_map/ppermute | solution.py:250
  3.3 1.3 %collective-permute-start.2 = (bf16[1,64,16384]{2,1,0:T(8,128)(2,1)S(1)}, bf16[1,64,16384]{2,1,0:T(8,128)(2,1)}, u32[]{:S(2)}, u32[]{:S(2)}) collective-permute-start(bf16[1,64,16384]{2,1,0:T(8,128)(2,1)S(1)} %slice.30.own_ref), channel_id=1, source_target_pairs={{1,9},{5,13},{8,0},{9,17},{12,4},{13,21},{16,8},{17,25},{20,12},{2... | collective-permute-start | bytes 6291464 | tf_op jit(solution)/shard_map/ppermute | solution.py:249
  4.6 1.3 %slice.31.own_ref = bf16[1,64,12288]{2,1,0:T(8,128)(2,1)} slice(bf16[1,64,32768]{2,1,0:T(8,128)(2,1)S(1)} %copy-done), slice={[0:1], [0:64], [16384:28672]} | slice | bytes 3145728 | tf_op jit(solution)/shard_map/slice | solution.py:255
  5.9 1.4 %collective-permute-start.5 = (bf16[1,64,12288]{2,1,0:T(8,128)(2,1)}, bf16[1,64,12288]{2,1,0:T(8,128)(2,1)}, u32[]{:S(2)}, u32[]{:S(2)}) collective-permute-start(bf16[1,64,12288]{2,1,0:T(8,128)(2,1)} %slice.31.own_ref), channel_id=1, source_target_pairs={{1,5},{4,0},{9,13},{12,8},{17,21},{20,16},{25,29},{28,24},{3,7},{6... | collective-permute-start | bytes 4718600 | tf_op jit(solution)/shard_map/ppermute | solution.py:250
  7.4 1.3 %collective-permute-start.6 = (bf16[1,64,12288]{2,1,0:T(8,128)(2,1)}, bf16[1,64,12288]{2,1,0:T(8,128)(2,1)}, u32[]{:S(2)}, u32[]{:S(2)}) collective-permute-start(bf16[1,64,12288]{2,1,0:T(8,128)(2,1)} %slice.31.own_ref), channel_id=1, source_target_pairs={{1,9},{5,13},{8,0},{9,17},{12,4},{13,21},{16,8},{17,25},{20,12},{2... | collective-permute-start | bytes 4718600 | tf_op jit(solution)/shard_map/ppermute | solution.py:249
  8.7 7.0 %own_tile_and_sums.1 = f32[136,128]{1,0:T(8,128)S(1)} custom-call(bf16[1,64,32768]{2,1,0:T(8,128)(2,1)S(1)} %copy-done, s32[1,32768]{1,0:T(1,128)S(1)} %copy-done.1), custom_call_target="tpu_custom_call" | custom-call | flops 8589934592 | bytes 16777216 | tf_op jit(solution)/shard_map/own_tile_and_sums/pallas_call | solution.py:69
  15.7 3.0 %collective-permute-start = (f32[136,128]{1,0:T(8,128)S(1)}, f32[136,128]{1,0:T(8,128)S(1)}, u32[]{:S(2)}, u32[]{:S(2)}) collective-permute-start(f32[136,128]{1,0:T(8,128)S(1)} %own_tile_and_sums.1), channel_id=1, source_target_pairs={{0,2},{2,0},{1,3},{3,1},{4,6},{6,4},{5,7},{7,5},{8,10},{10,8},{9,1... | collective-permute-start | bytes 208904 | tf_op jit(solution)/shard_map/ppermute | solution.py:264
  18.7 1.1 %slice.29.own_ref = bf16[1,64,4096]{2,1,0:T(8,128)(2,1)S(1)} slice(bf16[1,64,32768]{2,1,0:T(8,128)(2,1)} %frames_ref.1), slice={[0:1], [0:64], [28672:32768]} | slice | bytes 1048576 | tf_op jit(solution)/shard_map/slice | solution.py:255
  19.8 0.1 pad_add_fusion.place_ref
  19.9 1.1 %collective-permute-done = f32[136,128]{1,0:T(8,128)S(1)} collective-permute-done((f32[136,128]{1,0:T(8,128)S(1)}, f32[136,128]{1,0:T(8,128)S(1)}, u32[]{:S(2)}, u32[]{:S(2)}) %collective-permute-start) | collective-permute-done | bytes 69664 | tf_op jit(solution)/shard_map/ppermute | solution.py:264
  21.0 0.1 fusion.5
  21.2 9.2 %collective-permute-done.1.near_ref = bf16[1,64,16384]{2,1,0:T(8,128)(2,1)} collective-permute-done((bf16[1,64,16384]{2,1,0:T(8,128)(2,1)S(1)}, bf16[1,64,16384]{2,1,0:T(8,128)(2,1)}, u32[]{:S(2)}, u32[]{:S(2)}) %collective-permute-start.1) | collective-permute-done | bytes 2097184 | tf_op jit(solution)/shard_map/ppermute | solution.py:250
  30.4 2.0 %collective-permute-done.2.far_ref = bf16[1,64,16384]{2,1,0:T(8,128)(2,1)} collective-permute-done((bf16[1,64,16384]{2,1,0:T(8,128)(2,1)S(1)}, bf16[1,64,16384]{2,1,0:T(8,128)(2,1)}, u32[]{:S(2)}, u32[]{:S(2)}) %collective-permute-start.2) | collective-permute-done | bytes 2097184 | tf_op jit(solution)/shard_map/ppermute | solution.py:249
  32.4 1.3 %collective-permute-start.3 = (bf16[1,64,4096]{2,1,0:T(8,128)(2,1)S(1)}, bf16[1,64,4096]{2,1,0:T(8,128)(2,1)S(1)}, u32[]{:S(2)}, u32[]{:S(2)}) collective-permute-start(bf16[1,64,4096]{2,1,0:T(8,128)(2,1)S(1)} %slice.29.own_ref), channel_id=1, source_target_pairs={{1,5},{4,0},{9,13},{12,8},{17,21},{20,16},{25,29},{28,24},{3,7},{6... | collective-permute-start | bytes 1572872 | tf_op jit(solution)/shard_map/ppermute | solution.py:250
  33.7 1.3 %collective-permute-start.4 = (bf16[1,64,4096]{2,1,0:T(8,128)(2,1)S(1)}, bf16[1,64,4096]{2,1,0:T(8,128)(2,1)S(1)}, u32[]{:S(2)}, u32[]{:S(2)}) collective-permute-start(bf16[1,64,4096]{2,1,0:T(8,128)(2,1)S(1)} %slice.29.own_ref), channel_id=1, source_target_pairs={{1,9},{5,13},{8,0},{9,17},{12,4},{13,21},{16,8},{17,25},{20,12},{2... | collective-permute-start | bytes 1572872 | tf_op jit(solution)/shard_map/ppermute | solution.py:249
  35.0 7.4 %chunk_tiles.3 = (f32[512,128]{1,0:T(8,128)S(1)}, f32[8,128]{1,0:T(8,128)S(1)}) custom-call(s32[2]{0:T(128)S(1)} %pad_add_fusion.place_ref, bf16[1,64,16384]{2,1,0:T(8,128)(2,1)S(1)} %slice.30.own_ref, s32[1,32768]{1,0:T(1,128)S(1)} %copy-done.1, bf16[1,64,16384]{2,1,0:T(8,128)(2,1)} %collective-permute-done.1.near_ref, ...), custom_call_target="tpu_custom_call" | custom-call | flops 8589934592 | bytes 8388608 | tf_op jit(solution)/shard_map/chunk_tiles/pallas_call | solution.py:158
  42.4 4.9 %collective-permute-done.5.near_ref = bf16[1,64,12288]{2,1,0:T(8,128)(2,1)} collective-permute-done((bf16[1,64,12288]{2,1,0:T(8,128)(2,1)}, bf16[1,64,12288]{2,1,0:T(8,128)(2,1)}, u32[]{:S(2)}, u32[]{:S(2)}) %collective-permute-start.5) | collective-permute-done | bytes 1572896 | tf_op jit(solution)/shard_map/ppermute | solution.py:250
  47.2 2.0 %collective-permute-done.6.far_ref = bf16[1,64,12288]{2,1,0:T(8,128)(2,1)} collective-permute-done((bf16[1,64,12288]{2,1,0:T(8,128)(2,1)}, bf16[1,64,12288]{2,1,0:T(8,128)(2,1)}, u32[]{:S(2)}, u32[]{:S(2)}) %collective-permute-start.6) | collective-permute-done | bytes 1572896 | tf_op jit(solution)/shard_map/ppermute | solution.py:249
  49.2 5.9 %chunk_tiles.4 = (f32[512,128]{1,0:T(8,128)S(1)}, f32[8,128]{1,0:T(8,128)S(1)}) custom-call(s32[2]{0:T(128)S(1)} %pad_add_fusion.place_ref, bf16[1,64,12288]{2,1,0:T(8,128)(2,1)} %slice.31.own_ref, s32[1,32768]{1,0:T(1,128)S(1)} %copy-done.1, bf16[1,64,12288]{2,1,0:T(8,128)(2,1)} %collective-permute-done.5.near_ref, ...), custom_call_target="tpu_custom_call" | custom-call | flops 6442450944 | bytes 6291456 | tf_op jit(solution)/shard_map/chunk_tiles/pallas_call | solution.py:158
  55.2 0.0 collective-permute-done.3.near_ref
  55.2 0.0 collective-permute-done.4.far_ref
  55.2 2.1 %chunk_tiles.5 = (f32[136,128]{1,0:T(8,128)S(1)}, f32[136,128]{1,0:T(8,128)S(1)}, f32[136,128]{1,0:T(8,128)S(1)}, f32[136,128]{1,0:T(8,128)S(1)}) custom-call(s32[2]{0:T(128)S(1)} %pad_add_fusion.place_ref, bf16[1,64,4096]{2,1,0:T(8,128)(2,1)S(1)} %slice.29.own_ref, s32[1,32768]{1,0:T(1,128)S(1)} %copy-done.1, ...), custom_call_target="tpu_custom_call" | custom-call | flops 2147483648 | bytes 2097152 | tf_op jit(solution)/shard_map/chunk_tiles/pallas_call | solution.py:158
  57.3 7.2 %collective-permute-start.10 = (f32[136,128]{1,0:T(8,128)S(1)}, f32[136,128]{1,0:T(8,128)S(1)}, u32[]{:S(2)}, u32[]{:S(2)}) collective-permute-start(f32[136,128]{1,0:T(8,128)S(1)} %get-tuple-element.22), channel_id=1, source_target_pairs={{0,6},{2,4},{5,3},{7,1},{8,14},{10,12},{13,11},{15,9},{16,22},{18,... | collective-permute-start | bytes 208904 | tf_op jit(solution)/shard_map/ppermute | solution.py:287
  64.5 0.7 collective-permute-start.7
  65.2 2.0 %collective-permute-start.8 = (f32[136,128]{1,0:T(8,128)S(1)}, f32[136,128]{1,0:T(8,128)S(1)}, u32[]{:S(2)}, u32[]{:S(2)}) collective-permute-start(f32[136,128]{1,0:T(8,128)S(1)} %get-tuple-element.20), channel_id=1, source_target_pairs={{0,2},{2,0},{4,6},{6,4},{8,10},{10,8},{9,3},{11,1},{12,14},{14,12}... | collective-permute-start | bytes 208904 | tf_op jit(solution)/shard_map/ppermute | solution.py:287
  67.2 1.8 %collective-permute-start.9 = (f32[136,128]{1,0:T(8,128)S(1)}, f32[136,128]{1,0:T(8,128)S(1)}, u32[]{:S(2)}, u32[]{:S(2)}) collective-permute-start(f32[136,128]{1,0:T(8,128)S(1)} %get-tuple-element.21), channel_id=1, source_target_pairs={{0,4},{2,6},{5,1},{7,3},{8,12},{10,14},{13,9},{15,11},{16,20},{18,... | collective-permute-start | bytes 208904 | tf_op jit(solution)/shard_map/ppermute | solution.py:287
  69.0 0.1 pad_maximum_fusion.factor_ref
  69.1 2.3 %collective-permute-done.8.refs_1_ = f32[136,128]{1,0:T(8,128)S(1)} collective-permute-done((f32[136,128]{1,0:T(8,128)S(1)}, f32[136,128]{1,0:T(8,128)S(1)}, u32[]{:S(2)}, u32[]{:S(2)}) %collective-permute-start.8) | collective-permute-done | bytes 69664 | tf_op jit(solution)/shard_map/ppermute | solution.py:287
  71.4 0.0 collective-permute-done.9.refs_2_
  71.4 1.8 %normalise_and_skew.1 = f32[1,4,64,64]{3,2,1,0:T(8,128)} custom-call(s32[2]{0:T(128)S(1)} %pad_add_fusion.place_ref, f32[128,128]{1,0:T(8,128)S(1)} %pad_maximum_fusion.factor_ref, f32[136,128]{1,0:T(8,128)S(1)} %add.32.own_ref, f32[136,128]{1,0:T(8,128)S(1)} %get-tuple-element.19.kept_ref, f32[136,128]{1,0:T(8,128)S(1)} %collective-permute-done.7.refs_0_, ...), custom_call_target="tpu_custom_call" | custom-call | tf_op jit(solution)/shard_map/normalise_and_skew/pallas_call | solution.py:206
  (11 shorter events, 0.0 us)
Async XLA Ops:
  0.0 4.6 %copy-start = (bf16[1,64,32768]{2,1,0:T(8,128)(2,1)S(1)}, bf16[1,64,32768]{2,1,0:T(8,128)(2,1)}, u32[]{:S(2)}) copy-start(bf16[1,64,32768]{2,1,0:T(8,128)(2,1)} %frames_ref.1) | copy-start | bytes 12582916
  1.9 6.8 %copy-start.1 = (s32[1,32768]{1,0:T(1,128)S(1)}, s32[1,32768]{1,0:T(1,128)}, u32[]{:S(2)}) copy-start(s32[1,32768]{1,0:T(1,128)} %label_ref.7) | copy-start | bytes 393220
  1.9 28.5 %collective-permute-start.1 = (bf16[1,64,16384]{2,1,0:T(8,128)(2,1)S(1)}, bf16[1,64,16384]{2,1,0:T(8,128)(2,1)}, u32[]{:S(2)}, u32[]{:S(2)}) collective-permute-start(bf16[1,64,16384]{2,1,0:T(8,128)(2,1)S(1)} %slice.30.own_ref), channel_id=1, source_target_pairs={{1,5},{4,0},{9,13},{12,8},{17,21},{20,16},{25,29},{28,24},{3,7},{6... | collective-permute-start | bytes 6291464 | tf_op jit(solution)/shard_map/ppermute | solution.py:250
  3.3 29.0 %collective-permute-start.2 = (bf16[1,64,16384]{2,1,0:T(8,128)(2,1)S(1)}, bf16[1,64,16384]{2,1,0:T(8,128)(2,1)}, u32[]{:S(2)}, u32[]{:S(2)}) collective-permute-start(bf16[1,64,16384]{2,1,0:T(8,128)(2,1)S(1)} %slice.30.own_ref), channel_id=1, source_target_pairs={{1,9},{5,13},{8,0},{9,17},{12,4},{13,21},{16,8},{17,25},{20,12},{2... | collective-permute-start | bytes 6291464 | tf_op jit(solution)/shard_map/ppermute | solution.py:249
  5.9 15.1 %copy-start.2 = (s32[1,4]{1,0:T(1,128)S(1)}, s32[1,4]{1,0:T(1,128)}, u32[]{:S(2)}) copy-start(s32[1,4]{1,0:T(1,128)} %param.5) | copy-start | bytes 52
  5.9 41.3 %collective-permute-start.5 = (bf16[1,64,12288]{2,1,0:T(8,128)(2,1)}, bf16[1,64,12288]{2,1,0:T(8,128)(2,1)}, u32[]{:S(2)}, u32[]{:S(2)}) collective-permute-start(bf16[1,64,12288]{2,1,0:T(8,128)(2,1)} %slice.31.own_ref), channel_id=1, source_target_pairs={{1,5},{4,0},{9,13},{12,8},{17,21},{20,16},{25,29},{28,24},{3,7},{6... | collective-permute-start | bytes 4718600 | tf_op jit(solution)/shard_map/ppermute | solution.py:250
  7.4 41.9 %collective-permute-start.6 = (bf16[1,64,12288]{2,1,0:T(8,128)(2,1)}, bf16[1,64,12288]{2,1,0:T(8,128)(2,1)}, u32[]{:S(2)}, u32[]{:S(2)}) collective-permute-start(bf16[1,64,12288]{2,1,0:T(8,128)(2,1)} %slice.31.own_ref), channel_id=1, source_target_pairs={{1,9},{5,13},{8,0},{9,17},{12,4},{13,21},{16,8},{17,25},{20,12},{2... | collective-permute-start | bytes 4718600 | tf_op jit(solution)/shard_map/ppermute | solution.py:249
  15.7 5.3 %collective-permute-start = (f32[136,128]{1,0:T(8,128)S(1)}, f32[136,128]{1,0:T(8,128)S(1)}, u32[]{:S(2)}, u32[]{:S(2)}) collective-permute-start(f32[136,128]{1,0:T(8,128)S(1)} %own_tile_and_sums.1), channel_id=1, source_target_pairs={{0,2},{2,0},{1,3},{3,1},{4,6},{6,4},{5,7},{7,5},{8,10},{10,8},{9,1... | collective-permute-start | bytes 208904 | tf_op jit(solution)/shard_map/ppermute | solution.py:264
  32.4 22.8 %collective-permute-start.3 = (bf16[1,64,4096]{2,1,0:T(8,128)(2,1)S(1)}, bf16[1,64,4096]{2,1,0:T(8,128)(2,1)S(1)}, u32[]{:S(2)}, u32[]{:S(2)}) collective-permute-start(bf16[1,64,4096]{2,1,0:T(8,128)(2,1)S(1)} %slice.29.own_ref), channel_id=1, source_target_pairs={{1,5},{4,0},{9,13},{12,8},{17,21},{20,16},{25,29},{28,24},{3,7},{6... | collective-permute-start | bytes 1572872 | tf_op jit(solution)/shard_map/ppermute | solution.py:250
  33.7 21.5 %collective-permute-start.4 = (bf16[1,64,4096]{2,1,0:T(8,128)(2,1)S(1)}, bf16[1,64,4096]{2,1,0:T(8,128)(2,1)S(1)}, u32[]{:S(2)}, u32[]{:S(2)}) collective-permute-start(bf16[1,64,4096]{2,1,0:T(8,128)(2,1)S(1)} %slice.29.own_ref), channel_id=1, source_target_pairs={{1,9},{5,13},{8,0},{9,17},{12,4},{13,21},{16,8},{17,25},{20,12},{2... | collective-permute-start | bytes 1572872 | tf_op jit(solution)/shard_map/ppermute | solution.py:249
  57.3 11.8 %collective-permute-start.10 = (f32[136,128]{1,0:T(8,128)S(1)}, f32[136,128]{1,0:T(8,128)S(1)}, u32[]{:S(2)}, u32[]{:S(2)}) collective-permute-start(f32[136,128]{1,0:T(8,128)S(1)} %get-tuple-element.22), channel_id=1, source_target_pairs={{0,6},{2,4},{5,3},{7,1},{8,14},{10,12},{13,11},{15,9},{16,22},{18,... | collective-permute-start | bytes 208904 | tf_op jit(solution)/shard_map/ppermute | solution.py:287
  64.5 4.6 %collective-permute-start.7 = (f32[136,128]{1,0:T(8,128)S(1)}, f32[136,128]{1,0:T(8,128)S(1)}, u32[]{:S(2)}, u32[]{:S(2)}) collective-permute-start(f32[136,128]{1,0:T(8,128)S(1)} %get-tuple-element.19.kept_ref), channel_id=1, source_target_pairs={{9,1},{11,3},{13,5},{15,7},{17,9},{19,11},{21,13},{23,15},{25,17},... | collective-permute-start | bytes 208904 | tf_op jit(solution)/shard_map/ppermute | solution.py:287
  65.2 6.2 %collective-permute-start.8 = (f32[136,128]{1,0:T(8,128)S(1)}, f32[136,128]{1,0:T(8,128)S(1)}, u32[]{:S(2)}, u32[]{:S(2)}) collective-permute-start(f32[136,128]{1,0:T(8,128)S(1)} %get-tuple-element.20), channel_id=1, source_target_pairs={{0,2},{2,0},{4,6},{6,4},{8,10},{10,8},{9,3},{11,1},{12,14},{14,12}... | collective-permute-start | bytes 208904 | tf_op jit(solution)/shard_map/ppermute | solution.py:287
  67.2 4.2 %collective-permute-start.9 = (f32[136,128]{1,0:T(8,128)S(1)}, f32[136,128]{1,0:T(8,128)S(1)}, u32[]{:S(2)}, u32[]{:S(2)}) collective-permute-start(f32[136,128]{1,0:T(8,128)S(1)} %get-tuple-element.21), channel_id=1, source_target_pairs={{0,4},{2,6},{5,1},{7,3},{8,12},{10,14},{13,9},{15,11},{16,20},{18,... | collective-permute-start | bytes 208904 | tf_op jit(solution)/shard_map/ppermute | solution.py:287

commit v2 on v1

v2 whole, which is shorter than its diff:
```python
import functools

import jax
import jax.numpy as jnp
from jax import lax
from jax.experimental import pallas as pl
from jax.experimental.pallas import tpu as pltpu
from jax.sharding import PartitionSpec as P

DELAYS_STORED = 128
PIX = 65536
RADII = 4
ROWS = 64
UNITS = 16
SIZES = (7, 5, 3, 1)
GATES = (None, None, None, None)
STRIP = 2048
NT = (((1,), (1,)), ((), ()))


def packed(tile):
    half = tile.shape[0] // 2
    return jnp.concatenate([tile[:half], tile[half:]], axis=1)


def masked_by_annulus(block, label):
    return [block * (label == a).astype(block.dtype) for a in range(RADII)]


def annulus_rows(label):
    ids = lax.broadcasted_iota(jnp.int32, (16, label.shape[1]), 0)
    return (label == ids).astype(jnp.float32).astype(jnp.bfloat16)


def products(rows, columns):
    return lax.dot_general(
        jnp.concatenate(rows, axis=0), columns, NT, preferred_element_type=jnp.float32
    )


def strips(size):
    return [(begin, min(begin + STRIP, size)) for begin in range(0, size, STRIP)]


def own_kernel(label_ref, *refs):
    *piece_refs, out_ref = refs
    half = RADII * ROWS
    total, offset = None, 0
    for piece_ref in piece_refs:
        size = piece_ref.shape[2]
        for begin, end in strips(size):
            block = piece_ref[0, :, begin:end]
            label = label_ref[:, offset + begin : offset + end]
            part = products(masked_by_annulus(block, label) + [annulus_rows(label)], block)
            total = part if total is None else total + part
        offset += size
    tile, sums = total[:half], total[half : half + 8]
    t = lax.rem(lax.broadcasted_iota(jnp.int32, tile.shape, 0), ROWS)
    below = lax.broadcasted_iota(jnp.int32, tile.shape, 1) < t
    out_ref[: 2 * ROWS] = packed(jnp.where(below, 0.0, tile))
    out_ref[2 * ROWS :] = jnp.concatenate([sums, sums], axis=1)


def cost(pixels, rows, columns):
    return pl.CostEstimate(
        flops=2 * rows * columns * pixels, bytes_accessed=2 * columns * pixels, transcendentals=0
    )


def own_part(label, pieces):
    vmem = pl.BlockSpec(memory_space=pltpu.VMEM)
    return pl.pallas_call(
        own_kernel,
        in_specs=[vmem] * (1 + len(pieces)),
        out_specs=vmem,
        out_shape=jax.ShapeDtypeStruct((2 * ROWS + 8, 2 * ROWS), jnp.float32),
        compiler_params=pltpu.CompilerParams(vmem_limit_bytes=8 << 20),
        cost_estimate=cost(label.shape[1], 512, 256),
        name="own_tile_and_sums",
    )(label, *pieces)


def chunk_kernel(start, first, last, place_ref, own_ref, label_ref, far_ref, near_ref, *refs):
    if first:
        before_ref = None
    else:
        before_ref, *refs = refs
    if last:
        *out_refs, acc = refs
    else:
        (acc,) = refs
    half = RADII * ROWS
    later = place_ref[0] == 1
    pieces = strips(near_ref.shape[2])

    def add(with_near):
        total = None
        for begin, end in pieces:
            own, near, far = (ref[0, :, begin:end] for ref in (own_ref, near_ref, far_ref))
            earliest = jnp.where(later, far, own)
            latest = jnp.where(later, own, far)
            label = label_ref[:, start + begin : start + end]
            rows = [annulus_rows(label)] + masked_by_annulus(earliest, label)
            if with_near:
                rows += masked_by_annulus(near, label)
            part = products(rows, jnp.concatenate([near, latest], axis=0))
            total = part if total is None else total + part
        count = total.shape[0]
        acc[:count] = total if first else total + before_ref[:count]
        if not with_near:
            acc[count:] = jnp.zeros_like(acc[count:])

    @pl.when(place_ref[2] == 1)
    def _():
        add(True)

    @pl.when(place_ref[2] == 0)
    def _():
        add(False)

    if not last:
        return
    shape = (half, ROWS)
    t = lax.rem(lax.broadcasted_iota(jnp.int32, shape, 0), ROWS)
    below = lax.broadcasted_iota(jnp.int32, shape, 1) < t
    near_tile = acc[16 : 16 + half, :ROWS]
    far_tile = acc[16 : 16 + half, ROWS:]
    next_tile = acc[16 + half :, ROWS:]
    second = place_ref[1] == 1
    here = (jnp.where(below, near_tile, 0.0), jnp.where(below, far_tile, near_tile))
    after = (jnp.where(below, next_tile, 0.0), jnp.where(below, 0.0, next_tile))
    sums = acc[:8]
    lane = lax.broadcasted_iota(jnp.int32, sums.shape, 1)
    beside = (lane < ROWS) & (place_ref[2] == 1)
    after_sums = jnp.where(beside, pltpu.roll(sums, ROWS, 1), 0.0)
    for k, ((low, high), row) in enumerate(((here, sums), (after, after_sums))):
        out_refs[2 * k][: 2 * ROWS] = packed(jnp.where(second, high, low))
        out_refs[2 * k + 1][: 2 * ROWS] = packed(jnp.where(second, low, high))
        out_refs[2 * k][2 * ROWS :] = row
        out_refs[2 * k + 1][2 * ROWS :] = row


def chunk_part(place, piece, label, start, near, far, before, last):
    size = near.shape[2]
    acc_shape = (16 + 2 * RADII * ROWS, 2 * ROWS)
    message = (2 * ROWS + 8, 2 * ROWS)
    vmem = pl.BlockSpec(memory_space=pltpu.VMEM)
    operands = [place, piece, label, far, near] + ([] if before is None else [before])
    shapes = [message] * 4 if last else [acc_shape]
    return pl.pallas_call(
        functools.partial(chunk_kernel, start, before is None, last),
        in_specs=[pl.BlockSpec(memory_space=pltpu.SMEM)] + [vmem] * (len(operands) - 1),
        out_specs=[vmem] * len(shapes),
        out_shape=[jax.ShapeDtypeStruct(shape, jnp.float32) for shape in shapes],
        scratch_shapes=[pltpu.VMEM(acc_shape, jnp.float32)] if last else [],
        compiler_params=pltpu.CompilerParams(vmem_limit_bytes=8 << 20),
        cost_estimate=cost(size, 1024, 256),
        name="chunk_tiles",
    )(*operands)


def final_kernel(place_ref, factor_ref, own_ref, kept_ref, *refs):
    *message_refs, out_ref = refs
    total = jnp.where(place_ref[0] == 0, kept_ref[...], 0.0)
    for ref in message_refs:
        total = total + ref[...]
    own = own_ref[...]
    first = place_ref[1] == 0
    tile = total[: 2 * ROWS] + jnp.where(first, own[: 2 * ROWS], 0.0)
    ahead, present = total[2 * ROWS :], own[2 * ROWS :]
    lane = lax.broadcasted_iota(jnp.int32, ahead.shape, 1)
    moved = pltpu.roll(ahead, ROWS, 1)
    same = jnp.where(first, present, jnp.where(lane < ROWS, ahead, moved))
    beyond = jnp.where(first == (lane < ROWS), ahead, moved)
    t = lax.rem(lax.broadcasted_iota(jnp.int32, tile.shape, 0), ROWS)
    s = lax.rem(lax.broadcasted_iota(jnp.int32, tile.shape, 1), ROWS)

    def spread(row):
        pairs = [jnp.where(lane[:1] < ROWS, row[a : a + 1], row[2 + a : 3 + a]) for a in range(2)]
        return jnp.concatenate([jnp.broadcast_to(pair, (ROWS, 2 * ROWS)) for pair in pairs], axis=0)

    far = jnp.where(s < t, spread(beyond), spread(same))
    factor = factor_ref[...]
    tile = jnp.where(factor > 0.0, tile * factor / far, 0.0)
    for group in range(2):
        part = tile[:, group * ROWS : (group + 1) * ROWS]
        twice = jnp.concatenate([part, part], axis=1)
        for bit in range(6):
            turned = pltpu.roll(twice, 128 - (1 << bit), 1)
            twice = jnp.where((t >> bit) & 1 == 1, turned, twice)
        for a in range(2):
            out_ref[0, 2 * group + a] = twice[a * ROWS : (a + 1) * ROWS, :ROWS]


def final_part(place, factor, own, kept, messages):
    vmem = pl.BlockSpec(memory_space=pltpu.VMEM)
    return pl.pallas_call(
        final_kernel,
        in_specs=[pl.BlockSpec(memory_space=pltpu.SMEM)] + [vmem] * (3 + len(messages)),
        out_specs=vmem,
        out_shape=jax.ShapeDtypeStruct((1, RADII, ROWS, ROWS), jnp.float32),
        compiler_params=pltpu.CompilerParams(vmem_limit_bytes=8 << 20),
        name="normalise_and_skew",
    )(place, factor, own, kept, *messages)


def factors(own, lag_width):
    tm, pix = lax.axis_index("tm"), lax.axis_index("pix")
    devices = lax.axis_size("tm")
    t = lax.broadcasted_iota(jnp.int32, (RADII, ROWS, ROWS), 1)
    s = lax.broadcasted_iota(jnp.int32, (RADII, ROWS, ROWS), 2)
    lag = jnp.where(s >= t, s - t, s - t + ROWS) + pix * ROWS
    valid = (lag < lag_width[0][:, None, None]) & (tm * ROWS + t + lag < devices * ROWS)
    annulus_size = PIX // RADII
    result = jnp.where(valid, annulus_size / own[:, :, None], 0.0)
    return packed(result.reshape(RADII * ROWS, ROWS))


def shards(frames, annulus_label, lag_width):
    devices = lax.axis_size("tm")
    pixels = frames.shape[2]
    pb, pix = lax.axis_index("pb"), lax.axis_index("pix")
    has_near = (lax.axis_index("tm") % 2 == pb)
    place = jnp.stack([pb, pix, has_near.astype(jnp.int32)]).astype(jnp.int32)

    def far_pairs():
        for i in range(devices):
            for band, target in ((0, i - 2), (1, i + 2)):
                if 0 <= target < devices:
                    yield 2 * i + band, 2 * target + band

    def near_pairs():
        for i in range(devices):
            band, target = (0, i - 1) if i % 2 else (1, i + 1)
            if target < devices:
                yield 2 * i + band, 2 * target + band

    tm_pb = ("tm", "pb")

    def sent(piece):
        near = lax.ppermute(piece, tm_pb, list(near_pairs()))
        far = lax.ppermute(piece, tm_pb, list(far_pairs()))
        return near, far

    unit = pixels // UNITS
    starts = [sum(SIZES[:index]) * unit for index in range(len(SIZES))]
    pieces = [
        lax.slice_in_dim(frames, start, start + count * unit, axis=2) for start, count in zip(starts, SIZES)
    ]
    own = own_part(annulus_label, pieces)
    own = own + lax.ppermute(own, "pix", [(0, 1), (1, 0)])
    factor = factors(own[2 * ROWS : 2 * ROWS + RADII, :ROWS], lag_width)

    received, states, sendable = {}, [], list(pieces)

    def send(index):
        piece = pieces[index]
        if GATES[index]:
            kind, after = GATES[index]
            gate = {"done": received.get(after), "own": own, "state": states[after] if kind == "state" else None}
            piece, _ = lax.optimization_barrier((piece, gate[kind]))
        received[index] = sent(piece)

    for index in range(len(SIZES)):
        for other in range(len(SIZES)):
            gate = GATES[other]
            if other not in received and (gate is None or gate[1] < index):
                send(other)
        near, far = received[index]
        last = index == len(SIZES) - 1
        before = states[-1] if states else None
        result = chunk_part(place, pieces[index], annulus_label, starts[index], near, far, before, last)
        states.append(result if last else result[0])
    state = states[-1]
    here_same, here_other, after_same, after_other = state

    def message_pairs(step, flip):
        for i in range(devices):
            for band in range(2):
                target = i ^ 1 if step else (i if band == 0 else i - 2)
                if not 0 <= target < devices or not (step or flip or band):
                    continue
                for x in range(2):
                    yield (i * 2 + x) * 2 + band, (target * 2 + (x ^ flip)) * 2 + band

    everywhere = ("tm", "pix", "pb")
    messages = [
        lax.ppermute(message, everywhere, list(message_pairs(step, flip)))
        for message, step, flip in (
            (here_same, 0, 0),
            (here_other, 0, 1),
            (after_same, 1, 0),
            (after_other, 1, 1),
        )
    ]
    return final_part(place, factor, own, here_same, messages)


def solution(mesh):
    return jax.shard_map(
        shards,
        mesh=mesh,
        in_specs=(P("pb", "tm", "pix"), P("pb", "pix"), P("pb", None)),
        out_specs=P("pb", None, "tm", "pix"),
        check_vma=False,
    )
```

time: 73.6 us -> 69.4 us (0.943)
  Pallas kernels: 24.3 us -> 21.6 us
  starting transfers between devices: 22.7 us -> 20.1 us
  local copies, waits for them, and re-layouts: 4.27 us -> 6.3 us
  waiting for transfers between devices: 21.5 us -> 19.8 us
    ppermute x3 -> x4, waiting for transfers between devices: 14.1 us -> 0.99 us  [sent(): near = lax.ppermute(piece, tm_pb, list(near_pairs()))]
    ppermute x3 -> x4, waiting for transfers between devices: 3.97 us -> 12.2 us  [sent(): far = lax.ppermute(piece, tm_pb, list(far_pairs()))]
    ppermute x4, starting transfers between devices: 11.7 us -> 6.7 us  [shards(): lax.ppermute(message, everywhere, list(message_pairs(step, flip)))]
    pallas_call x4 -> x5, Pallas kernels: 22.5 us -> 19.8 us  [the longest x4 14.9 us: chunk_part(): pl.pallas_call(functools.partial(chunk_kernel, start, before is None, las...]
    ppermute x4, waiting for transfers between devices: 2.32 us -> 4.47 us  [shards(): lax.ppermute(message, everywhere, list(message_pairs(step, flip)))]
    ppermute x3 -> x4, starting transfers between devices: 3.88 us -> 5.29 us  [sent(): far = lax.ppermute(piece, tm_pb, list(far_pairs()))]
    slice x3 -> x4, local copies, waits for them, and re-layouts: 4.25 us -> 5.37 us  [shards(): lax.slice_in_dim(frames, start, start + count * unit, axis=2)]
    ppermute x1, waiting for transfers between devices: 1.11 us -> 2.21 us  [shards(): own = own + lax.ppermute(own, 'pix', [(0, 1), (1, 0)])]
  transfers between devices with their start and end apart: 11 -> 13, of which waited for: 6 -> 8; matrix products, arithmetic and copies ran while one was open for 4% -> 6% of each run, Pallas kernels for 28% -> 27%
where the time goes in v2:
time: 69.4 us; the launch traced here: 68.4 us
  Pallas kernels  21.6 us (31%)
  starting transfers between devices  20.1 us (29%)
  waiting for transfers between devices  19.8 us (29%)
  local copies, waits for them, and re-layouts  6.3 us (9%)
    pallas_call x4, Pallas kernels, chunk_part(): pl.pallas_call(functools.partial(chunk_kernel, start, before is None, las...  14.9 us
    ppermute x4, waiting for transfers between devices, sent(): far = lax.ppermute(piece, tm_pb, list(far_pairs()))  12.2 us
    ppermute x4, starting transfers between devices, shards(): lax.ppermute(message, everywhere, list(message_pairs(step, flip)))  6.7 us
    slice x4, local copies, waits for them, and re-layouts, shards(): lax.slice_in_dim(frames, start, start + count * unit, axis=2)  5.37 us
    ppermute x4, starting transfers between devices, sent(): far = lax.ppermute(piece, tm_pb, list(far_pairs()))  5.29 us
    ppermute x4, starting transfers between devices, sent(): near = lax.ppermute(piece, tm_pb, list(near_pairs()))  5.15 us
    pallas_call x1, Pallas kernels, own_part(): pl.pallas_call(own_kernel, in_specs=[vmem] * (1 + len(pieces)), out_specs...  4.81 us
    ppermute x4, waiting for transfers between devices, shards(): lax.ppermute(message, everywhere, list(message_pairs(step, flip)))  4.47 us
  transfers between devices with their start and end apart: 13, of which 8 were waited for; matrix products, arithmetic and copies ran while one was open for 6% of the time, Pallas kernels for 27%

profile of v2, /device:TPU:0, one launch (start us, length us, event | category | flops | bytes accessed | tf_op | source)
XLA Modules:
  0.0 68.4 jit_solution(10517861422095530222)
XLA Ops:
  0.0 1.6 %slice.27.refs_0_.own_ref = bf16[1,64,14336]{2,1,0:T(8,128)(2,1)S(1)} slice(bf16[1,64,32768]{2,1,0:T(8,128)(2,1)} %param.3), slice={[0:1], [0:64], [0:14336]} | slice | bytes 3670016 | tf_op jit(solution)/shard_map/slice | solution.py:248
  1.6 1.4 %collective-permute-start.7 = (bf16[1,64,14336]{2,1,0:T(8,128)(2,1)S(1)}, bf16[1,64,14336]{2,1,0:T(8,128)(2,1)}, u32[]{:S(2)}, u32[]{:S(2)}) collective-permute-start(bf16[1,64,14336]{2,1,0:T(8,128)(2,1)S(1)} %slice.27.refs_0_.own_ref), channel_id=1, source_target_pairs={{1,9},{5,13},{8,0},{9,17},{12,4},{13,21},{16,8},{17,25},{20,12},{2... | collective-permute-start | bytes 5505032 | tf_op jit(solution)/shard_map/ppermute | solution.py:242
  3.1 1.3 %collective-permute-start.8 = (bf16[1,64,14336]{2,1,0:T(8,128)(2,1)S(1)}, bf16[1,64,14336]{2,1,0:T(8,128)(2,1)}, u32[]{:S(2)}, u32[]{:S(2)}) collective-permute-start(bf16[1,64,14336]{2,1,0:T(8,128)(2,1)S(1)} %slice.27.refs_0_.own_ref), channel_id=1, source_target_pairs={{1,5},{4,0},{9,13},{12,8},{17,21},{20,16},{25,29},{28,24},{3,7},{6... | collective-permute-start | bytes 5505032 | tf_op jit(solution)/shard_map/ppermute | solution.py:241
  4.4 1.4 %slice.28.refs_1_.own_ref = bf16[1,64,10240]{2,1,0:T(8,128)(2,1)S(1)} slice(bf16[1,64,32768]{2,1,0:T(8,128)(2,1)} %param.3), slice={[0:1], [0:64], [14336:24576]} | slice | bytes 2621440 | tf_op jit(solution)/shard_map/slice | solution.py:248
  5.8 1.3 %collective-permute-start.5 = (bf16[1,64,10240]{2,1,0:T(8,128)(2,1)S(1)}, bf16[1,64,10240]{2,1,0:T(8,128)(2,1)}, u32[]{:S(2)}, u32[]{:S(2)}) collective-permute-start(bf16[1,64,10240]{2,1,0:T(8,128)(2,1)S(1)} %slice.28.refs_1_.own_ref), channel_id=1, source_target_pairs={{1,9},{5,13},{8,0},{9,17},{12,4},{13,21},{16,8},{17,25},{20,12},{2... | collective-permute-start | bytes 3932168 | tf_op jit(solution)/shard_map/ppermute | solution.py:242
  7.1 1.3 %collective-permute-start.6 = (bf16[1,64,10240]{2,1,0:T(8,128)(2,1)S(1)}, bf16[1,64,10240]{2,1,0:T(8,128)(2,1)}, u32[]{:S(2)}, u32[]{:S(2)}) collective-permute-start(bf16[1,64,10240]{2,1,0:T(8,128)(2,1)S(1)} %slice.28.refs_1_.own_ref), channel_id=1, source_target_pairs={{1,5},{4,0},{9,13},{12,8},{17,21},{20,16},{25,29},{28,24},{3,7},{6... | collective-permute-start | bytes 3932168 | tf_op jit(solution)/shard_map/ppermute | solution.py:241
  8.4 1.2 %slice.29.refs_2_.own_ref = bf16[1,64,6144]{2,1,0:T(8,128)(2,1)S(1)} slice(bf16[1,64,32768]{2,1,0:T(8,128)(2,1)} %param.3), slice={[0:1], [0:64], [24576:30720]} | slice | bytes 1572864 | tf_op jit(solution)/shard_map/slice | solution.py:248
  9.6 1.2 %slice.30.refs_3_.own_ref = bf16[1,64,2048]{2,1,0:T(8,128)(2,1)S(1)} slice(bf16[1,64,32768]{2,1,0:T(8,128)(2,1)} %param.3), slice={[0:1], [0:64], [30720:32768]} | slice | bytes 524288 | tf_op jit(solution)/shard_map/slice | solution.py:248
  10.8 4.8 %own_tile_and_sums.1 = f32[136,128]{1,0:T(8,128)S(1)} custom-call(s32[1,32768]{1,0:T(1,128)S(1)} %copy-done.2, bf16[1,64,14336]{2,1,0:T(8,128)(2,1)S(1)} %slice.27.refs_0_.own_ref, bf16[1,64,10240]{2,1,0:T(8,128)(2,1)S(1)} %slice.28.refs_1_.own_ref, bf16[1,64,6144]{2,1,0:T(8,128)(2,1)S(1)} %slice.29.refs_2_.own_ref, ...), custom_call_target="tpu_custom_call" | custom-call | flops 8589934592 | bytes 16777216 | tf_op jit(solution)/shard_map/own_tile_and_sums/pallas_call | solution.py:72
  15.6 3.0 %collective-permute-start = (f32[136,128]{1,0:T(8,128)S(1)}, f32[136,128]{1,0:T(8,128)S(1)}, u32[]{:S(2)}, u32[]{:S(2)}) collective-permute-start(f32[136,128]{1,0:T(8,128)S(1)} %own_tile_and_sums.1), channel_id=1, source_target_pairs={{0,2},{2,0},{1,3},{3,1},{4,6},{6,4},{5,7},{7,5},{8,10},{10,8},{9,1... | collective-permute-start | bytes 208904 | tf_op jit(solution)/shard_map/ppermute | solution.py:251
  18.7 2.2 %collective-permute-done = f32[136,128]{1,0:T(8,128)S(1)} collective-permute-done((f32[136,128]{1,0:T(8,128)S(1)}, f32[136,128]{1,0:T(8,128)S(1)}, u32[]{:S(2)}, u32[]{:S(2)}) %collective-permute-start) | collective-permute-done | bytes 69664 | tf_op jit(solution)/shard_map/ppermute | solution.py:251
  20.9 1.3 %collective-permute-start.3 = (bf16[1,64,6144]{2,1,0:T(8,128)(2,1)}, bf16[1,64,6144]{2,1,0:T(8,128)(2,1)S(1)}, u32[]{:S(2)}, u32[]{:S(2)}) collective-permute-start(bf16[1,64,6144]{2,1,0:T(8,128)(2,1)} %copy-done), channel_id=1, source_target_pairs={{1,9},{5,13},{8,0},{9,17},{12,4},{13,21},{16,8},{17,25},{20,12},{2... | collective-permute-start | bytes 2359304 | tf_op jit(solution)/shard_map/ppermute | solution.py:242
  22.2 0.1 fusion.5
  22.3 5.7 %collective-permute-done.7.far_ref = bf16[1,64,14336]{2,1,0:T(8,128)(2,1)} collective-permute-done((bf16[1,64,14336]{2,1,0:T(8,128)(2,1)S(1)}, bf16[1,64,14336]{2,1,0:T(8,128)(2,1)}, u32[]{:S(2)}, u32[]{:S(2)}) %collective-permute-start.7) | collective-permute-done | bytes 1835040 | tf_op jit(solution)/shard_map/ppermute | solution.py:242
  28.0 1.3 %collective-permute-start.4 = (bf16[1,64,6144]{2,1,0:T(8,128)(2,1)}, bf16[1,64,6144]{2,1,0:T(8,128)(2,1)S(1)}, u32[]{:S(2)}, u32[]{:S(2)}) collective-permute-start(bf16[1,64,6144]{2,1,0:T(8,128)(2,1)} %copy-done), channel_id=1, source_target_pairs={{1,5},{4,0},{9,13},{12,8},{17,21},{20,16},{25,29},{28,24},{3,7},{6... | collective-permute-start | bytes 2359304 | tf_op jit(solution)/shard_map/ppermute | solution.py:241
  29.3 1.3 %collective-permute-start.1 = (bf16[1,64,2048]{2,1,0:T(8,128)(2,1)S(1)}, bf16[1,64,2048]{2,1,0:T(8,128)(2,1)S(1)}, u32[]{:S(2)}, u32[]{:S(2)}) collective-permute-start(bf16[1,64,2048]{2,1,0:T(8,128)(2,1)S(1)} %slice.30.refs_3_.own_ref), channel_id=1, source_target_pairs={{1,9},{5,13},{8,0},{9,17},{12,4},{13,21},{16,8},{17,25},{20,12},{2... | collective-permute-start | bytes 786440 | tf_op jit(solution)/shard_map/ppermute | solution.py:242
  30.6 0.9 %copy-done.3 = s32[1,32768]{1,0:T(1,128)S(1)} copy-done((s32[1,32768]{1,0:T(1,128)S(1)}, s32[1,32768]{1,0:T(1,128)}, u32[]{:S(2)}) %copy-start.3) | copy-done | bytes 131096
  31.5 6.1 %chunk_tiles.4.refs_0_ = f32[528,128]{1,0:T(8,128)S(1)} custom-call(s32[3]{0:T(128)S(1)} %pad_add_fusion.place_ref, bf16[1,64,14336]{2,1,0:T(8,128)(2,1)S(1)} %slice.27.refs_0_.own_ref, s32[1,32768]{1,0:T(1,128)S(1)} %copy-done.3, bf16[1,64,14336]{2,1,0:T(8,128)(2,1)} %collective-permute-done.7.far_ref, bf16[1,64,14336]{2,1,0:T(8,128)(2,1)} %collective-permute-done.8.near_ref), custom_call_target="tpu_custom_call" | custom-call | flops 7516192768 | bytes 7340032 | tf_op jit(solution)/shard_map/chunk_tiles/pallas_call | solution.py:150
  37.7 4.4 %collective-permute-done.5.far_ref = bf16[1,64,10240]{2,1,0:T(8,128)(2,1)} collective-permute-done((bf16[1,64,10240]{2,1,0:T(8,128)(2,1)S(1)}, bf16[1,64,10240]{2,1,0:T(8,128)(2,1)}, u32[]{:S(2)}, u32[]{:S(2)}) %collective-permute-start.5) | collective-permute-done | bytes 1310752 | tf_op jit(solution)/shard_map/ppermute | solution.py:242
  42.0 1.3 %collective-permute-start.2 = (bf16[1,64,2048]{2,1,0:T(8,128)(2,1)S(1)}, bf16[1,64,2048]{2,1,0:T(8,128)(2,1)S(1)}, u32[]{:S(2)}, u32[]{:S(2)}) collective-permute-start(bf16[1,64,2048]{2,1,0:T(8,128)(2,1)S(1)} %slice.30.refs_3_.own_ref), channel_id=1, source_target_pairs={{1,5},{4,0},{9,13},{12,8},{17,21},{20,16},{25,29},{28,24},{3,7},{6... | collective-permute-start | bytes 786440 | tf_op jit(solution)/shard_map/ppermute | solution.py:241
  43.3 4.9 %chunk_tiles.5.refs_0_ = f32[528,128]{1,0:T(8,128)S(1)} custom-call(s32[3]{0:T(128)S(1)} %pad_add_fusion.place_ref, bf16[1,64,10240]{2,1,0:T(8,128)(2,1)S(1)} %slice.28.refs_1_.own_ref, s32[1,32768]{1,0:T(1,128)S(1)} %copy-done.3, bf16[1,64,10240]{2,1,0:T(8,128)(2,1)} %collective-permute-done.5.far_ref, ...), custom_call_target="tpu_custom_call" | custom-call | flops 5368709120 | bytes 5242880 | tf_op jit(solution)/shard_map/chunk_tiles/pallas_call | solution.py:150
  48.3 2.1 %collective-permute-done.3.far_ref = bf16[1,64,6144]{2,1,0:T(8,128)(2,1)S(1)} collective-permute-done((bf16[1,64,6144]{2,1,0:T(8,128)(2,1)}, bf16[1,64,6144]{2,1,0:T(8,128)(2,1)S(1)}, u32[]{:S(2)}, u32[]{:S(2)}) %collective-permute-start.3) | collective-permute-done | bytes 786464 | tf_op jit(solution)/shard_map/ppermute | solution.py:242
  50.4 0.6 collective-permute-done.4.near_ref
  51.0 2.4 %chunk_tiles.6.refs_0_ = f32[528,128]{1,0:T(8,128)S(1)} custom-call(s32[3]{0:T(128)S(1)} %pad_add_fusion.place_ref, bf16[1,64,6144]{2,1,0:T(8,128)(2,1)S(1)} %copy-done.1, s32[1,32768]{1,0:T(1,128)S(1)} %copy-done.3, bf16[1,64,6144]{2,1,0:T(8,128)(2,1)S(1)} %collective-permute-done.3.far_ref, bf16[1,64,6144]{2,1,0:T(8,128)(2,1)S(1)} %collective-permute-done.4.near_ref, ...), custom_call_target="tpu_custom_call" | custom-call | flops 3221225472 | bytes 3145728 | tf_op jit(solution)/shard_map/chunk_tiles/pallas_call | solution.py:150
  53.4 0.4 collective-permute-done.2.near_ref
  53.8 1.5 %chunk_tiles.7 = (f32[136,128]{1,0:T(8,128)S(1)}, f32[136,128]{1,0:T(8,128)S(1)}, f32[136,128]{1,0:T(8,128)S(1)}, f32[136,128]{1,0:T(8,128)S(1)}) custom-call(s32[3]{0:T(128)S(1)} %pad_add_fusion.place_ref, bf16[1,64,2048]{2,1,0:T(8,128)(2,1)S(1)} %slice.30.refs_3_.own_ref, s32[1,32768]{1,0:T(1,128)S(1)} %copy-done.3, ...), custom_call_target="tpu_custom_call" | custom-call | flops 1073741824 | bytes 1048576 | tf_op jit(solution)/shard_map/chunk_tiles/pallas_call | solution.py:150
  55.3 4.5 %collective-permute-start.10 = (f32[136,128]{1,0:T(8,128)S(1)}, f32[136,128]{1,0:T(8,128)S(1)}, u32[]{:S(2)}, u32[]{:S(2)}) collective-permute-start(f32[136,128]{1,0:T(8,128)S(1)} %get-tuple-element.10), channel_id=1, source_target_pairs={{0,2},{2,0},{4,6},{6,4},{8,10},{10,8},{9,3},{11,1},{12,14},{14,12}... | collective-permute-start | bytes 208904 | tf_op jit(solution)/shard_map/ppermute | solution.py:288
  59.9 1.5 %collective-permute-start.12 = (f32[136,128]{1,0:T(8,128)S(1)}, f32[136,128]{1,0:T(8,128)S(1)}, u32[]{:S(2)}, u32[]{:S(2)}) collective-permute-start(f32[136,128]{1,0:T(8,128)S(1)} %get-tuple-element.12), channel_id=1, source_target_pairs={{0,6},{2,4},{1,7},{3,5},{4,2},{6,0},{5,3},{7,1},{8,14},{10,12},{9,... | collective-permute-start | bytes 208904 | tf_op jit(solution)/shard_map/ppermute | solution.py:288
  61.4 0.7 collective-permute-start.9
  62.1 2.1 %collective-permute-done.11.refs_2_ = f32[136,128]{1,0:T(8,128)S(1)} collective-permute-done((f32[136,128]{1,0:T(8,128)S(1)}, f32[136,128]{1,0:T(8,128)S(1)}, u32[]{:S(2)}, u32[]{:S(2)}) %collective-permute-start.11) | collective-permute-done | bytes 69664 | tf_op jit(solution)/shard_map/ppermute | solution.py:288
  64.2 2.4 %collective-permute-done.12.refs_3_ = f32[136,128]{1,0:T(8,128)S(1)} collective-permute-done((f32[136,128]{1,0:T(8,128)S(1)}, f32[136,128]{1,0:T(8,128)S(1)}, u32[]{:S(2)}, u32[]{:S(2)}) %collective-permute-start.12) | collective-permute-done | bytes 69664 | tf_op jit(solution)/shard_map/ppermute | solution.py:288
  66.6 1.8 %normalise_and_skew.1 = f32[1,4,64,64]{3,2,1,0:T(8,128)} custom-call(s32[3]{0:T(128)S(1)} %pad_add_fusion.place_ref, f32[128,128]{1,0:T(8,128)S(1)} %pad_maximum_fusion.factor_ref, f32[136,128]{1,0:T(8,128)S(1)} %add.37.own_ref, f32[136,128]{1,0:T(8,128)S(1)} %get-tuple-element.9.kept_ref, f32[136,128]{1,0:T(8,128)S(1)} %collective-permute-done.9.refs_0_, ...), custom_call_target="tpu_custom_call" | custom-call | tf_op jit(solution)/shard_map/normalise_and_skew/pallas_call | solution.py:197
  (21 shorter events, 0.3 us)
Async XLA Ops:
  1.6 9.1 %copy-start.2 = (s32[1,32768]{1,0:T(1,128)S(1)}, s32[1,32768]{1,0:T(1,128)}, u32[]{:S(2)}) copy-start(s32[1,32768]{1,0:T(1,128)} %label_ref.9) | copy-start | bytes 393220
  1.6 26.4 %collective-permute-start.7 = (bf16[1,64,14336]{2,1,0:T(8,128)(2,1)S(1)}, bf16[1,64,14336]{2,1,0:T(8,128)(2,1)}, u32[]{:S(2)}, u32[]{:S(2)}) collective-permute-start(bf16[1,64,14336]{2,1,0:T(8,128)(2,1)S(1)} %slice.27.refs_0_.own_ref), channel_id=1, source_target_pairs={{1,9},{5,13},{8,0},{9,17},{12,4},{13,21},{16,8},{17,25},{20,12},{2... | collective-permute-start | bytes 5505032 | tf_op jit(solution)/shard_map/ppermute | solution.py:242
  3.1 26.2 %collective-permute-start.8 = (bf16[1,64,14336]{2,1,0:T(8,128)(2,1)S(1)}, bf16[1,64,14336]{2,1,0:T(8,128)(2,1)}, u32[]{:S(2)}, u32[]{:S(2)}) collective-permute-start(bf16[1,64,14336]{2,1,0:T(8,128)(2,1)S(1)} %slice.27.refs_0_.own_ref), channel_id=1, source_target_pairs={{1,5},{4,0},{9,13},{12,8},{17,21},{20,16},{25,29},{28,24},{3,7},{6... | collective-permute-start | bytes 5505032 | tf_op jit(solution)/shard_map/ppermute | solution.py:241
  5.8 36.3 %collective-permute-start.5 = (bf16[1,64,10240]{2,1,0:T(8,128)(2,1)S(1)}, bf16[1,64,10240]{2,1,0:T(8,128)(2,1)}, u32[]{:S(2)}, u32[]{:S(2)}) collective-permute-start(bf16[1,64,10240]{2,1,0:T(8,128)(2,1)S(1)} %slice.28.refs_1_.own_ref), channel_id=1, source_target_pairs={{1,9},{5,13},{8,0},{9,17},{12,4},{13,21},{16,8},{17,25},{20,12},{2... | collective-permute-start | bytes 3932168 | tf_op jit(solution)/shard_map/ppermute | solution.py:242
  7.1 36.3 %collective-permute-start.6 = (bf16[1,64,10240]{2,1,0:T(8,128)(2,1)S(1)}, bf16[1,64,10240]{2,1,0:T(8,128)(2,1)}, u32[]{:S(2)}, u32[]{:S(2)}) collective-permute-start(bf16[1,64,10240]{2,1,0:T(8,128)(2,1)S(1)} %slice.28.refs_1_.own_ref), channel_id=1, source_target_pairs={{1,5},{4,0},{9,13},{12,8},{17,21},{20,16},{25,29},{28,24},{3,7},{6... | collective-permute-start | bytes 3932168 | tf_op jit(solution)/shard_map/ppermute | solution.py:241
  9.6 6.0 %copy-start = (bf16[1,64,6144]{2,1,0:T(8,128)(2,1)}, bf16[1,64,6144]{2,1,0:T(8,128)(2,1)S(1)}, u32[]{:S(2)}) copy-start(bf16[1,64,6144]{2,1,0:T(8,128)(2,1)S(1)} %slice.29.refs_2_.own_ref) | copy-start | bytes 2359300
  10.7 11.4 %copy-start.4 = (s32[1,4]{1,0:T(1,128)S(1)}, s32[1,4]{1,0:T(1,128)}, u32[]{:S(2)}) copy-start(s32[1,4]{1,0:T(1,128)} %param.5) | copy-start | bytes 52
  15.6 5.3 %collective-permute-start = (f32[136,128]{1,0:T(8,128)S(1)}, f32[136,128]{1,0:T(8,128)S(1)}, u32[]{:S(2)}, u32[]{:S(2)}) collective-permute-start(f32[136,128]{1,0:T(8,128)S(1)} %own_tile_and_sums.1), channel_id=1, source_target_pairs={{0,2},{2,0},{1,3},{3,1},{4,6},{6,4},{5,7},{7,5},{8,10},{10,8},{9,1... | collective-permute-start | bytes 208904 | tf_op jit(solution)/shard_map/ppermute | solution.py:251
  20.9 29.5 %collective-permute-start.3 = (bf16[1,64,6144]{2,1,0:T(8,128)(2,1)}, bf16[1,64,6144]{2,1,0:T(8,128)(2,1)S(1)}, u32[]{:S(2)}, u32[]{:S(2)}) collective-permute-start(bf16[1,64,6144]{2,1,0:T(8,128)(2,1)} %copy-done), channel_id=1, source_target_pairs={{1,9},{5,13},{8,0},{9,17},{12,4},{13,21},{16,8},{17,25},{20,12},{2... | collective-permute-start | bytes 2359304 | tf_op jit(solution)/shard_map/ppermute | solution.py:242
  28.0 23.0 %collective-permute-start.4 = (bf16[1,64,6144]{2,1,0:T(8,128)(2,1)}, bf16[1,64,6144]{2,1,0:T(8,128)(2,1)S(1)}, u32[]{:S(2)}, u32[]{:S(2)}) collective-permute-start(bf16[1,64,6144]{2,1,0:T(8,128)(2,1)} %copy-done), channel_id=1, source_target_pairs={{1,5},{4,0},{9,13},{12,8},{17,21},{20,16},{25,29},{28,24},{3,7},{6... | collective-permute-start | bytes 2359304 | tf_op jit(solution)/shard_map/ppermute | solution.py:241
  29.3 24.1 %collective-permute-start.1 = (bf16[1,64,2048]{2,1,0:T(8,128)(2,1)S(1)}, bf16[1,64,2048]{2,1,0:T(8,128)(2,1)S(1)}, u32[]{:S(2)}, u32[]{:S(2)}) collective-permute-start(bf16[1,64,2048]{2,1,0:T(8,128)(2,1)S(1)} %slice.30.refs_3_.own_ref), channel_id=1, source_target_pairs={{1,9},{5,13},{8,0},{9,17},{12,4},{13,21},{16,8},{17,25},{20,12},{2... | collective-permute-start | bytes 786440 | tf_op jit(solution)/shard_map/ppermute | solution.py:242
  30.6 0.9 %copy-start.3 = (s32[1,32768]{1,0:T(1,128)S(1)}, s32[1,32768]{1,0:T(1,128)}, u32[]{:S(2)}) copy-start(s32[1,32768]{1,0:T(1,128)} %label_ref.9) | copy-start | bytes 393220
  37.6 13.3 %copy-start.1 = (bf16[1,64,6144]{2,1,0:T(8,128)(2,1)S(1)}, bf16[1,64,6144]{2,1,0:T(8,128)(2,1)}, u32[]{:S(2)}) copy-start(bf16[1,64,6144]{2,1,0:T(8,128)(2,1)} %copy-done) | copy-start | bytes 2359300
  42.0 11.7 %collective-permute-start.2 = (bf16[1,64,2048]{2,1,0:T(8,128)(2,1)S(1)}, bf16[1,64,2048]{2,1,0:T(8,128)(2,1)S(1)}, u32[]{:S(2)}, u32[]{:S(2)}) collective-permute-start(bf16[1,64,2048]{2,1,0:T(8,128)(2,1)S(1)} %slice.30.refs_3_.own_ref), channel_id=1, source_target_pairs={{1,5},{4,0},{9,13},{12,8},{17,21},{20,16},{25,29},{28,24},{3,7},{6... | collective-permute-start | bytes 786440 | tf_op jit(solution)/shard_map/ppermute | solution.py:241
  55.3 6.8 %collective-permute-start.10 = (f32[136,128]{1,0:T(8,128)S(1)}, f32[136,128]{1,0:T(8,128)S(1)}, u32[]{:S(2)}, u32[]{:S(2)}) collective-permute-start(f32[136,128]{1,0:T(8,128)S(1)} %get-tuple-element.10), channel_id=1, source_target_pairs={{0,2},{2,0},{4,6},{6,4},{8,10},{10,8},{9,3},{11,1},{12,14},{14,12}... | collective-permute-start | bytes 208904 | tf_op jit(solution)/shard_map/ppermute | solution.py:288
  59.8 4.4 %collective-permute-start.11 = (f32[136,128]{1,0:T(8,128)S(1)}, f32[136,128]{1,0:T(8,128)S(1)}, u32[]{:S(2)}, u32[]{:S(2)}) collective-permute-start(f32[136,128]{1,0:T(8,128)S(1)} %get-tuple-element.11), channel_id=1, source_target_pairs={{0,4},{2,6},{1,5},{3,7},{4,0},{6,2},{5,1},{7,3},{8,12},{10,14},{9,... | collective-permute-start | bytes 208904 | tf_op jit(solution)/shard_map/ppermute | solution.py:288
  59.9 6.7 %collective-permute-start.12 = (f32[136,128]{1,0:T(8,128)S(1)}, f32[136,128]{1,0:T(8,128)S(1)}, u32[]{:S(2)}, u32[]{:S(2)}) collective-permute-start(f32[136,128]{1,0:T(8,128)S(1)} %get-tuple-element.12), channel_id=1, source_target_pairs={{0,6},{2,4},{1,7},{3,5},{4,2},{6,0},{5,3},{7,1},{8,14},{10,12},{9,... | collective-permute-start | bytes 208904 | tf_op jit(solution)/shard_map/ppermute | solution.py:288
  61.4 5.2 %collective-permute-start.9 = (f32[136,128]{1,0:T(8,128)S(1)}, f32[136,128]{1,0:T(8,128)S(1)}, u32[]{:S(2)}, u32[]{:S(2)}) collective-permute-start(f32[136,128]{1,0:T(8,128)S(1)} %get-tuple-element.9.kept_ref), channel_id=1, source_target_pairs={{9,1},{11,3},{13,5},{15,7},{17,9},{19,11},{21,13},{23,15},{25,17},... | collective-permute-start | bytes 208904 | tf_op jit(solution)/shard_map/ppermute | solution.py:288

commit v3 on v2

--- a/solution.py
+++ b/solution.py
@@ -16,6 +16,11 @@
 GATES = (None, None, None, None)
 STRIP = 2048
 NT = (((1,), (1,)), ((), ()))
+
+
+def place():
+    band = lax.axis_index("pb")
+    return band, lax.axis_index("pix") == 1, lax.rem(lax.axis_index("tm"), 2) == band
 
 
 def packed(tile):
@@ -80,7 +85,7 @@
     )(label, *pieces)
 
 
-def chunk_kernel(start, first, last, place_ref, own_ref, label_ref, far_ref, near_ref, *refs):
+def chunk_kernel(start, first, last, own_ref, label_ref, far_ref, near_ref, *refs):
     if first:
         before_ref = None
     else:
@@ -90,7 +95,8 @@
     else:
         (acc,) = refs
     half = RADII * ROWS
-    later = place_ref[0] == 1
+    band, second, has_near = place()
+    later = band == 1
     pieces = strips(near_ref.shape[2])
 
     def add(with_near):
@@ -110,11 +116,11 @@
         if not with_near:
             acc[count:] = jnp.zeros_like(acc[count:])
 
-    @pl.when(place_ref[2] == 1)
+    @pl.when(has_near)
     def _():
         add(True)
 
-    @pl.when(place_ref[2] == 0)
+    @pl.when(jnp.logical_not(has_near))
     def _():
         add(False)
 
@@ -126,30 +132,40 @@
     near_tile = acc[16 : 16 + half, :ROWS]
     far_tile = acc[16 : 16 + half, ROWS:]
     next_tile = acc[16 + half :, ROWS:]
-    second = place_ref[1] == 1
     here = (jnp.where(below, near_tile, 0.0), jnp.where(below, far_tile, near_tile))
-    after = (jnp.where(below, next_tile, 0.0), jnp.where(below, 0.0, next_tile))
     sums = acc[:8]
-    lane = lax.broadcasted_iota(jnp.int32, sums.shape, 1)
-    beside = (lane < ROWS) & (place_ref[2] == 1)
+    for ref, part in zip(out_refs[:2], (here, here[::-1])):
+        ref[: 2 * ROWS] = packed(jnp.where(second, part[1], part[0]))
+        ref[2 * ROWS :] = sums
+
+    row = lax.broadcasted_iota(jnp.int32, (ROWS, 2 * ROWS), 0)
+    lane = lax.broadcasted_iota(jnp.int32, (ROWS, 2 * ROWS), 1)
+    column = lax.rem(lane, ROWS)
+    tiles = packed(next_tile)
+    upright = tiles[:ROWS]
+    turned = tiles.T
+    turned = jnp.where(lane < ROWS, pltpu.roll(turned[:ROWS], ROWS, 1), turned[ROWS:])
+    low = jnp.where(column < row, upright, turned)
+    high = jnp.where(column < row, turned, upright)
+    diagonal = jnp.sum(jnp.where(column == row, turned, 0.0), axis=0, keepdims=True)
+    beside = (lane[:8] < ROWS) & has_near
     after_sums = jnp.where(beside, pltpu.roll(sums, ROWS, 1), 0.0)
-    for k, ((low, high), row) in enumerate(((here, sums), (after, after_sums))):
-        out_refs[2 * k][: 2 * ROWS] = packed(jnp.where(second, high, low))
-        out_refs[2 * k + 1][: 2 * ROWS] = packed(jnp.where(second, low, high))
-        out_refs[2 * k][2 * ROWS :] = row
-        out_refs[2 * k + 1][2 * ROWS :] = row
-
-
-def chunk_part(place, piece, label, start, near, far, before, last):
+    after_sums = jnp.where(row[:8] == RADII, diagonal, after_sums)
+    for ref, part in zip(out_refs[2:], ((low, high), (high, low))):
+        ref[:ROWS] = jnp.where(second, part[1], part[0])
+        ref[ROWS:] = after_sums
+
+
+def chunk_part(piece, label, start, near, far, before, last):
     size = near.shape[2]
     acc_shape = (16 + 2 * RADII * ROWS, 2 * ROWS)
-    message = (2 * ROWS + 8, 2 * ROWS)
+    here, after = (2 * ROWS + 8, 2 * ROWS), (ROWS + 8, 2 * ROWS)
     vmem = pl.BlockSpec(memory_space=pltpu.VMEM)
-    operands = [place, piece, label, far, near] + ([] if before is None else [before])
-    shapes = [message] * 4 if last else [acc_shape]
+    operands = [piece, label, far, near] + ([] if before is None else [before])
+    shapes = [here, here, after, after] if last else [acc_shape]
     return pl.pallas_call(
         functools.partial(chunk_kernel, start, before is None, last),
-        in_specs=[pl.BlockSpec(memory_space=pltpu.SMEM)] + [vmem] * (len(operands) - 1),
+        in_specs=[vmem] * len(operands),
         out_specs=[vmem] * len(shapes),
         out_shape=[jax.ShapeDtypeStruct(shape, jnp.float32) for shape in shapes],
         scratch_shapes=[pltpu.VMEM(acc_shape, jnp.float32)] if last else [],
@@ -159,49 +175,58 @@
     )(*operands)
 
 
-def final_kernel(place_ref, factor_ref, own_ref, kept_ref, *refs):
-    *message_refs, out_ref = refs
-    total = jnp.where(place_ref[0] == 0, kept_ref[...], 0.0)
-    for ref in message_refs:
-        total = total + ref[...]
+def final_kernel(factor_ref, own_ref, kept_ref, here_ref, same_ref, other_ref, out_ref):
+    band, second, _ = place()
+    first = jnp.logical_not(second)
+    here = jnp.where(band == 0, kept_ref[...], here_ref[...])
+    after = same_ref[...] + other_ref[...]
     own = own_ref[...]
-    first = place_ref[1] == 0
-    tile = total[: 2 * ROWS] + jnp.where(first, own[: 2 * ROWS], 0.0)
-    ahead, present = total[2 * ROWS :], own[2 * ROWS :]
-    lane = lax.broadcasted_iota(jnp.int32, ahead.shape, 1)
+    row = lax.broadcasted_iota(jnp.int32, (ROWS, 2 * ROWS), 0)
+    lane = lax.broadcasted_iota(jnp.int32, (ROWS, 2 * ROWS), 1)
+    column = lax.rem(lane, ROWS)
+    below, above = column < row, column > row
+
+    body = after[:ROWS]
+    upright = jnp.where(below == first, body, 0.0)
+    diagonal = jnp.where(column == row, after[ROWS + RADII : ROWS + RADII + 1], 0.0)
+    turned = jnp.where(first, jnp.where(above, body, 0.0), jnp.where(below, body, diagonal))
+    turned = jnp.concatenate([turned, turned], axis=0).T
+    turned = jnp.where(lane < ROWS, turned[:ROWS], pltpu.roll(turned[ROWS:], ROWS, 1))
+
+    ahead, present = here[2 * ROWS :] + after[ROWS:], own[2 * ROWS :]
+    left = lane[:8] < ROWS
     moved = pltpu.roll(ahead, ROWS, 1)
-    same = jnp.where(first, present, jnp.where(lane < ROWS, ahead, moved))
-    beyond = jnp.where(first == (lane < ROWS), ahead, moved)
-    t = lax.rem(lax.broadcasted_iota(jnp.int32, tile.shape, 0), ROWS)
-    s = lax.rem(lax.broadcasted_iota(jnp.int32, tile.shape, 1), ROWS)
-
-    def spread(row):
-        pairs = [jnp.where(lane[:1] < ROWS, row[a : a + 1], row[2 + a : 3 + a]) for a in range(2)]
-        return jnp.concatenate([jnp.broadcast_to(pair, (ROWS, 2 * ROWS)) for pair in pairs], axis=0)
-
-    far = jnp.where(s < t, spread(beyond), spread(same))
+    same = jnp.where(first, present, jnp.where(left, ahead, moved))
+    beyond = jnp.where(first == left, ahead, moved)
     factor = factor_ref[...]
-    tile = jnp.where(factor > 0.0, tile * factor / far, 0.0)
-    for group in range(2):
-        part = tile[:, group * ROWS : (group + 1) * ROWS]
-        twice = jnp.concatenate([part, part], axis=1)
-        for bit in range(6):
-            turned = pltpu.roll(twice, 128 - (1 << bit), 1)
-            twice = jnp.where((t >> bit) & 1 == 1, turned, twice)
-        for a in range(2):
-            out_ref[0, 2 * group + a] = twice[a * ROWS : (a + 1) * ROWS, :ROWS]
-
-
-def final_part(place, factor, own, kept, messages):
+    for a, added in enumerate((upright, turned)):
+        rows = slice(a * ROWS, (a + 1) * ROWS)
+        tile = here[rows] + added + jnp.where(first, own[rows], 0.0)
+        near_sum, far_sum = (
+            jnp.where(left[:1], sums[a : a + 1], sums[2 + a : 3 + a]) for sums in (same, beyond)
+        )
+        far = jnp.where(below, far_sum, near_sum)
+        tile = jnp.where(factor[rows] > 0.0, tile * factor[rows] / far, 0.0)
+        swapped = pltpu.roll(tile, ROWS, 1)
+        for group, twice in enumerate((jnp.where(lane < ROWS, tile, swapped), jnp.where(lane < ROWS, swapped, tile))):
+            blocks = [pltpu.roll(twice[t : t + 8], 2 * ROWS - t, 1) if t else twice[:8] for t in range(0, ROWS, 8)]
+            twice = jnp.concatenate(blocks, axis=0)
+            for bit in range(3):
+                moved = pltpu.roll(twice, 2 * ROWS - (1 << bit), 1)
+                twice = jnp.where((row >> bit) & 1 == 1, moved, twice)
+            out_ref[0, 2 * group + a] = twice[:, :ROWS]
+
+
+def final_part(factor, own, kept, messages):
     vmem = pl.BlockSpec(memory_space=pltpu.VMEM)
     return pl.pallas_call(
         final_kernel,
-        in_specs=[pl.BlockSpec(memory_space=pltpu.SMEM)] + [vmem] * (3 + len(messages)),
+        in_specs=[vmem] * (3 + len(messages)),
         out_specs=vmem,
         out_shape=jax.ShapeDtypeStruct((1, RADII, ROWS, ROWS), jnp.float32),
         compiler_params=pltpu.CompilerParams(vmem_limit_bytes=8 << 20),
         name="normalise_and_skew",
-    )(place, factor, own, kept, *messages)
+    )(factor, own, kept, *messages)
 
 
 def factors(own, lag_width):
@@ -220,8 +245,6 @@
     devices = lax.axis_size("tm")
     pixels = frames.shape[2]
     pb, pix = lax.axis_index("pb"), lax.axis_index("pix")
-    has_near = (lax.axis_index("tm") % 2 == pb)
-    place = jnp.stack([pb, pix, has_near.astype(jnp.int32)]).astype(jnp.int32)
 
     def far_pairs():
         for i in range(devices):
@@ -269,31 +292,22 @@
         near, far = received[index]
         last = index == len(SIZES) - 1
         before = states[-1] if states else None
-        result = chunk_part(place, pieces[index], annulus_label, starts[index], near, far, before, last)
+        result = chunk_part(pieces[index], annulus_label, starts[index], near, far, before, last)
         states.append(result if last else result[0])
     state = states[-1]
     here_same, here_other, after_same, after_other = state
 
-    def message_pairs(step, flip):
-        for i in range(devices):
-            for band in range(2):
-                target = i ^ 1 if step else (i if band == 0 else i - 2)
-                if not 0 <= target < devices or not (step or flip or band):
-                    continue
-                for x in range(2):
-                    yield (i * 2 + x) * 2 + band, (target * 2 + (x ^ flip)) * 2 + band
-
-    everywhere = ("tm", "pix", "pb")
-    messages = [
-        lax.ppermute(message, everywhere, list(message_pairs(step, flip)))
-        for message, step, flip in (
-            (here_same, 0, 0),
-            (here_other, 0, 1),
-            (after_same, 1, 0),
-            (after_other, 1, 1),
-        )
-    ]
-    return final_part(place, factor, own, here_same, messages)
+    def swapped(message, flip):
+        pairs = [
+            (i * 2 + x, (i ^ 1) * 2 + (x ^ flip)) for i in range(devices) for x in range(2) if i ^ 1 < devices
+        ]
+        return lax.ppermute(message, ("tm", "pix"), pairs)
+
+    beside = lax.ppermute(here_other, "pix", [(0, 1), (1, 0)])
+    after = [swapped(after_same, 0), swapped(after_other, 1)]
+    here = here_same + beside
+    handed = lax.ppermute(here, tm_pb, [(2 * i + 1, 2 * i - 3) for i in range(2, devices)])
+    return final_part(factor, own, here, [handed, *after])
 
 
 def solution(mesh):

time: 69.4 us -> 66.8 us (0.963)
  the two profiles are of different devices: /device:TPU:0 before, /device:TPU:7 now
where the time goes in v3:
time: 66.8 us; the launch traced here: 66.3 us
  starting transfers between devices  21 us (31%)
  Pallas kernels  19.7 us (29%)
  waiting for transfers between devices  18.8 us (28%)
  local copies, waits for them, and re-layouts  6.31 us (9%)
    pallas_call x4, Pallas kernels, chunk_part(): pl.pallas_call(functools.partial(chunk_kernel, start, before is None, las...  13.7 us
    ppermute x4, starting transfers between devices, sent(): far = lax.ppermute(piece, tm_pb, list(far_pairs()))  11.4 us
    ppermute x4, waiting for transfers between devices, sent(): near = lax.ppermute(piece, tm_pb, list(near_pairs()))  10.6 us
    slice x4, local copies, waits for them, and re-layouts, shards(): lax.slice_in_dim(frames, start, start + count * unit, axis=2)  5.37 us
    ppermute x4, starting transfers between devices, sent(): near = lax.ppermute(piece, tm_pb, list(near_pairs()))  5.28 us
    pallas_call x1, Pallas kernels, own_part(): pl.pallas_call(own_kernel, in_specs=[vmem] * (1 + len(pieces)), out_specs...  4.81 us
    ppermute x1, waiting for transfers between devices, shards(): own = own + lax.ppermute(own, 'pix', [(0, 1), (1, 0)])  3.73 us
    ppermute x1, waiting for transfers between devices, shards(): lax.ppermute(here, tm_pb, [(2 * i + 1, 2 * i - 3) for i in range(2, devic...  3.64 us
  transfers between devices with their start and end apart: 13, of which 7 were waited for; matrix products, arithmetic and copies ran while one was open for 6% of the time, Pallas kernels for 26%

profile of v3, /device:TPU:7, one launch (start us, length us, event | category | flops | bytes accessed | tf_op | source)
XLA Modules:
  0.0 66.3 jit_solution(8865182942729394877)
XLA Ops:
  0.0 1.6 %slice.27.refs_0_.own_ref = bf16[1,64,14336]{2,1,0:T(8,128)(2,1)S(1)} slice(bf16[1,64,32768]{2,1,0:T(8,128)(2,1)} %param.3), slice={[0:1], [0:64], [0:14336]} | slice | bytes 3670016 | tf_op jit(solution)/shard_map/slice | solution.py:271
  1.6 4.6 %collective-permute-start.7 = (bf16[1,64,14336]{2,1,0:T(8,128)(2,1)S(1)}, bf16[1,64,14336]{2,1,0:T(8,128)(2,1)}, u32[]{:S(2)}, u32[]{:S(2)}) collective-permute-start(bf16[1,64,14336]{2,1,0:T(8,128)(2,1)S(1)} %slice.27.refs_0_.own_ref), channel_id=1, source_target_pairs={{1,9},{5,13},{8,0},{9,17},{12,4},{13,21},{16,8},{17,25},{20,12},{2... | collective-permute-start | bytes 5505032 | tf_op jit(solution)/shard_map/ppermute | solution.py:265
  6.2 1.3 %collective-permute-start.8 = (bf16[1,64,14336]{2,1,0:T(8,128)(2,1)S(1)}, bf16[1,64,14336]{2,1,0:T(8,128)(2,1)}, u32[]{:S(2)}, u32[]{:S(2)}) collective-permute-start(bf16[1,64,14336]{2,1,0:T(8,128)(2,1)S(1)} %slice.27.refs_0_.own_ref), channel_id=1, source_target_pairs={{1,5},{4,0},{9,13},{12,8},{17,21},{20,16},{25,29},{28,24},{3,7},{6... | collective-permute-start | bytes 5505032 | tf_op jit(solution)/shard_map/ppermute | solution.py:264
  7.5 1.4 %slice.28.refs_1_.own_ref = bf16[1,64,10240]{2,1,0:T(8,128)(2,1)S(1)} slice(bf16[1,64,32768]{2,1,0:T(8,128)(2,1)} %param.3), slice={[0:1], [0:64], [14336:24576]} | slice | bytes 2621440 | tf_op jit(solution)/shard_map/slice | solution.py:271
  8.9 3.0 %collective-permute-start.5 = (bf16[1,64,10240]{2,1,0:T(8,128)(2,1)S(1)}, bf16[1,64,10240]{2,1,0:T(8,128)(2,1)}, u32[]{:S(2)}, u32[]{:S(2)}) collective-permute-start(bf16[1,64,10240]{2,1,0:T(8,128)(2,1)S(1)} %slice.28.refs_1_.own_ref), channel_id=1, source_target_pairs={{1,9},{5,13},{8,0},{9,17},{12,4},{13,21},{16,8},{17,25},{20,12},{2... | collective-permute-start | bytes 3932168 | tf_op jit(solution)/shard_map/ppermute | solution.py:265
  12.0 1.3 %collective-permute-start.6 = (bf16[1,64,10240]{2,1,0:T(8,128)(2,1)S(1)}, bf16[1,64,10240]{2,1,0:T(8,128)(2,1)}, u32[]{:S(2)}, u32[]{:S(2)}) collective-permute-start(bf16[1,64,10240]{2,1,0:T(8,128)(2,1)S(1)} %slice.28.refs_1_.own_ref), channel_id=1, source_target_pairs={{1,5},{4,0},{9,13},{12,8},{17,21},{20,16},{25,29},{28,24},{3,7},{6... | collective-permute-start | bytes 3932168 | tf_op jit(solution)/shard_map/ppermute | solution.py:264
  13.3 1.2 %slice.29.refs_2_.own_ref = bf16[1,64,6144]{2,1,0:T(8,128)(2,1)S(1)} slice(bf16[1,64,32768]{2,1,0:T(8,128)(2,1)} %param.3), slice={[0:1], [0:64], [24576:30720]} | slice | bytes 1572864 | tf_op jit(solution)/shard_map/slice | solution.py:271
  14.5 1.2 %slice.30.refs_3_.own_ref = bf16[1,64,2048]{2,1,0:T(8,128)(2,1)S(1)} slice(bf16[1,64,32768]{2,1,0:T(8,128)(2,1)} %param.3), slice={[0:1], [0:64], [30720:32768]} | slice | bytes 524288 | tf_op jit(solution)/shard_map/slice | solution.py:271
  15.6 4.8 %own_tile_and_sums.1 = f32[136,128]{1,0:T(8,128)S(1)} custom-call(s32[1,32768]{1,0:T(1,128)S(1)} %copy-done.2, bf16[1,64,14336]{2,1,0:T(8,128)(2,1)S(1)} %slice.27.refs_0_.own_ref, bf16[1,64,10240]{2,1,0:T(8,128)(2,1)S(1)} %slice.28.refs_1_.own_ref, bf16[1,64,6144]{2,1,0:T(8,128)(2,1)S(1)} %slice.29.refs_2_.own_ref, ...), custom_call_target="tpu_custom_call" | custom-call | flops 8589934592 | bytes 16777216 | tf_op jit(solution)/shard_map/own_tile_and_sums/pallas_call | solution.py:77
  20.5 0.3 collective-permute-start
  20.8 3.7 %collective-permute-done = f32[136,128]{1,0:T(8,128)S(1)} collective-permute-done((f32[136,128]{1,0:T(8,128)S(1)}, f32[136,128]{1,0:T(8,128)S(1)}, u32[]{:S(2)}, u32[]{:S(2)}) %collective-permute-start) | collective-permute-done | bytes 69664 | tf_op jit(solution)/shard_map/ppermute | solution.py:274
  24.5 1.8 %collective-permute-start.3 = (bf16[1,64,6144]{2,1,0:T(8,128)(2,1)}, bf16[1,64,6144]{2,1,0:T(8,128)(2,1)S(1)}, u32[]{:S(2)}, u32[]{:S(2)}) collective-permute-start(bf16[1,64,6144]{2,1,0:T(8,128)(2,1)} %copy-done), channel_id=1, source_target_pairs={{1,9},{5,13},{8,0},{9,17},{12,4},{13,21},{16,8},{17,25},{20,12},{2... | collective-permute-start | bytes 2359304 | tf_op jit(solution)/shard_map/ppermute | solution.py:265
  26.3 0.1 fusion.5
  26.5 1.3 %collective-permute-start.4 = (bf16[1,64,6144]{2,1,0:T(8,128)(2,1)}, bf16[1,64,6144]{2,1,0:T(8,128)(2,1)S(1)}, u32[]{:S(2)}, u32[]{:S(2)}) collective-permute-start(bf16[1,64,6144]{2,1,0:T(8,128)(2,1)} %copy-done), channel_id=1, source_target_pairs={{1,5},{4,0},{9,13},{12,8},{17,21},{20,16},{25,29},{28,24},{3,7},{6... | collective-permute-start | bytes 2359304 | tf_op jit(solution)/shard_map/ppermute | solution.py:264
  27.8 2.8 %collective-permute-done.8.near_ref = bf16[1,64,14336]{2,1,0:T(8,128)(2,1)} collective-permute-done((bf16[1,64,14336]{2,1,0:T(8,128)(2,1)S(1)}, bf16[1,64,14336]{2,1,0:T(8,128)(2,1)}, u32[]{:S(2)}, u32[]{:S(2)}) %collective-permute-start.8) | collective-permute-done | bytes 1835040 | tf_op jit(solution)/shard_map/ppermute | solution.py:264
  30.6 2.0 %collective-permute-start.1 = (bf16[1,64,2048]{2,1,0:T(8,128)(2,1)S(1)}, bf16[1,64,2048]{2,1,0:T(8,128)(2,1)S(1)}, u32[]{:S(2)}, u32[]{:S(2)}) collective-permute-start(bf16[1,64,2048]{2,1,0:T(8,128)(2,1)S(1)} %slice.30.refs_3_.own_ref), channel_id=1, source_target_pairs={{1,9},{5,13},{8,0},{9,17},{12,4},{13,21},{16,8},{17,25},{20,12},{2... | collective-permute-start | bytes 786440 | tf_op jit(solution)/shard_map/ppermute | solution.py:265
  32.6 0.9 %copy-done.3 = s32[1,32768]{1,0:T(1,128)S(1)} copy-done((s32[1,32768]{1,0:T(1,128)S(1)}, s32[1,32768]{1,0:T(1,128)}, u32[]{:S(2)}) %copy-start.3) | copy-done | bytes 131096
  33.5 6.1 %chunk_tiles.4.refs_0_ = f32[528,128]{1,0:T(8,128)S(1)} custom-call(bf16[1,64,14336]{2,1,0:T(8,128)(2,1)S(1)} %slice.27.refs_0_.own_ref, s32[1,32768]{1,0:T(1,128)S(1)} %copy-done.3, bf16[1,64,14336]{2,1,0:T(8,128)(2,1)} %collective-permute-done.7.far_ref, bf16[1,64,14336]{2,1,0:T(8,128)(2,1)} %collective-permute-done.8.near_ref), custom_call_target="tpu_custom_call" | custom-call | flops 7516192768 | bytes 7340032 | tf_op jit(solution)/shard_map/chunk_tiles/pallas_call | solution.py:166
  39.6 1.4 %collective-permute-start.2 = (bf16[1,64,2048]{2,1,0:T(8,128)(2,1)S(1)}, bf16[1,64,2048]{2,1,0:T(8,128)(2,1)S(1)}, u32[]{:S(2)}, u32[]{:S(2)}) collective-permute-start(bf16[1,64,2048]{2,1,0:T(8,128)(2,1)S(1)} %slice.30.refs_3_.own_ref), channel_id=1, source_target_pairs={{1,5},{4,0},{9,13},{12,8},{17,21},{20,16},{25,29},{28,24},{3,7},{6... | collective-permute-start | bytes 786440 | tf_op jit(solution)/shard_map/ppermute | solution.py:264
  41.0 3.5 %collective-permute-done.6.near_ref = bf16[1,64,10240]{2,1,0:T(8,128)(2,1)} collective-permute-done((bf16[1,64,10240]{2,1,0:T(8,128)(2,1)S(1)}, bf16[1,64,10240]{2,1,0:T(8,128)(2,1)}, u32[]{:S(2)}, u32[]{:S(2)}) %collective-permute-start.6) | collective-permute-done | bytes 1310752 | tf_op jit(solution)/shard_map/ppermute | solution.py:264
  44.5 4.7 %chunk_tiles.5.refs_0_ = f32[528,128]{1,0:T(8,128)S(1)} custom-call(bf16[1,64,10240]{2,1,0:T(8,128)(2,1)S(1)} %slice.28.refs_1_.own_ref, s32[1,32768]{1,0:T(1,128)S(1)} %copy-done.4, bf16[1,64,10240]{2,1,0:T(8,128)(2,1)} %collective-permute-done.5.far_ref, bf16[1,64,10240]{2,1,0:T(8,128)(2,1)} %collective-permute-done.6.near_ref, ...), custom_call_target="tpu_custom_call" | custom-call | flops 5368709120 | bytes 5242880 | tf_op jit(solution)/shard_map/chunk_tiles/pallas_call | solution.py:166
  49.2 3.4 %collective-permute-done.4.near_ref = bf16[1,64,6144]{2,1,0:T(8,128)(2,1)S(1)} collective-permute-done((bf16[1,64,6144]{2,1,0:T(8,128)(2,1)}, bf16[1,64,6144]{2,1,0:T(8,128)(2,1)S(1)}, u32[]{:S(2)}, u32[]{:S(2)}) %collective-permute-start.4) | collective-permute-done | bytes 786464 | tf_op jit(solution)/shard_map/ppermute | solution.py:264
  52.7 1.9 %chunk_tiles.6.refs_0_ = f32[528,128]{1,0:T(8,128)S(1)} custom-call(bf16[1,64,6144]{2,1,0:T(8,128)(2,1)S(1)} %copy-done.1, s32[1,32768]{1,0:T(1,128)S(1)} %copy-done.4, bf16[1,64,6144]{2,1,0:T(8,128)(2,1)S(1)} %collective-permute-done.3.far_ref, bf16[1,64,6144]{2,1,0:T(8,128)(2,1)S(1)} %collective-permute-done.4.near_ref, f32[528,128]{1,0:T(8,128)S(1)} %chunk_tiles.5.refs_0_), custom_call_target="tpu_custom_call" | custom-call | flops 3221225472 | bytes 3145728 | tf_op jit(solution)/shard_map/chunk_tiles/pallas_call | solution.py:166
  54.5 0.9 %collective-permute-done.2.near_ref = bf16[1,64,2048]{2,1,0:T(8,128)(2,1)S(1)} collective-permute-done((bf16[1,64,2048]{2,1,0:T(8,128)(2,1)S(1)}, bf16[1,64,2048]{2,1,0:T(8,128)(2,1)S(1)}, u32[]{:S(2)}, u32[]{:S(2)}) %collective-permute-start.2) | collective-permute-done | bytes 262176 | tf_op jit(solution)/shard_map/ppermute | solution.py:264
  55.5 1.0 %chunk_tiles.7 = (f32[136,128]{1,0:T(8,128)S(1)}, f32[136,128]{1,0:T(8,128)S(1)}, f32[72,128]{1,0:T(8,128)S(1)}, f32[72,128]{1,0:T(8,128)S(1)}) custom-call(bf16[1,64,2048]{2,1,0:T(8,128)(2,1)S(1)} %slice.30.refs_3_.own_ref, s32[1,32768]{1,0:T(1,128)S(1)} %copy-done.4, bf16[1,64,2048]{2,1,0:T(8,128)(2,1)S(1)} %collective-permute-done.1.far_ref, ...), custom_call_target="tpu_custom_call" | custom-call | flops 1073741824 | bytes 1048576 | tf_op jit(solution)/shard_map/chunk_tiles/pallas_call | solution.py:166
  56.4 0.3 collective-permute-start.9
  56.9 2.4 %collective-permute-start.12 = (f32[72,128]{1,0:T(8,128)S(1)}, f32[72,128]{1,0:T(8,128)S(1)}, u32[]{:S(2)}, u32[]{:S(2)}) collective-permute-start(f32[72,128]{1,0:T(8,128)S(1)} %get-tuple-element.12), channel_id=1, source_target_pairs={{0,6},{2,4},{4,2},{6,0},{8,14},{10,12},{12,10},{14,8},{16,22},{18,... | collective-permute-start | bytes 110600 | tf_op jit(solution)/shard_map/ppermute | solution.py:304
  59.2 0.8 %collective-permute-done.9 = f32[136,128]{1,0:T(8,128)S(1)} collective-permute-done((f32[136,128]{1,0:T(8,128)S(1)}, f32[136,128]{1,0:T(8,128)S(1)}, u32[]{:S(2)}, u32[]{:S(2)}) %collective-permute-start.9) | collective-permute-done | bytes 69664 | tf_op jit(solution)/shard_map/ppermute | solution.py:306
  60.1 1.3 %collective-permute-start.10 = (f32[136,128]{1,0:T(8,128)S(1)}, f32[136,128]{1,0:T(8,128)S(1)}, u32[]{:S(2)}, u32[]{:S(2)}) collective-permute-start(f32[136,128]{1,0:T(8,128)S(1)} %add.36.kept_ref), channel_id=1, source_target_pairs={{9,1},{13,5},{17,9},{21,13},{25,17},{29,21},{11,3},{15,7},{19,11},... | collective-permute-start | bytes 208904 | tf_op jit(solution)/shard_map/ppermute | solution.py:309
  61.4 0.1 pad_maximum_fusion.factor_ref
  61.5 3.6 %collective-permute-done.10.here_ref = f32[136,128]{1,0:T(8,128)S(1)} collective-permute-done((f32[136,128]{1,0:T(8,128)S(1)}, f32[136,128]{1,0:T(8,128)S(1)}, u32[]{:S(2)}, u32[]{:S(2)}) %collective-permute-start.10) | collective-permute-done | bytes 69664 | tf_op jit(solution)/shard_map/ppermute | solution.py:309
  65.2 1.2 %normalise_and_skew.1 = f32[1,4,64,64]{3,2,1,0:T(8,128)} custom-call(f32[128,128]{1,0:T(8,128)S(1)} %pad_maximum_fusion.factor_ref, f32[136,128]{1,0:T(8,128)S(1)} %add.35.own_ref, f32[136,128]{1,0:T(8,128)S(1)} %add.36.kept_ref, f32[136,128]{1,0:T(8,128)S(1)} %collective-permute-done.10.here_ref, f32[72,128]{1,0:T(8,128)S(1)} %collective-permute-done.11.same_ref, ...), custom_call_target="tpu_custom_call" | custom-call | tf_op jit(solution)/shard_map/normalise_and_skew/pallas_call | solution.py:222
  (23 shorter events, 0.2 us)
Async XLA Ops:
  1.6 14.0 %copy-start.2 = (s32[1,32768]{1,0:T(1,128)S(1)}, s32[1,32768]{1,0:T(1,128)}, u32[]{:S(2)}) copy-start(s32[1,32768]{1,0:T(1,128)} %label_ref.9) | copy-start | bytes 393220
  1.6 24.8 %collective-permute-start.7 = (bf16[1,64,14336]{2,1,0:T(8,128)(2,1)S(1)}, bf16[1,64,14336]{2,1,0:T(8,128)(2,1)}, u32[]{:S(2)}, u32[]{:S(2)}) collective-permute-start(bf16[1,64,14336]{2,1,0:T(8,128)(2,1)S(1)} %slice.27.refs_0_.own_ref), channel_id=1, source_target_pairs={{1,9},{5,13},{8,0},{9,17},{12,4},{13,21},{16,8},{17,25},{20,12},{2... | collective-permute-start | bytes 5505032 | tf_op jit(solution)/shard_map/ppermute | solution.py:265
  6.2 24.4 %collective-permute-start.8 = (bf16[1,64,14336]{2,1,0:T(8,128)(2,1)S(1)}, bf16[1,64,14336]{2,1,0:T(8,128)(2,1)}, u32[]{:S(2)}, u32[]{:S(2)}) collective-permute-start(bf16[1,64,14336]{2,1,0:T(8,128)(2,1)S(1)} %slice.27.refs_0_.own_ref), channel_id=1, source_target_pairs={{1,5},{4,0},{9,13},{12,8},{17,21},{20,16},{25,29},{28,24},{3,7},{6... | collective-permute-start | bytes 5505032 | tf_op jit(solution)/shard_map/ppermute | solution.py:264
  8.9 30.7 %collective-permute-start.5 = (bf16[1,64,10240]{2,1,0:T(8,128)(2,1)S(1)}, bf16[1,64,10240]{2,1,0:T(8,128)(2,1)}, u32[]{:S(2)}, u32[]{:S(2)}) collective-permute-start(bf16[1,64,10240]{2,1,0:T(8,128)(2,1)S(1)} %slice.28.refs_1_.own_ref), channel_id=1, source_target_pairs={{1,9},{5,13},{8,0},{9,17},{12,4},{13,21},{16,8},{17,25},{20,12},{2... | collective-permute-start | bytes 3932168 | tf_op jit(solution)/shard_map/ppermute | solution.py:265
  12.0 32.6 %collective-permute-start.6 = (bf16[1,64,10240]{2,1,0:T(8,128)(2,1)S(1)}, bf16[1,64,10240]{2,1,0:T(8,128)(2,1)}, u32[]{:S(2)}, u32[]{:S(2)}) collective-permute-start(bf16[1,64,10240]{2,1,0:T(8,128)(2,1)S(1)} %slice.28.refs_1_.own_ref), channel_id=1, source_target_pairs={{1,5},{4,0},{9,13},{12,8},{17,21},{20,16},{25,29},{28,24},{3,7},{6... | collective-permute-start | bytes 3932168 | tf_op jit(solution)/shard_map/ppermute | solution.py:264
  14.4 6.0 %copy-start = (bf16[1,64,6144]{2,1,0:T(8,128)(2,1)}, bf16[1,64,6144]{2,1,0:T(8,128)(2,1)S(1)}, u32[]{:S(2)}) copy-start(bf16[1,64,6144]{2,1,0:T(8,128)(2,1)S(1)} %slice.29.refs_2_.own_ref) | copy-start | bytes 2359300
  15.6 10.7 %copy-start.5 = (s32[1,4]{1,0:T(1,128)S(1)}, s32[1,4]{1,0:T(1,128)}, u32[]{:S(2)}) copy-start(s32[1,4]{1,0:T(1,128)} %param.5) | copy-start | bytes 52
  20.5 4.1 %collective-permute-start = (f32[136,128]{1,0:T(8,128)S(1)}, f32[136,128]{1,0:T(8,128)S(1)}, u32[]{:S(2)}, u32[]{:S(2)}) collective-permute-start(f32[136,128]{1,0:T(8,128)S(1)} %own_tile_and_sums.1), channel_id=1, source_target_pairs={{0,2},{2,0},{1,3},{3,1},{4,6},{6,4},{5,7},{7,5},{8,10},{10,8},{9,1... | collective-permute-start | bytes 208904 | tf_op jit(solution)/shard_map/ppermute | solution.py:274
  24.5 24.7 %collective-permute-start.3 = (bf16[1,64,6144]{2,1,0:T(8,128)(2,1)}, bf16[1,64,6144]{2,1,0:T(8,128)(2,1)S(1)}, u32[]{:S(2)}, u32[]{:S(2)}) collective-permute-start(bf16[1,64,6144]{2,1,0:T(8,128)(2,1)} %copy-done), channel_id=1, source_target_pairs={{1,9},{5,13},{8,0},{9,17},{12,4},{13,21},{16,8},{17,25},{20,12},{2... | collective-permute-start | bytes 2359304 | tf_op jit(solution)/shard_map/ppermute | solution.py:265
  26.3 18.2 %copy-start.4 = (s32[1,32768]{1,0:T(1,128)S(1)}, s32[1,32768]{1,0:T(1,128)}, u32[]{:S(2)}) copy-start(s32[1,32768]{1,0:T(1,128)} %label_ref.9) | copy-start | bytes 393220
  26.5 26.2 %collective-permute-start.4 = (bf16[1,64,6144]{2,1,0:T(8,128)(2,1)}, bf16[1,64,6144]{2,1,0:T(8,128)(2,1)S(1)}, u32[]{:S(2)}, u32[]{:S(2)}) collective-permute-start(bf16[1,64,6144]{2,1,0:T(8,128)(2,1)} %copy-done), channel_id=1, source_target_pairs={{1,5},{4,0},{9,13},{12,8},{17,21},{20,16},{25,29},{28,24},{3,7},{6... | collective-permute-start | bytes 2359304 | tf_op jit(solution)/shard_map/ppermute | solution.py:264
  30.6 24.0 %collective-permute-start.1 = (bf16[1,64,2048]{2,1,0:T(8,128)(2,1)S(1)}, bf16[1,64,2048]{2,1,0:T(8,128)(2,1)S(1)}, u32[]{:S(2)}, u32[]{:S(2)}) collective-permute-start(bf16[1,64,2048]{2,1,0:T(8,128)(2,1)S(1)} %slice.30.refs_3_.own_ref), channel_id=1, source_target_pairs={{1,9},{5,13},{8,0},{9,17},{12,4},{13,21},{16,8},{17,25},{20,12},{2... | collective-permute-start | bytes 786440 | tf_op jit(solution)/shard_map/ppermute | solution.py:265
  32.6 0.9 %copy-start.3 = (s32[1,32768]{1,0:T(1,128)S(1)}, s32[1,32768]{1,0:T(1,128)}, u32[]{:S(2)}) copy-start(s32[1,32768]{1,0:T(1,128)} %label_ref.9) | copy-start | bytes 393220
  39.6 13.1 %copy-start.1 = (bf16[1,64,6144]{2,1,0:T(8,128)(2,1)S(1)}, bf16[1,64,6144]{2,1,0:T(8,128)(2,1)}, u32[]{:S(2)}) copy-start(bf16[1,64,6144]{2,1,0:T(8,128)(2,1)} %copy-done) | copy-start | bytes 2359300
  39.6 15.8 %collective-permute-start.2 = (bf16[1,64,2048]{2,1,0:T(8,128)(2,1)S(1)}, bf16[1,64,2048]{2,1,0:T(8,128)(2,1)S(1)}, u32[]{:S(2)}, u32[]{:S(2)}) collective-permute-start(bf16[1,64,2048]{2,1,0:T(8,128)(2,1)S(1)} %slice.30.refs_3_.own_ref), channel_id=1, source_target_pairs={{1,5},{4,0},{9,13},{12,8},{17,21},{20,16},{25,29},{28,24},{3,7},{6... | collective-permute-start | bytes 786440 | tf_op jit(solution)/shard_map/ppermute | solution.py:264
  56.4 3.6 %collective-permute-start.9 = (f32[136,128]{1,0:T(8,128)S(1)}, f32[136,128]{1,0:T(8,128)S(1)}, u32[]{:S(2)}, u32[]{:S(2)}) collective-permute-start(f32[136,128]{1,0:T(8,128)S(1)} %get-tuple-element.10), channel_id=1, source_target_pairs={{0,2},{2,0},{1,3},{3,1},{4,6},{6,4},{5,7},{7,5},{8,10},{10,8},{9,1... | collective-permute-start | bytes 208904 | tf_op jit(solution)/shard_map/ppermute | solution.py:306
  56.8 4.7 %collective-permute-start.11 = (f32[72,128]{1,0:T(8,128)S(1)}, f32[72,128]{1,0:T(8,128)S(1)}, u32[]{:S(2)}, u32[]{:S(2)}) collective-permute-start(f32[72,128]{1,0:T(8,128)S(1)} %get-tuple-element.11), channel_id=1, source_target_pairs={{0,4},{2,6},{4,0},{6,2},{8,12},{10,14},{12,8},{14,10},{16,20},{18,... | collective-permute-start | bytes 110600 | tf_op jit(solution)/shard_map/ppermute | solution.py:304
  56.9 4.6 %collective-permute-start.12 = (f32[72,128]{1,0:T(8,128)S(1)}, f32[72,128]{1,0:T(8,128)S(1)}, u32[]{:S(2)}, u32[]{:S(2)}) collective-permute-start(f32[72,128]{1,0:T(8,128)S(1)} %get-tuple-element.12), channel_id=1, source_target_pairs={{0,6},{2,4},{4,2},{6,0},{8,14},{10,12},{12,10},{14,8},{16,22},{18,... | collective-permute-start | bytes 110600 | tf_op jit(solution)/shard_map/ppermute | solution.py:304
  60.1 5.1 %collective-permute-start.10 = (f32[136,128]{1,0:T(8,128)S(1)}, f32[136,128]{1,0:T(8,128)S(1)}, u32[]{:S(2)}, u32[]{:S(2)}) collective-permute-start(f32[136,128]{1,0:T(8,128)S(1)} %add.36.kept_ref), channel_id=1, source_target_pairs={{9,1},{13,5},{17,9},{21,13},{25,17},{29,21},{11,3},{15,7},{19,11},... | collective-permute-start | bytes 208904 | tf_op jit(solution)/shard_map/ppermute | solution.py:309

commit v4 on v3

--- a/solution.py
+++ b/solution.py
@@ -13,7 +13,6 @@
 ROWS = 64
 UNITS = 16
 SIZES = (7, 5, 3, 1)
-GATES = (None, None, None, None)
 STRIP = 2048
 NT = (((1,), (1,)), ((), ()))
 
@@ -85,11 +84,18 @@
     )(label, *pieces)
 
 
-def chunk_kernel(start, first, last, own_ref, label_ref, far_ref, near_ref, *refs):
+def chunk_kernel(start, first, last, own_ref, label_ref, *refs):
+    if first:
+        far_alone_ref, near_ref, far_ref, *refs = refs
+    else:
+        far_ref, near_ref, *refs = refs
+        far_alone_ref = far_ref
     if first:
         before_ref = None
     else:
         before_ref, *refs = refs
+    if not last:
+        _, *refs = refs
     if last:
         *out_refs, acc = refs
     else:
@@ -101,8 +107,9 @@
 
     def add(with_near):
         total = None
+        sources = (own_ref, near_ref, far_ref if with_near else far_alone_ref)
         for begin, end in pieces:
-            own, near, far = (ref[0, :, begin:end] for ref in (own_ref, near_ref, far_ref))
+            own, near, far = (ref[0, :, begin:end] for ref in sources)
             earliest = jnp.where(later, far, own)
             latest = jnp.where(later, own, far)
             label = label_ref[:, start + begin : start + end]
@@ -156,12 +163,14 @@
         ref[ROWS:] = after_sums
 
 
-def chunk_part(piece, label, start, near, far, before, last):
-    size = near.shape[2]
+def chunk_part(piece, label, start, far, near, before, awaited, last):
+    size = piece.shape[2]
     acc_shape = (16 + 2 * RADII * ROWS, 2 * ROWS)
     here, after = (2 * ROWS + 8, 2 * ROWS), (ROWS + 8, 2 * ROWS)
     vmem = pl.BlockSpec(memory_space=pltpu.VMEM)
-    operands = [piece, label, far, near] + ([] if before is None else [before])
+    operands = [piece, label, far[0], near, *far[1:]] + ([] if before is None else [before])
+    if not last:
+        operands.append(awaited)
     shapes = [here, here, after, after] if last else [acc_shape]
     return pl.pallas_call(
         functools.partial(chunk_kernel, start, before is None, last),
@@ -246,10 +255,10 @@
     pixels = frames.shape[2]
     pb, pix = lax.axis_index("pb"), lax.axis_index("pix")
 
-    def far_pairs():
+    def far_pairs(parities):
         for i in range(devices):
             for band, target in ((0, i - 2), (1, i + 2)):
-                if 0 <= target < devices:
+                if 0 <= target < devices and (i % 2 == band) in parities:
                     yield 2 * i + band, 2 * target + band
 
     def near_pairs():
@@ -260,10 +269,16 @@
 
     tm_pb = ("tm", "pb")
 
-    def sent(piece):
+    def sent(piece, first):
+        def far(*parities):
+            return lax.ppermute(piece, tm_pb, list(far_pairs(parities)))
+
+        if not first:
+            alone = far(False, True)
+            return [alone], lax.ppermute(piece, tm_pb, list(near_pairs()))
+        alone = far(False)
         near = lax.ppermute(piece, tm_pb, list(near_pairs()))
-        far = lax.ppermute(piece, tm_pb, list(far_pairs()))
-        return near, far
+        return [alone, far(True)], near
 
     unit = pixels // UNITS
     starts = [sum(SIZES[:index]) * unit for index in range(len(SIZES))]
@@ -271,28 +286,20 @@
         lax.slice_in_dim(frames, start, start + count * unit, axis=2) for start, count in zip(starts, SIZES)
     ]
     own = own_part(annulus_label, pieces)
+    received = [sent(piece, index == 0) for index, piece in enumerate(pieces)]
+    own, _ = lax.optimization_barrier((own, received[0]))
     own = own + lax.ppermute(own, "pix", [(0, 1), (1, 0)])
     factor = factors(own[2 * ROWS : 2 * ROWS + RADII, :ROWS], lag_width)
 
-    received, states, sendable = {}, [], list(pieces)
-
-    def send(index):
-        piece = pieces[index]
-        if GATES[index]:
-            kind, after = GATES[index]
-            gate = {"done": received.get(after), "own": own, "state": states[after] if kind == "state" else None}
-            piece, _ = lax.optimization_barrier((piece, gate[kind]))
-        received[index] = sent(piece)
-
-    for index in range(len(SIZES)):
-        for other in range(len(SIZES)):
-            gate = GATES[other]
-            if other not in received and (gate is None or gate[1] < index):
-                send(other)
-        near, far = received[index]
+    states = []
+    for index, (piece, (far, near)) in enumerate(zip(pieces, received)):
         last = index == len(SIZES) - 1
         before = states[-1] if states else None
-        result = chunk_part(pieces[index], annulus_label, starts[index], near, far, before, last)
+        awaited = own
+        if index == 0:
+            corner = lax.optimization_barrier(far[0][:, :8, :128])
+            awaited = corner + near[:, :8, :128]
+        result = chunk_part(piece, annulus_label, starts[index], far, near, before, awaited, last)
         states.append(result if last else result[0])
     state = states[-1]
     here_same, here_other, after_same, after_other = state

time: 66.8 us -> 65.9 us (0.987)
  the two profiles are of different devices: /device:TPU:7 before, /device:TPU:0 now
where the time goes in v4:
time: 65.9 us; the launch traced here: 65.4 us
  Pallas kernels  20.2 us (31%)
  starting transfers between devices  18.6 us (28%)
  waiting for transfers between devices  18.5 us (28%)
  local copies, waits for them, and re-layouts  6.99 us (11%)
  other arithmetic  0.89 us (1%)
    pallas_call x4, Pallas kernels, chunk_part(): pl.pallas_call(functools.partial(chunk_kernel, start, before is None, las...  14.2 us
    ppermute x1, waiting for transfers between devices, sent(): near = lax.ppermute(piece, tm_pb, list(near_pairs()))  10.1 us
    ppermute x5, starting transfers between devices, far(): return lax.ppermute(piece, tm_pb, list(far_pairs(parities)))  7.22 us
    ppermute x5, waiting for transfers between devices, far(): return lax.ppermute(piece, tm_pb, list(far_pairs(parities)))  6.01 us
    slice x4, local copies, waits for them, and re-layouts, shards(): lax.slice_in_dim(frames, start, start + count * unit, axis=2)  5.37 us
    pallas_call x1, Pallas kernels, own_part(): pl.pallas_call(own_kernel, in_specs=[vmem] * (1 + len(pieces)), out_specs...  4.81 us
    ppermute x3, starting transfers between devices, sent(): return ([alone], lax.ppermute(piece, tm_pb, list(near_pairs())))  3.85 us
    ppermute x1, starting transfers between devices, shards(): own = own + lax.ppermute(own, 'pix', [(0, 1), (1, 0)])  1.99 us
  transfers between devices with their start and end apart: 14, of which 8 were waited for; matrix products, arithmetic and copies ran while one was open for 8% of the time, Pallas kernels for 28%

profile of v4, /device:TPU:0, one launch (start us, length us, event | category | flops | bytes accessed | tf_op | source)
XLA Modules:
  0.0 65.4 jit_solution(1640409408432977292)
XLA Ops:
  0.0 1.6 %slice.33.refs_0_.own_ref = bf16[1,64,14336]{2,1,0:T(8,128)(2,1)S(1)} slice(bf16[1,64,32768]{2,1,0:T(8,128)(2,1)} %param.3), slice={[0:1], [0:64], [0:14336]} | slice | bytes 3670016 | tf_op jit(solution)/shard_map/slice | solution.py:286
  1.6 2.0 %collective-permute-start = (bf16[1,64,14336]{2,1,0:T(8,128)(2,1)S(1)}, bf16[1,64,14336]{2,1,0:T(8,128)(2,1)}, u32[]{:S(2)}, u32[]{:S(2)}) collective-permute-start(bf16[1,64,14336]{2,1,0:T(8,128)(2,1)S(1)} %slice.33.refs_0_.own_ref), channel_id=1, source_target_pairs={{1,9},{9,17},{12,4},{17,25},{20,12},{28,20},{3,11},{11,19},{14,6},... | collective-permute-start | bytes 5505032 | tf_op jit(solution)/shard_map/ppermute | solution.py:274
  3.7 1.3 %collective-permute-start.2 = (bf16[1,64,14336]{2,1,0:T(8,128)(2,1)S(1)}, bf16[1,64,14336]{2,1,0:T(8,128)(2,1)}, u32[]{:S(2)}, u32[]{:S(2)}) collective-permute-start(bf16[1,64,14336]{2,1,0:T(8,128)(2,1)S(1)} %slice.33.refs_0_.own_ref), channel_id=1, source_target_pairs={{1,5},{4,0},{9,13},{12,8},{17,21},{20,16},{25,29},{28,24},{3,7},{6... | collective-permute-start | bytes 5505032 | tf_op jit(solution)/shard_map/ppermute | solution.py:280
  5.0 1.3 %collective-permute-start.1 = (bf16[1,64,14336]{2,1,0:T(8,128)(2,1)S(1)}, bf16[1,64,14336]{2,1,0:T(8,128)(2,1)}, u32[]{:S(2)}, u32[]{:S(2)}) collective-permute-start(bf16[1,64,14336]{2,1,0:T(8,128)(2,1)S(1)} %slice.33.refs_0_.own_ref), channel_id=1, source_target_pairs={{5,13},{8,0},{13,21},{16,8},{21,29},{24,16},{7,15},{10,2},{15,23},... | collective-permute-start | bytes 5505032 | tf_op jit(solution)/shard_map/ppermute | solution.py:274
  6.3 1.4 %slice.34.refs_1_.own_ref = bf16[1,64,10240]{2,1,0:T(8,128)(2,1)S(1)} slice(bf16[1,64,32768]{2,1,0:T(8,128)(2,1)} %param.3), slice={[0:1], [0:64], [14336:24576]} | slice | bytes 2621440 | tf_op jit(solution)/shard_map/slice | solution.py:286
  7.7 1.3 %collective-permute-start.8 = (bf16[1,64,10240]{2,1,0:T(8,128)(2,1)S(1)}, bf16[1,64,10240]{2,1,0:T(8,128)(2,1)}, u32[]{:S(2)}, u32[]{:S(2)}) collective-permute-start(bf16[1,64,10240]{2,1,0:T(8,128)(2,1)S(1)} %slice.34.refs_1_.own_ref), channel_id=1, source_target_pairs={{1,9},{5,13},{8,0},{9,17},{12,4},{13,21},{16,8},{17,25},{20,12},{2... | collective-permute-start | bytes 3932168 | tf_op jit(solution)/shard_map/ppermute | solution.py:274
  9.0 1.3 %collective-permute-start.9 = (bf16[1,64,10240]{2,1,0:T(8,128)(2,1)S(1)}, bf16[1,64,10240]{2,1,0:T(8,128)(2,1)}, u32[]{:S(2)}, u32[]{:S(2)}) collective-permute-start(bf16[1,64,10240]{2,1,0:T(8,128)(2,1)S(1)} %slice.34.refs_1_.own_ref), channel_id=1, source_target_pairs={{1,5},{4,0},{9,13},{12,8},{17,21},{20,16},{25,29},{28,24},{3,7},{6... | collective-permute-start | bytes 3932168 | tf_op jit(solution)/shard_map/ppermute | solution.py:278
  10.3 1.2 %slice.35.refs_2_.own_ref = bf16[1,64,6144]{2,1,0:T(8,128)(2,1)S(1)} slice(bf16[1,64,32768]{2,1,0:T(8,128)(2,1)} %param.3), slice={[0:1], [0:64], [24576:30720]} | slice | bytes 1572864 | tf_op jit(solution)/shard_map/slice | solution.py:286
  11.5 1.2 %slice.36.refs_3_.own_ref = bf16[1,64,2048]{2,1,0:T(8,128)(2,1)S(1)} slice(bf16[1,64,32768]{2,1,0:T(8,128)(2,1)} %param.3), slice={[0:1], [0:64], [30720:32768]} | slice | bytes 524288 | tf_op jit(solution)/shard_map/slice | solution.py:286
  12.7 4.8 %own_tile_and_sums.1 = f32[136,128]{1,0:T(8,128)S(1)} custom-call(s32[1,32768]{1,0:T(1,128)S(1)} %copy-done.2, bf16[1,64,14336]{2,1,0:T(8,128)(2,1)S(1)} %slice.33.refs_0_.own_ref, bf16[1,64,10240]{2,1,0:T(8,128)(2,1)S(1)} %slice.34.refs_1_.own_ref, bf16[1,64,6144]{2,1,0:T(8,128)(2,1)S(1)} %slice.35.refs_2_.own_ref, ...), custom_call_target="tpu_custom_call" | custom-call | flops 8589934592 | bytes 16777216 | tf_op jit(solution)/shard_map/own_tile_and_sums/pallas_call | solution.py:76
  17.5 1.3 %collective-permute-start.6 = (bf16[1,64,6144]{2,1,0:T(8,128)(2,1)}, bf16[1,64,6144]{2,1,0:T(8,128)(2,1)S(1)}, u32[]{:S(2)}, u32[]{:S(2)}) collective-permute-start(bf16[1,64,6144]{2,1,0:T(8,128)(2,1)} %copy-done), channel_id=1, source_target_pairs={{1,9},{5,13},{8,0},{9,17},{12,4},{13,21},{16,8},{17,25},{20,12},{2... | collective-permute-start | bytes 2359304 | tf_op jit(solution)/shard_map/ppermute | solution.py:274
  18.8 10.1 %collective-permute-done.2.refs_1_ = bf16[1,64,14336]{2,1,0:T(8,128)(2,1)} collective-permute-done((bf16[1,64,14336]{2,1,0:T(8,128)(2,1)S(1)}, bf16[1,64,14336]{2,1,0:T(8,128)(2,1)}, u32[]{:S(2)}, u32[]{:S(2)}) %collective-permute-start.2) | collective-permute-done | bytes 1835040 | tf_op jit(solution)/shard_map/ppermute | solution.py:280
  28.9 1.3 %collective-permute-start.7 = (bf16[1,64,6144]{2,1,0:T(8,128)(2,1)}, bf16[1,64,6144]{2,1,0:T(8,128)(2,1)S(1)}, u32[]{:S(2)}, u32[]{:S(2)}) collective-permute-start(bf16[1,64,6144]{2,1,0:T(8,128)(2,1)} %copy-done), channel_id=1, source_target_pairs={{1,5},{4,0},{9,13},{12,8},{17,21},{20,16},{25,29},{28,24},{3,7},{6... | collective-permute-start | bytes 2359304 | tf_op jit(solution)/shard_map/ppermute | solution.py:278
  30.2 1.0 %collective-permute-done.1.refs_2_ = bf16[1,64,14336]{2,1,0:T(8,128)(2,1)} collective-permute-done((bf16[1,64,14336]{2,1,0:T(8,128)(2,1)S(1)}, bf16[1,64,14336]{2,1,0:T(8,128)(2,1)}, u32[]{:S(2)}, u32[]{:S(2)}) %collective-permute-start.1) | collective-permute-done | bytes 1835040 | tf_op jit(solution)/shard_map/ppermute | solution.py:274
  31.2 2.0 %collective-permute-start.3 = (f32[136,128]{1,0:T(8,128)S(1)}, f32[136,128]{1,0:T(8,128)S(1)}, u32[]{:S(2)}, u32[]{:S(2)}) collective-permute-start(f32[136,128]{1,0:T(8,128)S(1)} %own_tile_and_sums.1), channel_id=1, source_target_pairs={{0,2},{2,0},{1,3},{3,1},{4,6},{6,4},{5,7},{7,5},{8,10},{10,8},{9,1... | collective-permute-start | bytes 208904 | tf_op jit(solution)/shard_map/ppermute | solution.py:291
  33.2 0.7 %slice.47 = bf16[1,8,128]{2,1,0:T(8,128)(2,1)S(1)} slice(bf16[1,64,14336]{2,1,0:T(8,128)(2,1)} %collective-permute-done.refs_0_), slice={[0:1], [0:8], [0:128]} | slice | bytes 4096 | tf_op jit(solution)/shard_map/slice | solution.py:300
  34.5 0.9 %copy-done.3 = s32[1,32768]{1,0:T(1,128)S(1)} copy-done((s32[1,32768]{1,0:T(1,128)S(1)}, s32[1,32768]{1,0:T(1,128)}, u32[]{:S(2)}) %copy-start.3) | copy-done | bytes 131096
  35.5 6.7 %chunk_tiles.4.refs_2_ = f32[528,128]{1,0:T(8,128)S(1)} custom-call(bf16[1,64,14336]{2,1,0:T(8,128)(2,1)S(1)} %slice.33.refs_0_.own_ref, s32[1,32768]{1,0:T(1,128)S(1)} %copy-done.3, bf16[1,64,14336]{2,1,0:T(8,128)(2,1)} %collective-permute-done.refs_0_, bf16[1,64,14336]{2,1,0:T(8,128)(2,1)} %collective-permute-done.2.refs_1_, ...), custom_call_target="tpu_custom_call" | custom-call | flops 7516192768 | bytes 7340032 | tf_op jit(solution)/shard_map/chunk_tiles/pallas_call | solution.py:175
  42.1 1.3 %collective-permute-start.4 = (bf16[1,64,2048]{2,1,0:T(8,128)(2,1)S(1)}, bf16[1,64,2048]{2,1,0:T(8,128)(2,1)S(1)}, u32[]{:S(2)}, u32[]{:S(2)}) collective-permute-start(bf16[1,64,2048]{2,1,0:T(8,128)(2,1)S(1)} %slice.36.refs_3_.own_ref), channel_id=1, source_target_pairs={{1,9},{5,13},{8,0},{9,17},{12,4},{13,21},{16,8},{17,25},{20,12},{2... | collective-permute-start | bytes 786440 | tf_op jit(solution)/shard_map/ppermute | solution.py:274
  43.5 1.8 %collective-permute-done.8.refs_0_ = bf16[1,64,10240]{2,1,0:T(8,128)(2,1)} collective-permute-done((bf16[1,64,10240]{2,1,0:T(8,128)(2,1)S(1)}, bf16[1,64,10240]{2,1,0:T(8,128)(2,1)}, u32[]{:S(2)}, u32[]{:S(2)}) %collective-permute-start.8) | collective-permute-done | bytes 1310752 | tf_op jit(solution)/shard_map/ppermute | solution.py:274
  45.3 1.3 %collective-permute-start.5 = (bf16[1,64,2048]{2,1,0:T(8,128)(2,1)S(1)}, bf16[1,64,2048]{2,1,0:T(8,128)(2,1)S(1)}, u32[]{:S(2)}, u32[]{:S(2)}) collective-permute-start(bf16[1,64,2048]{2,1,0:T(8,128)(2,1)S(1)} %slice.36.refs_3_.own_ref), channel_id=1, source_target_pairs={{1,5},{4,0},{9,13},{12,8},{17,21},{20,16},{25,29},{28,24},{3,7},{6... | collective-permute-start | bytes 786440 | tf_op jit(solution)/shard_map/ppermute | solution.py:278
  46.6 4.7 %chunk_tiles.5.refs_2_ = f32[528,128]{1,0:T(8,128)S(1)} custom-call(bf16[1,64,10240]{2,1,0:T(8,128)(2,1)S(1)} %slice.34.refs_1_.own_ref, s32[1,32768]{1,0:T(1,128)S(1)} %copy-done.3, bf16[1,64,10240]{2,1,0:T(8,128)(2,1)} %collective-permute-done.8.refs_0_, bf16[1,64,10240]{2,1,0:T(8,128)(2,1)} %collective-permute-done.9.refs_1_, ...), custom_call_target="tpu_custom_call" | custom-call | flops 5368709120 | bytes 5242880 | tf_op jit(solution)/shard_map/chunk_tiles/pallas_call | solution.py:175
  51.3 2.3 %collective-permute-done.6.refs_0_ = bf16[1,64,6144]{2,1,0:T(8,128)(2,1)S(1)} collective-permute-done((bf16[1,64,6144]{2,1,0:T(8,128)(2,1)}, bf16[1,64,6144]{2,1,0:T(8,128)(2,1)S(1)}, u32[]{:S(2)}, u32[]{:S(2)}) %collective-permute-start.6) | collective-permute-done | bytes 786464 | tf_op jit(solution)/shard_map/ppermute | solution.py:274
  53.6 1.9 %chunk_tiles.6.refs_2_ = f32[528,128]{1,0:T(8,128)S(1)} custom-call(bf16[1,64,6144]{2,1,0:T(8,128)(2,1)S(1)} %copy-done.1, s32[1,32768]{1,0:T(1,128)S(1)} %copy-done.3, bf16[1,64,6144]{2,1,0:T(8,128)(2,1)S(1)} %collective-permute-done.6.refs_0_, bf16[1,64,6144]{2,1,0:T(8,128)(2,1)S(1)} %collective-permute-done.7.refs_1_, f32[528,128]{1,0:T(8,128)S(1)} %chunk_tiles.5.refs_2_, ...), custom_call_target="tpu_custom_call" | custom-call | flops 3221225472 | bytes 3145728 | tf_op jit(solution)/shard_map/chunk_tiles/pallas_call | solution.py:175
  55.5 0.9 %collective-permute-done.4.refs_0_ = bf16[1,64,2048]{2,1,0:T(8,128)(2,1)S(1)} collective-permute-done((bf16[1,64,2048]{2,1,0:T(8,128)(2,1)S(1)}, bf16[1,64,2048]{2,1,0:T(8,128)(2,1)S(1)}, u32[]{:S(2)}, u32[]{:S(2)}) %collective-permute-start.4) | collective-permute-done | bytes 262176 | tf_op jit(solution)/shard_map/ppermute | solution.py:274
  56.4 1.0 %chunk_tiles.7 = (f32[136,128]{1,0:T(8,128)S(1)}, f32[136,128]{1,0:T(8,128)S(1)}, f32[72,128]{1,0:T(8,128)S(1)}, f32[72,128]{1,0:T(8,128)S(1)}) custom-call(bf16[1,64,2048]{2,1,0:T(8,128)(2,1)S(1)} %slice.36.refs_3_.own_ref, s32[1,32768]{1,0:T(1,128)S(1)} %copy-done.3, bf16[1,64,2048]{2,1,0:T(8,128)(2,1)S(1)} %collective-permute-done.4.refs_0_, ...), custom_call_target="tpu_custom_call" | custom-call | flops 1073741824 | bytes 1048576 | tf_op jit(solution)/shard_map/chunk_tiles/pallas_call | solution.py:175
  57.4 2.0 %collective-permute-start.10 = (f32[136,128]{1,0:T(8,128)S(1)}, f32[136,128]{1,0:T(8,128)S(1)}, u32[]{:S(2)}, u32[]{:S(2)}) collective-permute-start(f32[136,128]{1,0:T(8,128)S(1)} %get-tuple-element.12), channel_id=1, source_target_pairs={{0,2},{2,0},{1,3},{3,1},{4,6},{6,4},{5,7},{7,5},{8,10},{10,8},{9,1... | collective-permute-start | bytes 208904 | tf_op jit(solution)/shard_map/ppermute | solution.py:313
  59.4 1.6 %collective-permute-start.13 = (f32[72,128]{1,0:T(8,128)S(1)}, f32[72,128]{1,0:T(8,128)S(1)}, u32[]{:S(2)}, u32[]{:S(2)}) collective-permute-start(f32[72,128]{1,0:T(8,128)S(1)} %get-tuple-element.14), channel_id=1, source_target_pairs={{0,6},{2,4},{4,2},{6,0},{8,14},{10,12},{12,10},{14,8},{16,22},{18,... | collective-permute-start | bytes 110600 | tf_op jit(solution)/shard_map/ppermute | solution.py:311
  61.1 0.8 %collective-permute-done.10 = f32[136,128]{1,0:T(8,128)S(1)} collective-permute-done((f32[136,128]{1,0:T(8,128)S(1)}, f32[136,128]{1,0:T(8,128)S(1)}, u32[]{:S(2)}, u32[]{:S(2)}) %collective-permute-start.10) | collective-permute-done | bytes 69664 | tf_op jit(solution)/shard_map/ppermute | solution.py:313
  62.6 0.7 %collective-permute-done.12.same_ref = f32[72,128]{1,0:T(8,128)S(1)} collective-permute-done((f32[72,128]{1,0:T(8,128)S(1)}, f32[72,128]{1,0:T(8,128)S(1)}, u32[]{:S(2)}, u32[]{:S(2)}) %collective-permute-start.12) | collective-permute-done | bytes 36896 | tf_op jit(solution)/shard_map/ppermute | solution.py:311
  63.3 0.9 %collective-permute-done.13.other_ref = f32[72,128]{1,0:T(8,128)S(1)} collective-permute-done((f32[72,128]{1,0:T(8,128)S(1)}, f32[72,128]{1,0:T(8,128)S(1)}, u32[]{:S(2)}, u32[]{:S(2)}) %collective-permute-start.13) | collective-permute-done | bytes 36896 | tf_op jit(solution)/shard_map/ppermute | solution.py:311
  64.2 1.2 %normalise_and_skew.1 = f32[1,4,64,64]{3,2,1,0:T(8,128)} custom-call(f32[128,128]{1,0:T(8,128)S(1)} %pad_maximum_fusion.factor_ref, f32[136,128]{1,0:T(8,128)S(1)} %add.38.refs_3_.own_ref, f32[136,128]{1,0:T(8,128)S(1)} %add.40.kept_ref, f32[136,128]{1,0:T(8,128)S(1)} %collective-permute-done.11.here_ref, f32[72,128]{1,0:T(8,128)S(1)} %collective-permute-done.12.same_ref, ...), custom_call_target="tpu_custom_call" | custom-call | tf_op jit(solution)/shard_map/normalise_and_skew/pallas_call | solution.py:231
  (25 shorter events, 1.6 us)
Async XLA Ops:
  1.6 11.0 %copy-start.2 = (s32[1,32768]{1,0:T(1,128)S(1)}, s32[1,32768]{1,0:T(1,128)}, u32[]{:S(2)}) copy-start(s32[1,32768]{1,0:T(1,128)} %label_ref.9) | copy-start | bytes 393220
  1.6 15.9 %collective-permute-start = (bf16[1,64,14336]{2,1,0:T(8,128)(2,1)S(1)}, bf16[1,64,14336]{2,1,0:T(8,128)(2,1)}, u32[]{:S(2)}, u32[]{:S(2)}) collective-permute-start(bf16[1,64,14336]{2,1,0:T(8,128)(2,1)S(1)} %slice.33.refs_0_.own_ref), channel_id=1, source_target_pairs={{1,9},{9,17},{12,4},{17,25},{20,12},{28,20},{3,11},{11,19},{14,6},... | collective-permute-start | bytes 5505032 | tf_op jit(solution)/shard_map/ppermute | solution.py:274
  3.7 25.2 %collective-permute-start.2 = (bf16[1,64,14336]{2,1,0:T(8,128)(2,1)S(1)}, bf16[1,64,14336]{2,1,0:T(8,128)(2,1)}, u32[]{:S(2)}, u32[]{:S(2)}) collective-permute-start(bf16[1,64,14336]{2,1,0:T(8,128)(2,1)S(1)} %slice.33.refs_0_.own_ref), channel_id=1, source_target_pairs={{1,5},{4,0},{9,13},{12,8},{17,21},{20,16},{25,29},{28,24},{3,7},{6... | collective-permute-start | bytes 5505032 | tf_op jit(solution)/shard_map/ppermute | solution.py:280
  5.0 26.2 %collective-permute-start.1 = (bf16[1,64,14336]{2,1,0:T(8,128)(2,1)S(1)}, bf16[1,64,14336]{2,1,0:T(8,128)(2,1)}, u32[]{:S(2)}, u32[]{:S(2)}) collective-permute-start(bf16[1,64,14336]{2,1,0:T(8,128)(2,1)S(1)} %slice.33.refs_0_.own_ref), channel_id=1, source_target_pairs={{5,13},{8,0},{13,21},{16,8},{21,29},{24,16},{7,15},{10,2},{15,23},... | collective-permute-start | bytes 5505032 | tf_op jit(solution)/shard_map/ppermute | solution.py:274
  7.7 37.6 %collective-permute-start.8 = (bf16[1,64,10240]{2,1,0:T(8,128)(2,1)S(1)}, bf16[1,64,10240]{2,1,0:T(8,128)(2,1)}, u32[]{:S(2)}, u32[]{:S(2)}) collective-permute-start(bf16[1,64,10240]{2,1,0:T(8,128)(2,1)S(1)} %slice.34.refs_1_.own_ref), channel_id=1, source_target_pairs={{1,9},{5,13},{8,0},{9,17},{12,4},{13,21},{16,8},{17,25},{20,12},{2... | collective-permute-start | bytes 3932168 | tf_op jit(solution)/shard_map/ppermute | solution.py:274
  9.0 37.6 %collective-permute-start.9 = (bf16[1,64,10240]{2,1,0:T(8,128)(2,1)S(1)}, bf16[1,64,10240]{2,1,0:T(8,128)(2,1)}, u32[]{:S(2)}, u32[]{:S(2)}) collective-permute-start(bf16[1,64,10240]{2,1,0:T(8,128)(2,1)S(1)} %slice.34.refs_1_.own_ref), channel_id=1, source_target_pairs={{1,5},{4,0},{9,13},{12,8},{17,21},{20,16},{25,29},{28,24},{3,7},{6... | collective-permute-start | bytes 3932168 | tf_op jit(solution)/shard_map/ppermute | solution.py:278
  11.5 6.0 %copy-start = (bf16[1,64,6144]{2,1,0:T(8,128)(2,1)}, bf16[1,64,6144]{2,1,0:T(8,128)(2,1)S(1)}, u32[]{:S(2)}) copy-start(bf16[1,64,6144]{2,1,0:T(8,128)(2,1)S(1)} %slice.35.refs_2_.own_ref) | copy-start | bytes 2359300
  17.5 36.1 %collective-permute-start.6 = (bf16[1,64,6144]{2,1,0:T(8,128)(2,1)}, bf16[1,64,6144]{2,1,0:T(8,128)(2,1)S(1)}, u32[]{:S(2)}, u32[]{:S(2)}) collective-permute-start(bf16[1,64,6144]{2,1,0:T(8,128)(2,1)} %copy-done), channel_id=1, source_target_pairs={{1,9},{5,13},{8,0},{9,17},{12,4},{13,21},{16,8},{17,25},{20,12},{2... | collective-permute-start | bytes 2359304 | tf_op jit(solution)/shard_map/ppermute | solution.py:274
  28.9 24.7 %collective-permute-start.7 = (bf16[1,64,6144]{2,1,0:T(8,128)(2,1)}, bf16[1,64,6144]{2,1,0:T(8,128)(2,1)S(1)}, u32[]{:S(2)}, u32[]{:S(2)}) collective-permute-start(bf16[1,64,6144]{2,1,0:T(8,128)(2,1)} %copy-done), channel_id=1, source_target_pairs={{1,5},{4,0},{9,13},{12,8},{17,21},{20,16},{25,29},{28,24},{3,7},{6... | collective-permute-start | bytes 2359304 | tf_op jit(solution)/shard_map/ppermute | solution.py:278
  31.2 10.9 %collective-permute-start.3 = (f32[136,128]{1,0:T(8,128)S(1)}, f32[136,128]{1,0:T(8,128)S(1)}, u32[]{:S(2)}, u32[]{:S(2)}) collective-permute-start(f32[136,128]{1,0:T(8,128)S(1)} %own_tile_and_sums.1), channel_id=1, source_target_pairs={{0,2},{2,0},{1,3},{3,1},{4,6},{6,4},{5,7},{7,5},{8,10},{10,8},{9,1... | collective-permute-start | bytes 208904 | tf_op jit(solution)/shard_map/ppermute | solution.py:291
  34.5 0.9 %copy-start.3 = (s32[1,32768]{1,0:T(1,128)S(1)}, s32[1,32768]{1,0:T(1,128)}, u32[]{:S(2)}) copy-start(s32[1,32768]{1,0:T(1,128)} %label_ref.9) | copy-start | bytes 393220
  42.1 14.2 %collective-permute-start.4 = (bf16[1,64,2048]{2,1,0:T(8,128)(2,1)S(1)}, bf16[1,64,2048]{2,1,0:T(8,128)(2,1)S(1)}, u32[]{:S(2)}, u32[]{:S(2)}) collective-permute-start(bf16[1,64,2048]{2,1,0:T(8,128)(2,1)S(1)} %slice.36.refs_3_.own_ref), channel_id=1, source_target_pairs={{1,9},{5,13},{8,0},{9,17},{12,4},{13,21},{16,8},{17,25},{20,12},{2... | collective-permute-start | bytes 786440 | tf_op jit(solution)/shard_map/ppermute | solution.py:274
  43.5 10.1 %copy-start.1 = (bf16[1,64,6144]{2,1,0:T(8,128)(2,1)S(1)}, bf16[1,64,6144]{2,1,0:T(8,128)(2,1)}, u32[]{:S(2)}) copy-start(bf16[1,64,6144]{2,1,0:T(8,128)(2,1)} %copy-done) | copy-start | bytes 2359300
  45.3 11.1 %collective-permute-start.5 = (bf16[1,64,2048]{2,1,0:T(8,128)(2,1)S(1)}, bf16[1,64,2048]{2,1,0:T(8,128)(2,1)S(1)}, u32[]{:S(2)}, u32[]{:S(2)}) collective-permute-start(bf16[1,64,2048]{2,1,0:T(8,128)(2,1)S(1)} %slice.36.refs_3_.own_ref), channel_id=1, source_target_pairs={{1,5},{4,0},{9,13},{12,8},{17,21},{20,16},{25,29},{28,24},{3,7},{6... | collective-permute-start | bytes 786440 | tf_op jit(solution)/shard_map/ppermute | solution.py:278
  55.5 5.5 %copy-start.4 = (s32[1,4]{1,0:T(1,128)S(1)}, s32[1,4]{1,0:T(1,128)}, u32[]{:S(2)}) copy-start(s32[1,4]{1,0:T(1,128)} %param.5) | copy-start | bytes 52
  57.4 4.5 %collective-permute-start.10 = (f32[136,128]{1,0:T(8,128)S(1)}, f32[136,128]{1,0:T(8,128)S(1)}, u32[]{:S(2)}, u32[]{:S(2)}) collective-permute-start(f32[136,128]{1,0:T(8,128)S(1)} %get-tuple-element.12), channel_id=1, source_target_pairs={{0,2},{2,0},{1,3},{3,1},{4,6},{6,4},{5,7},{7,5},{8,10},{10,8},{9,1... | collective-permute-start | bytes 208904 | tf_op jit(solution)/shard_map/ppermute | solution.py:313
  59.4 4.0 %collective-permute-start.12 = (f32[72,128]{1,0:T(8,128)S(1)}, f32[72,128]{1,0:T(8,128)S(1)}, u32[]{:S(2)}, u32[]{:S(2)}) collective-permute-start(f32[72,128]{1,0:T(8,128)S(1)} %get-tuple-element.13), channel_id=1, source_target_pairs={{0,4},{2,6},{4,0},{6,2},{8,12},{10,14},{12,8},{14,10},{16,20},{18,... | collective-permute-start | bytes 110600 | tf_op jit(solution)/shard_map/ppermute | solution.py:311
  59.4 4.9 %collective-permute-start.13 = (f32[72,128]{1,0:T(8,128)S(1)}, f32[72,128]{1,0:T(8,128)S(1)}, u32[]{:S(2)}, u32[]{:S(2)}) collective-permute-start(f32[72,128]{1,0:T(8,128)S(1)} %get-tuple-element.14), channel_id=1, source_target_pairs={{0,6},{2,4},{4,2},{6,0},{8,14},{10,12},{12,10},{14,8},{16,22},{18,... | collective-permute-start | bytes 110600 | tf_op jit(solution)/shard_map/ppermute | solution.py:311
  61.9 2.4 %collective-permute-start.11 = (f32[136,128]{1,0:T(8,128)S(1)}, f32[136,128]{1,0:T(8,128)S(1)}, u32[]{:S(2)}, u32[]{:S(2)}) collective-permute-start(f32[136,128]{1,0:T(8,128)S(1)} %add.40.kept_ref), channel_id=1, source_target_pairs={{9,1},{13,5},{17,9},{21,13},{25,17},{29,21},{11,3},{15,7},{19,11},... | collective-permute-start | bytes 208904 | tf_op jit(solution)/shard_map/ppermute | solution.py:316

commit v5 on v4

--- a/solution.py
+++ b/solution.py
@@ -12,7 +12,7 @@
 RADII = 4
 ROWS = 64
 UNITS = 16
-SIZES = (7, 5, 3, 1)
+SIZES = (4, 8, 3, 1)
 STRIP = 2048
 NT = (((1,), (1,)), ((), ()))
 
@@ -46,8 +46,41 @@
     return [(begin, min(begin + STRIP, size)) for begin in range(0, size, STRIP)]
 
 
+def later_kernel(starts, frames_ref, *refs):
+    count = len(starts)
+    piece_refs, stage_refs, (in_semaphore, out_semaphore) = refs[:count], refs[count : 2 * count], refs[2 * count :]
+    reads, writes = [], []
+    for index, (start, piece_ref, stage_ref) in enumerate(zip(starts, piece_refs, stage_refs)):
+        source = frames_ref.at[:, :, start : start + piece_ref.shape[2]]
+        reads.append(pltpu.make_async_copy(source, stage_ref, in_semaphore.at[index]))
+        writes.append(pltpu.make_async_copy(stage_ref, piece_ref, out_semaphore.at[index]))
+    for read in reads:
+        read.start()
+    for read, write in zip(reads, writes):
+        read.wait()
+        write.start()
+    for write in writes:
+        write.wait()
+
+
+def later_pieces(frames, starts):
+    unit = frames.shape[2] // UNITS
+    shapes = [(1, ROWS, count * unit) for count in SIZES[1:]]
+    semaphores = pltpu.SemaphoreType.DMA((len(shapes),))
+    return pl.pallas_call(
+        functools.partial(later_kernel, starts),
+        in_specs=[pl.BlockSpec(memory_space=pl.ANY)],
+        out_specs=[pl.BlockSpec(memory_space=pl.ANY)] * len(shapes),
+        out_shape=[jax.ShapeDtypeStruct(shape, frames.dtype) for shape in shapes],
+        scratch_shapes=[pltpu.VMEM(shape, frames.dtype) for shape in shapes] + [semaphores] * 2,
+        compiler_params=pltpu.CompilerParams(vmem_limit_bytes=60 << 20),
+        name="later_pieces",
+    )(frames)
+
+
 def own_kernel(label_ref, *refs):
-    *piece_refs, out_ref = refs
+    *piece_refs, out_ref, copy_ref = refs
+    copy_ref[...] = piece_refs[2][...]
     half = RADII * ROWS
     total, offset = None, 0
     for piece_ref in piece_refs:
@@ -76,8 +109,11 @@
     return pl.pallas_call(
         own_kernel,
         in_specs=[vmem] * (1 + len(pieces)),
-        out_specs=vmem,
-        out_shape=jax.ShapeDtypeStruct((2 * ROWS + 8, 2 * ROWS), jnp.float32),
+        out_specs=[vmem] * 2,
+        out_shape=[
+            jax.ShapeDtypeStruct((2 * ROWS + 8, 2 * ROWS), jnp.float32),
+            jax.ShapeDtypeStruct(pieces[2].shape, pieces[2].dtype),
+        ],
         compiler_params=pltpu.CompilerParams(vmem_limit_bytes=8 << 20),
         cost_estimate=cost(label.shape[1], 512, 256),
         name="own_tile_and_sums",
@@ -179,7 +215,7 @@
         out_shape=[jax.ShapeDtypeStruct(shape, jnp.float32) for shape in shapes],
         scratch_shapes=[pltpu.VMEM(acc_shape, jnp.float32)] if last else [],
         compiler_params=pltpu.CompilerParams(vmem_limit_bytes=8 << 20),
-        cost_estimate=cost(size, 1024, 256),
+        cost_estimate=cost(size if before is not None else 20 * size, 1024, 256),
         name="chunk_tiles",
     )(*operands)
 
@@ -282,15 +318,14 @@
 
     unit = pixels // UNITS
     starts = [sum(SIZES[:index]) * unit for index in range(len(SIZES))]
-    pieces = [
-        lax.slice_in_dim(frames, start, start + count * unit, axis=2) for start, count in zip(starts, SIZES)
-    ]
-    own = own_part(annulus_label, pieces)
+    pieces = [lax.slice_in_dim(frames, 0, SIZES[0] * unit, axis=2), *later_pieces(frames, starts[1:])]
+    own, third = own_part(annulus_label, pieces)
     received = [sent(piece, index == 0) for index, piece in enumerate(pieces)]
     own, _ = lax.optimization_barrier((own, received[0]))
     own = own + lax.ppermute(own, "pix", [(0, 1), (1, 0)])
     factor = factors(own[2 * ROWS : 2 * ROWS + RADII, :ROWS], lag_width)
 
+    pieces[2] = third
     states = []
     for index, (piece, (far, near)) in enumerate(zip(pieces, received)):
         last = index == len(SIZES) - 1

time: 65.9 us -> 64.6 us (0.980)
  Pallas kernels: 20.2 us -> 24.1 us
  local copies, waits for them, and re-layouts: 6.99 us -> 3.86 us
  waiting for transfers between devices: 18.5 us -> 17.1 us
  other arithmetic: 0.89 us -> 0.23 us
    ppermute x1, waiting for transfers between devices: 10.1 us -> 0.01 us  [sent(): near = lax.ppermute(piece, tm_pb, list(near_pairs()))]
    ppermute x5, waiting for transfers between devices: 6.01 us -> 14.5 us  [far(): return lax.ppermute(piece, tm_pb, list(far_pairs(parities)))]
    slice x4 -> x1, local copies, waits for them, and re-layouts: 5.37 us -> 1.29 us  [shards(): lax.slice_in_dim(frames, 0, SIZES[0] * unit, axis=2)]
    pallas_call x0 -> x1, Pallas kernels: none -> 3.38 us  [later_pieces(): pl.pallas_call(functools.partial(later_kernel, starts), in_specs=[pl.Bloc...]
    unnamed x10 -> x12, local copies, waits for them, and re-layouts: 0.92 us -> 2.55 us
    ppermute x5, starting transfers between devices: 7.22 us -> 6.03 us  [far(): return lax.ppermute(piece, tm_pb, list(far_pairs(parities)))]
    pallas_call x1, Pallas kernels: 4.81 us -> 5.98 us  [own_part(): pl.pallas_call(own_kernel, in_specs=[vmem] * (1 + len(pieces)), out_specs...]
    ppermute x1, starting transfers between devices: 1.99 us -> 3 us  [shards(): own = own + lax.ppermute(own, 'pix', [(0, 1), (1, 0)])]
  transfers between devices with their start and end apart: 14 -> 14, of which waited for: 8 -> 6; matrix products, arithmetic and copies ran while one was open for 8% -> 0% of each run, Pallas kernels for 28% -> 34%
where the time goes in v5:
time: 64.6 us; the launch traced here: 64.1 us
  Pallas kernels  24.1 us (37%)
  starting transfers between devices  18.5 us (29%)
  waiting for transfers between devices  17.1 us (26%)
  local copies, waits for them, and re-layouts  3.86 us (6%)
    ppermute x5, waiting for transfers between devices, far(): return lax.ppermute(piece, tm_pb, list(far_pairs(parities)))  14.5 us
    pallas_call x4, Pallas kernels, chunk_part(): pl.pallas_call(functools.partial(chunk_kernel, start, before is None, las...  13.5 us
    ppermute x5, starting transfers between devices, far(): return lax.ppermute(piece, tm_pb, list(far_pairs(parities)))  6.03 us
    pallas_call x1, Pallas kernels, own_part(): pl.pallas_call(own_kernel, in_specs=[vmem] * (1 + len(pieces)), out_specs...  5.98 us
    ppermute x3, starting transfers between devices, sent(): return ([alone], lax.ppermute(piece, tm_pb, list(near_pairs())))  3.86 us
    pallas_call x1, Pallas kernels, later_pieces(): pl.pallas_call(functools.partial(later_kernel, starts), in_specs=[pl.Bloc...  3.38 us
    ppermute x1, starting transfers between devices, shards(): own = own + lax.ppermute(own, 'pix', [(0, 1), (1, 0)])  3 us
    unnamed x12, local copies, waits for them, and re-layouts  2.55 us
  transfers between devices with their start and end apart: 14, of which 6 were waited for; matrix products, arithmetic and copies ran while one was open for 0% of the time, Pallas kernels for 34%

profile of v5, /device:TPU:0, one launch (start us, length us, event | category | flops | bytes accessed | tf_op | source)
XLA Modules:
  0.0 64.1 jit_solution(3309554879363829369)
XLA Ops:
  0.0 1.3 %slice.24.refs_0_.own_ref = bf16[1,64,8192]{2,1,0:T(8,128)(2,1)S(1)} slice(bf16[1,64,32768]{2,1,0:T(8,128)(2,1)} %frames_ref.1), slice={[0:1], [0:64], [0:8192]} | slice | bytes 2097152 | tf_op jit(solution)/shard_map/slice | solution.py:321
  1.3 0.9 %collective-permute-start = (bf16[1,64,8192]{2,1,0:T(8,128)(2,1)S(1)}, bf16[1,64,8192]{2,1,0:T(8,128)(2,1)S(1)}, u32[]{:S(2)}, u32[]{:S(2)}) collective-permute-start(bf16[1,64,8192]{2,1,0:T(8,128)(2,1)S(1)} %slice.24.refs_0_.own_ref), channel_id=1, source_target_pairs={{1,9},{9,17},{12,4},{17,25},{20,12},{28,20},{3,11},{11,19},{14,6},... | collective-permute-start | bytes 3145736 | tf_op jit(solution)/shard_map/ppermute | solution.py:310
  2.2 1.3 %collective-permute-start.2 = (bf16[1,64,8192]{2,1,0:T(8,128)(2,1)S(1)}, bf16[1,64,8192]{2,1,0:T(8,128)(2,1)S(1)}, u32[]{:S(2)}, u32[]{:S(2)}) collective-permute-start(bf16[1,64,8192]{2,1,0:T(8,128)(2,1)S(1)} %slice.24.refs_0_.own_ref), channel_id=1, source_target_pairs={{1,5},{4,0},{9,13},{12,8},{17,21},{20,16},{25,29},{28,24},{3,7},{6... | collective-permute-start | bytes 3145736 | tf_op jit(solution)/shard_map/ppermute | solution.py:316
  3.5 1.3 %collective-permute-start.1 = (bf16[1,64,8192]{2,1,0:T(8,128)(2,1)S(1)}, bf16[1,64,8192]{2,1,0:T(8,128)(2,1)}, u32[]{:S(2)}, u32[]{:S(2)}) collective-permute-start(bf16[1,64,8192]{2,1,0:T(8,128)(2,1)S(1)} %slice.24.refs_0_.own_ref), channel_id=1, source_target_pairs={{5,13},{8,0},{13,21},{16,8},{21,29},{24,16},{7,15},{10,2},{15,23},... | collective-permute-start | bytes 3145736 | tf_op jit(solution)/shard_map/ppermute | solution.py:310
  4.8 3.4 %later_pieces.1 = (bf16[1,64,16384]{2,1,0:T(8,128)(2,1)}, bf16[1,64,6144]{2,1,0:T(8,128)(2,1)}, bf16[1,64,2048]{2,1,0:T(8,128)(2,1)}) custom-call(bf16[1,64,32768]{2,1,0:T(8,128)(2,1)} %frames_ref.1), custom_call_target="tpu_custom_call" | custom-call | tf_op jit(solution)/shard_map/later_pieces/pallas_call | solution.py:70
  8.2 1.3 %collective-permute-start.8 = (bf16[1,64,16384]{2,1,0:T(8,128)(2,1)}, bf16[1,64,16384]{2,1,0:T(8,128)(2,1)}, u32[]{:S(2)}, u32[]{:S(2)}) collective-permute-start(bf16[1,64,16384]{2,1,0:T(8,128)(2,1)} %get-tuple-element.15.refs_1_.own_ref), channel_id=1, source_target_pairs={{1,9},{5,13},{8,0},{9,17},{12,4},{13,21},{16,8},{17,25},{20,12},{2... | collective-permute-start | bytes 6291464 | tf_op jit(solution)/shard_map/ppermute | solution.py:310
  9.5 1.3 %collective-permute-start.9 = (bf16[1,64,16384]{2,1,0:T(8,128)(2,1)}, bf16[1,64,16384]{2,1,0:T(8,128)(2,1)}, u32[]{:S(2)}, u32[]{:S(2)}) collective-permute-start(bf16[1,64,16384]{2,1,0:T(8,128)(2,1)} %get-tuple-element.15.refs_1_.own_ref), channel_id=1, source_target_pairs={{1,5},{4,0},{9,13},{12,8},{17,21},{20,16},{25,29},{28,24},{3,7},{6... | collective-permute-start | bytes 6291464 | tf_op jit(solution)/shard_map/ppermute | solution.py:314
  10.8 1.6 %copy-done = bf16[1,64,16384]{2,1,0:T(8,128)(2,1)S(1)} copy-done((bf16[1,64,16384]{2,1,0:T(8,128)(2,1)S(1)}, bf16[1,64,16384]{2,1,0:T(8,128)(2,1)}, u32[]{:S(2)}) %copy-start) | copy-done | bytes 2097176
  12.4 0.9 %copy-done.2 = bf16[1,64,2048]{2,1,0:T(8,128)(2,1)S(1)} copy-done((bf16[1,64,2048]{2,1,0:T(8,128)(2,1)S(1)}, bf16[1,64,2048]{2,1,0:T(8,128)(2,1)}, u32[]{:S(2)}) %copy-start.2) | copy-done | bytes 262168
  13.3 6.0 %own_tile_and_sums.1 = (f32[136,128]{1,0:T(8,128)S(1)}, bf16[1,64,6144]{2,1,0:T(8,128)(2,1)S(1)}) custom-call(s32[1,32768]{1,0:T(1,128)S(1)} %copy-done.4, bf16[1,64,8192]{2,1,0:T(8,128)(2,1)S(1)} %slice.24.refs_0_.own_ref, bf16[1,64,16384]{2,1,0:T(8,128)(2,1)S(1)} %copy-done, bf16[1,64,6144]{2,1,0:T(8,128)(2,1)} %get-tuple-element.16.refs_2_, ...), custom_call_target="tpu_custom_call" | custom-call | flops 8589934592 | bytes 16777216 | tf_op jit(solution)/shard_map/own_tile_and_sums/pallas_call | solution.py:109
  19.3 1.3 %collective-permute-start.6 = (bf16[1,64,6144]{2,1,0:T(8,128)(2,1)}, bf16[1,64,6144]{2,1,0:T(8,128)(2,1)S(1)}, u32[]{:S(2)}, u32[]{:S(2)}) collective-permute-start(bf16[1,64,6144]{2,1,0:T(8,128)(2,1)} %get-tuple-element.16.refs_2_), channel_id=1, source_target_pairs={{1,9},{5,13},{8,0},{9,17},{12,4},{13,21},{16,8},{17,25},{20,12},{2... | collective-permute-start | bytes 2359304 | tf_op jit(solution)/shard_map/ppermute | solution.py:310
  20.6 1.3 %collective-permute-start.7 = (bf16[1,64,6144]{2,1,0:T(8,128)(2,1)}, bf16[1,64,6144]{2,1,0:T(8,128)(2,1)S(1)}, u32[]{:S(2)}, u32[]{:S(2)}) collective-permute-start(bf16[1,64,6144]{2,1,0:T(8,128)(2,1)} %get-tuple-element.16.refs_2_), channel_id=1, source_target_pairs={{1,5},{4,0},{9,13},{12,8},{17,21},{20,16},{25,29},{28,24},{3,7},{6... | collective-permute-start | bytes 2359304 | tf_op jit(solution)/shard_map/ppermute | solution.py:314
  21.9 3.0 %collective-permute-start.3 = (f32[136,128]{1,0:T(8,128)S(1)}, f32[136,128]{1,0:T(8,128)S(1)}, u32[]{:S(2)}, u32[]{:S(2)}) collective-permute-start(f32[136,128]{1,0:T(8,128)S(1)} %get-tuple-element.19), channel_id=1, source_target_pairs={{0,2},{2,0},{1,3},{3,1},{4,6},{6,4},{5,7},{7,5},{8,10},{10,8},{9,1... | collective-permute-start | bytes 208904 | tf_op jit(solution)/shard_map/ppermute | solution.py:325
  25.0 3.8 %chunk_tiles.4.refs_2_ = f32[528,128]{1,0:T(8,128)S(1)} custom-call(bf16[1,64,8192]{2,1,0:T(8,128)(2,1)S(1)} %slice.24.refs_0_.own_ref, s32[1,32768]{1,0:T(1,128)S(1)} %copy-done.4, bf16[1,64,8192]{2,1,0:T(8,128)(2,1)S(1)} %collective-permute-done.refs_0_, bf16[1,64,8192]{2,1,0:T(8,128)(2,1)S(1)} %collective-permute-done.2.refs_1_, ...), custom_call_target="tpu_custom_call" | custom-call | flops 85899345920 | bytes 83886080 | tf_op jit(solution)/shard_map/chunk_tiles/pallas_call | solution.py:211
  28.8 1.3 %collective-permute-start.4 = (bf16[1,64,2048]{2,1,0:T(8,128)(2,1)S(1)}, bf16[1,64,2048]{2,1,0:T(8,128)(2,1)S(1)}, u32[]{:S(2)}, u32[]{:S(2)}) collective-permute-start(bf16[1,64,2048]{2,1,0:T(8,128)(2,1)S(1)} %copy-done.3), channel_id=1, source_target_pairs={{1,9},{5,13},{8,0},{9,17},{12,4},{13,21},{16,8},{17,25},{20,12},{2... | collective-permute-start | bytes 786440 | tf_op jit(solution)/shard_map/ppermute | solution.py:310
  30.1 0.1 fusion.5
  30.3 13.5 %collective-permute-done.8.refs_0_ = bf16[1,64,16384]{2,1,0:T(8,128)(2,1)} collective-permute-done((bf16[1,64,16384]{2,1,0:T(8,128)(2,1)}, bf16[1,64,16384]{2,1,0:T(8,128)(2,1)}, u32[]{:S(2)}, u32[]{:S(2)}) %collective-permute-start.8) | collective-permute-done | bytes 2097184 | tf_op jit(solution)/shard_map/ppermute | solution.py:310
  43.8 1.3 %collective-permute-start.5 = (bf16[1,64,2048]{2,1,0:T(8,128)(2,1)S(1)}, bf16[1,64,2048]{2,1,0:T(8,128)(2,1)S(1)}, u32[]{:S(2)}, u32[]{:S(2)}) collective-permute-start(bf16[1,64,2048]{2,1,0:T(8,128)(2,1)S(1)} %copy-done.3), channel_id=1, source_target_pairs={{1,5},{4,0},{9,13},{12,8},{17,21},{20,16},{25,29},{28,24},{3,7},{6... | collective-permute-start | bytes 786440 | tf_op jit(solution)/shard_map/ppermute | solution.py:314
  45.1 6.9 %chunk_tiles.5.refs_2_ = f32[528,128]{1,0:T(8,128)S(1)} custom-call(bf16[1,64,16384]{2,1,0:T(8,128)(2,1)S(1)} %copy-done.1, s32[1,32768]{1,0:T(1,128)S(1)} %copy-done.4, bf16[1,64,16384]{2,1,0:T(8,128)(2,1)} %collective-permute-done.8.refs_0_, bf16[1,64,16384]{2,1,0:T(8,128)(2,1)} %collective-permute-done.9.refs_1_, f32[528,128]{1,0:T(8,128)S(1)} %chunk_tiles.4.refs_2_, ...), custom_call_target="tpu_custom_call" | custom-call | flops 8589934592 | bytes 8388608 | tf_op jit(solution)/shard_map/chunk_tiles/pallas_call | solution.py:211
  52.0 0.1 collective-permute-done.6.refs_0_
  52.1 1.9 %chunk_tiles.6.refs_2_ = f32[528,128]{1,0:T(8,128)S(1)} custom-call(bf16[1,64,6144]{2,1,0:T(8,128)(2,1)S(1)} %get-tuple-element.20.own_ref, s32[1,32768]{1,0:T(1,128)S(1)} %copy-done.4, bf16[1,64,6144]{2,1,0:T(8,128)(2,1)S(1)} %collective-permute-done.6.refs_0_, bf16[1,64,6144]{2,1,0:T(8,128)(2,1)S(1)} %collective-permute-done.7.refs_1_, ...), custom_call_target="tpu_custom_call" | custom-call | flops 3221225472 | bytes 3145728 | tf_op jit(solution)/shard_map/chunk_tiles/pallas_call | solution.py:211
  54.0 0.9 %collective-permute-done.4.refs_0_ = bf16[1,64,2048]{2,1,0:T(8,128)(2,1)S(1)} collective-permute-done((bf16[1,64,2048]{2,1,0:T(8,128)(2,1)S(1)}, bf16[1,64,2048]{2,1,0:T(8,128)(2,1)S(1)}, u32[]{:S(2)}, u32[]{:S(2)}) %collective-permute-start.4) | collective-permute-done | bytes 262176 | tf_op jit(solution)/shard_map/ppermute | solution.py:310
  54.9 1.0 %chunk_tiles.7 = (f32[136,128]{1,0:T(8,128)S(1)}, f32[136,128]{1,0:T(8,128)S(1)}, f32[72,128]{1,0:T(8,128)S(1)}, f32[72,128]{1,0:T(8,128)S(1)}) custom-call(bf16[1,64,2048]{2,1,0:T(8,128)(2,1)S(1)} %copy-done.3, s32[1,32768]{1,0:T(1,128)S(1)} %copy-done.4, bf16[1,64,2048]{2,1,0:T(8,128)(2,1)S(1)} %collective-permute-done.4.refs_0_, ...), custom_call_target="tpu_custom_call" | custom-call | flops 1073741824 | bytes 1048576 | tf_op jit(solution)/shard_map/chunk_tiles/pallas_call | solution.py:211
  55.9 2.0 %collective-permute-start.10 = (f32[136,128]{1,0:T(8,128)S(1)}, f32[136,128]{1,0:T(8,128)S(1)}, u32[]{:S(2)}, u32[]{:S(2)}) collective-permute-start(f32[136,128]{1,0:T(8,128)S(1)} %get-tuple-element.22), channel_id=1, source_target_pairs={{0,2},{2,0},{1,3},{3,1},{4,6},{6,4},{5,7},{7,5},{8,10},{10,8},{9,1... | collective-permute-start | bytes 208904 | tf_op jit(solution)/shard_map/ppermute | solution.py:348
  57.9 0.1 collective-permute-start.12
  58.0 1.5 %collective-permute-start.13 = (f32[72,128]{1,0:T(8,128)S(1)}, f32[72,128]{1,0:T(8,128)S(1)}, u32[]{:S(2)}, u32[]{:S(2)}) collective-permute-start(f32[72,128]{1,0:T(8,128)S(1)} %get-tuple-element.24), channel_id=1, source_target_pairs={{0,6},{2,4},{4,2},{6,0},{8,14},{10,12},{12,10},{14,8},{16,22},{18,... | collective-permute-start | bytes 110600 | tf_op jit(solution)/shard_map/ppermute | solution.py:346
  59.5 1.0 %collective-permute-done.10 = f32[136,128]{1,0:T(8,128)S(1)} collective-permute-done((f32[136,128]{1,0:T(8,128)S(1)}, f32[136,128]{1,0:T(8,128)S(1)}, u32[]{:S(2)}, u32[]{:S(2)}) %collective-permute-start.10) | collective-permute-done | bytes 69664 | tf_op jit(solution)/shard_map/ppermute | solution.py:348
  60.5 0.7 %collective-permute-start.11 = (f32[136,128]{1,0:T(8,128)S(1)}, f32[136,128]{1,0:T(8,128)S(1)}, u32[]{:S(2)}, u32[]{:S(2)}) collective-permute-start(f32[136,128]{1,0:T(8,128)S(1)} %add.40.kept_ref), channel_id=1, source_target_pairs={{9,1},{13,5},{17,9},{21,13},{25,17},{29,21},{11,3},{15,7},{19,11},... | collective-permute-start | bytes 208904 | tf_op jit(solution)/shard_map/ppermute | solution.py:351
  61.2 0.1 pad_maximum_fusion.factor_ref
  61.3 0.7 %collective-permute-done.12.same_ref = f32[72,128]{1,0:T(8,128)S(1)} collective-permute-done((f32[72,128]{1,0:T(8,128)S(1)}, f32[72,128]{1,0:T(8,128)S(1)}, u32[]{:S(2)}, u32[]{:S(2)}) %collective-permute-start.12) | collective-permute-done | bytes 36896 | tf_op jit(solution)/shard_map/ppermute | solution.py:346
  61.9 0.9 %collective-permute-done.13.other_ref = f32[72,128]{1,0:T(8,128)S(1)} collective-permute-done((f32[72,128]{1,0:T(8,128)S(1)}, f32[72,128]{1,0:T(8,128)S(1)}, u32[]{:S(2)}, u32[]{:S(2)}) %collective-permute-start.13) | collective-permute-done | bytes 36896 | tf_op jit(solution)/shard_map/ppermute | solution.py:346
  62.9 1.2 %normalise_and_skew.1 = f32[1,4,64,64]{3,2,1,0:T(8,128)} custom-call(f32[128,128]{1,0:T(8,128)S(1)} %pad_maximum_fusion.factor_ref, f32[136,128]{1,0:T(8,128)S(1)} %add.38.refs_3_.own_ref, f32[136,128]{1,0:T(8,128)S(1)} %add.40.kept_ref, f32[136,128]{1,0:T(8,128)S(1)} %collective-permute-done.11.here_ref, f32[72,128]{1,0:T(8,128)S(1)} %collective-permute-done.12.same_ref, ...), custom_call_target="tpu_custom_call" | custom-call | tf_op jit(solution)/shard_map/normalise_and_skew/pallas_call | solution.py:267
  (25 shorter events, 0.1 us)
Async XLA Ops:
  1.3 9.5 %copy-start.4 = (s32[1,32768]{1,0:T(1,128)S(1)}, s32[1,32768]{1,0:T(1,128)}, u32[]{:S(2)}) copy-start(s32[1,32768]{1,0:T(1,128)} %label_ref.9) | copy-start | bytes 393220
  1.3 18.0 %collective-permute-start = (bf16[1,64,8192]{2,1,0:T(8,128)(2,1)S(1)}, bf16[1,64,8192]{2,1,0:T(8,128)(2,1)S(1)}, u32[]{:S(2)}, u32[]{:S(2)}) collective-permute-start(bf16[1,64,8192]{2,1,0:T(8,128)(2,1)S(1)} %slice.24.refs_0_.own_ref), channel_id=1, source_target_pairs={{1,9},{9,17},{12,4},{17,25},{20,12},{28,20},{3,11},{11,19},{14,6},... | collective-permute-start | bytes 3145736 | tf_op jit(solution)/shard_map/ppermute | solution.py:310
  2.2 18.5 %collective-permute-start.2 = (bf16[1,64,8192]{2,1,0:T(8,128)(2,1)S(1)}, bf16[1,64,8192]{2,1,0:T(8,128)(2,1)S(1)}, u32[]{:S(2)}, u32[]{:S(2)}) collective-permute-start(bf16[1,64,8192]{2,1,0:T(8,128)(2,1)S(1)} %slice.24.refs_0_.own_ref), channel_id=1, source_target_pairs={{1,5},{4,0},{9,13},{12,8},{17,21},{20,16},{25,29},{28,24},{3,7},{6... | collective-permute-start | bytes 3145736 | tf_op jit(solution)/shard_map/ppermute | solution.py:316
  3.5 18.5 %collective-permute-start.1 = (bf16[1,64,8192]{2,1,0:T(8,128)(2,1)S(1)}, bf16[1,64,8192]{2,1,0:T(8,128)(2,1)}, u32[]{:S(2)}, u32[]{:S(2)}) collective-permute-start(bf16[1,64,8192]{2,1,0:T(8,128)(2,1)S(1)} %slice.24.refs_0_.own_ref), channel_id=1, source_target_pairs={{5,13},{8,0},{13,21},{16,8},{21,29},{24,16},{7,15},{10,2},{15,23},... | collective-permute-start | bytes 3145736 | tf_op jit(solution)/shard_map/ppermute | solution.py:310
  8.2 35.6 %collective-permute-start.8 = (bf16[1,64,16384]{2,1,0:T(8,128)(2,1)}, bf16[1,64,16384]{2,1,0:T(8,128)(2,1)}, u32[]{:S(2)}, u32[]{:S(2)}) collective-permute-start(bf16[1,64,16384]{2,1,0:T(8,128)(2,1)} %get-tuple-element.15.refs_1_.own_ref), channel_id=1, source_target_pairs={{1,9},{5,13},{8,0},{9,17},{12,4},{13,21},{16,8},{17,25},{20,12},{2... | collective-permute-start | bytes 6291464 | tf_op jit(solution)/shard_map/ppermute | solution.py:310
  9.5 35.6 %collective-permute-start.9 = (bf16[1,64,16384]{2,1,0:T(8,128)(2,1)}, bf16[1,64,16384]{2,1,0:T(8,128)(2,1)}, u32[]{:S(2)}, u32[]{:S(2)}) collective-permute-start(bf16[1,64,16384]{2,1,0:T(8,128)(2,1)} %get-tuple-element.15.refs_1_.own_ref), channel_id=1, source_target_pairs={{1,5},{4,0},{9,13},{12,8},{17,21},{20,16},{25,29},{28,24},{3,7},{6... | collective-permute-start | bytes 6291464 | tf_op jit(solution)/shard_map/ppermute | solution.py:314
  10.8 1.6 %copy-start = (bf16[1,64,16384]{2,1,0:T(8,128)(2,1)S(1)}, bf16[1,64,16384]{2,1,0:T(8,128)(2,1)}, u32[]{:S(2)}) copy-start(bf16[1,64,16384]{2,1,0:T(8,128)(2,1)} %get-tuple-element.15.refs_1_.own_ref) | copy-start | bytes 6291460
  12.4 0.9 %copy-start.2 = (bf16[1,64,2048]{2,1,0:T(8,128)(2,1)S(1)}, bf16[1,64,2048]{2,1,0:T(8,128)(2,1)}, u32[]{:S(2)}) copy-start(bf16[1,64,2048]{2,1,0:T(8,128)(2,1)} %get-tuple-element.17.refs_3_.own_ref) | copy-start | bytes 786436
  19.3 32.7 %collective-permute-start.6 = (bf16[1,64,6144]{2,1,0:T(8,128)(2,1)}, bf16[1,64,6144]{2,1,0:T(8,128)(2,1)S(1)}, u32[]{:S(2)}, u32[]{:S(2)}) collective-permute-start(bf16[1,64,6144]{2,1,0:T(8,128)(2,1)} %get-tuple-element.16.refs_2_), channel_id=1, source_target_pairs={{1,9},{5,13},{8,0},{9,17},{12,4},{13,21},{16,8},{17,25},{20,12},{2... | collective-permute-start | bytes 2359304 | tf_op jit(solution)/shard_map/ppermute | solution.py:310
  20.6 31.4 %collective-permute-start.7 = (bf16[1,64,6144]{2,1,0:T(8,128)(2,1)}, bf16[1,64,6144]{2,1,0:T(8,128)(2,1)S(1)}, u32[]{:S(2)}, u32[]{:S(2)}) collective-permute-start(bf16[1,64,6144]{2,1,0:T(8,128)(2,1)} %get-tuple-element.16.refs_2_), channel_id=1, source_target_pairs={{1,5},{4,0},{9,13},{12,8},{17,21},{20,16},{25,29},{28,24},{3,7},{6... | collective-permute-start | bytes 2359304 | tf_op jit(solution)/shard_map/ppermute | solution.py:314
  21.9 6.8 %collective-permute-start.3 = (f32[136,128]{1,0:T(8,128)S(1)}, f32[136,128]{1,0:T(8,128)S(1)}, u32[]{:S(2)}, u32[]{:S(2)}) collective-permute-start(f32[136,128]{1,0:T(8,128)S(1)} %get-tuple-element.19), channel_id=1, source_target_pairs={{0,2},{2,0},{1,3},{3,1},{4,6},{6,4},{5,7},{7,5},{8,10},{10,8},{9,1... | collective-permute-start | bytes 208904 | tf_op jit(solution)/shard_map/ppermute | solution.py:325
  25.0 3.8 %copy-start.3 = (bf16[1,64,2048]{2,1,0:T(8,128)(2,1)S(1)}, bf16[1,64,2048]{2,1,0:T(8,128)(2,1)}, u32[]{:S(2)}) copy-start(bf16[1,64,2048]{2,1,0:T(8,128)(2,1)} %get-tuple-element.17.refs_3_.own_ref) | copy-start | bytes 786436
  25.0 5.2 %copy-start.5 = (s32[1,4]{1,0:T(1,128)S(1)}, s32[1,4]{1,0:T(1,128)}, u32[]{:S(2)}) copy-start(s32[1,4]{1,0:T(1,128)} %param.5) | copy-start | bytes 52
  25.0 20.1 %copy-start.1 = (bf16[1,64,16384]{2,1,0:T(8,128)(2,1)S(1)}, bf16[1,64,16384]{2,1,0:T(8,128)(2,1)}, u32[]{:S(2)}) copy-start(bf16[1,64,16384]{2,1,0:T(8,128)(2,1)} %get-tuple-element.15.refs_1_.own_ref) | copy-start | bytes 6291460
  28.8 26.1 %collective-permute-start.4 = (bf16[1,64,2048]{2,1,0:T(8,128)(2,1)S(1)}, bf16[1,64,2048]{2,1,0:T(8,128)(2,1)S(1)}, u32[]{:S(2)}, u32[]{:S(2)}) collective-permute-start(bf16[1,64,2048]{2,1,0:T(8,128)(2,1)S(1)} %copy-done.3), channel_id=1, source_target_pairs={{1,9},{5,13},{8,0},{9,17},{12,4},{13,21},{16,8},{17,25},{20,12},{2... | collective-permute-start | bytes 786440 | tf_op jit(solution)/shard_map/ppermute | solution.py:310
  43.8 11.1 %collective-permute-start.5 = (bf16[1,64,2048]{2,1,0:T(8,128)(2,1)S(1)}, bf16[1,64,2048]{2,1,0:T(8,128)(2,1)S(1)}, u32[]{:S(2)}, u32[]{:S(2)}) collective-permute-start(bf16[1,64,2048]{2,1,0:T(8,128)(2,1)S(1)} %copy-done.3), channel_id=1, source_target_pairs={{1,5},{4,0},{9,13},{12,8},{17,21},{20,16},{25,29},{28,24},{3,7},{6... | collective-permute-start | bytes 786440 | tf_op jit(solution)/shard_map/ppermute | solution.py:314
  55.9 4.6 %collective-permute-start.10 = (f32[136,128]{1,0:T(8,128)S(1)}, f32[136,128]{1,0:T(8,128)S(1)}, u32[]{:S(2)}, u32[]{:S(2)}) collective-permute-start(f32[136,128]{1,0:T(8,128)S(1)} %get-tuple-element.22), channel_id=1, source_target_pairs={{0,2},{2,0},{1,3},{3,1},{4,6},{6,4},{5,7},{7,5},{8,10},{10,8},{9,1... | collective-permute-start | bytes 208904 | tf_op jit(solution)/shard_map/ppermute | solution.py:348
  57.9 4.1 %collective-permute-start.12 = (f32[72,128]{1,0:T(8,128)S(1)}, f32[72,128]{1,0:T(8,128)S(1)}, u32[]{:S(2)}, u32[]{:S(2)}) collective-permute-start(f32[72,128]{1,0:T(8,128)S(1)} %get-tuple-element.23), channel_id=1, source_target_pairs={{0,4},{2,6},{4,0},{6,2},{8,12},{10,14},{12,8},{14,10},{16,20},{18,... | collective-permute-start | bytes 110600 | tf_op jit(solution)/shard_map/ppermute | solution.py:346
  58.0 4.9 %collective-permute-start.13 = (f32[72,128]{1,0:T(8,128)S(1)}, f32[72,128]{1,0:T(8,128)S(1)}, u32[]{:S(2)}, u32[]{:S(2)}) collective-permute-start(f32[72,128]{1,0:T(8,128)S(1)} %get-tuple-element.24), channel_id=1, source_target_pairs={{0,6},{2,4},{4,2},{6,0},{8,14},{10,12},{12,10},{14,8},{16,22},{18,... | collective-permute-start | bytes 110600 | tf_op jit(solution)/shard_map/ppermute | solution.py:346
  60.5 2.4 %collective-permute-start.11 = (f32[136,128]{1,0:T(8,128)S(1)}, f32[136,128]{1,0:T(8,128)S(1)}, u32[]{:S(2)}, u32[]{:S(2)}) collective-permute-start(f32[136,128]{1,0:T(8,128)S(1)} %add.40.kept_ref), channel_id=1, source_target_pairs={{9,1},{13,5},{17,9},{21,13},{25,17},{29,21},{11,3},{15,7},{19,11},... | collective-permute-start | bytes 208904 | tf_op jit(solution)/shard_map/ppermute | solution.py:351

commit v6 on v5

--- a/solution.py
+++ b/solution.py
@@ -120,22 +120,13 @@
     )(label, *pieces)
 
 
-def chunk_kernel(start, first, last, own_ref, label_ref, *refs):
-    if first:
-        far_alone_ref, near_ref, far_ref, *refs = refs
-    else:
-        far_ref, near_ref, *refs = refs
-        far_alone_ref = far_ref
-    if first:
-        before_ref = None
-    else:
+def chunk_kernel(start, first, last, own_ref, label_ref, far_ref, near_ref, *refs):
+    if not first:
         before_ref, *refs = refs
-    if not last:
-        _, *refs = refs
     if last:
         *out_refs, acc = refs
     else:
-        (acc,) = refs
+        _, acc = refs
     half = RADII * ROWS
     band, second, has_near = place()
     later = band == 1
@@ -143,15 +134,16 @@
 
     def add(with_near):
         total = None
-        sources = (own_ref, near_ref, far_ref if with_near else far_alone_ref)
         for begin, end in pieces:
-            own, near, far = (ref[0, :, begin:end] for ref in sources)
+            own, near, far = (ref[0, :, begin:end] for ref in (own_ref, near_ref, far_ref))
             earliest = jnp.where(later, far, own)
             latest = jnp.where(later, own, far)
             label = label_ref[:, start + begin : start + end]
             rows = [annulus_rows(label)] + masked_by_annulus(earliest, label)
             if with_near:
                 rows += masked_by_annulus(near, label)
+            else:
+                near = jnp.zeros_like(near)
             part = products(rows, jnp.concatenate([near, latest], axis=0))
             total = part if total is None else total + part
         count = total.shape[0]
@@ -204,7 +196,7 @@
     acc_shape = (16 + 2 * RADII * ROWS, 2 * ROWS)
     here, after = (2 * ROWS + 8, 2 * ROWS), (ROWS + 8, 2 * ROWS)
     vmem = pl.BlockSpec(memory_space=pltpu.VMEM)
-    operands = [piece, label, far[0], near, *far[1:]] + ([] if before is None else [before])
+    operands = [piece, label, far, near] + ([] if before is None else [before])
     if not last:
         operands.append(awaited)
     shapes = [here, here, after, after] if last else [acc_shape]
@@ -223,7 +215,8 @@
 def final_kernel(factor_ref, own_ref, kept_ref, here_ref, same_ref, other_ref, out_ref):
     band, second, _ = place()
     first = jnp.logical_not(second)
-    here = jnp.where(band == 0, kept_ref[...], here_ref[...])
+    inside = lax.axis_index("tm") < lax.axis_size("tm") - 2
+    here = jnp.where(band == 0, kept_ref[...], jnp.where(inside, here_ref[...], 0.0))
     after = same_ref[...] + other_ref[...]
     own = own_ref[...]
     row = lax.broadcasted_iota(jnp.int32, (ROWS, 2 * ROWS), 0)
@@ -291,36 +284,28 @@
     pixels = frames.shape[2]
     pb, pix = lax.axis_index("pb"), lax.axis_index("pix")
 
-    def far_pairs(parities):
+    def far_pairs():
         for i in range(devices):
             for band, target in ((0, i - 2), (1, i + 2)):
-                if 0 <= target < devices and (i % 2 == band) in parities:
-                    yield 2 * i + band, 2 * target + band
+                inside = 0 <= target < devices
+                yield 2 * i + band, 2 * (target if inside else i) + (band if inside else 1 - band)
 
     def near_pairs():
         for i in range(devices):
-            band, target = (0, i - 1) if i % 2 else (1, i + 1)
-            if target < devices:
-                yield 2 * i + band, 2 * target + band
+            yield 2 * i + (1 - i % 2), 2 * (i ^ 1) + (1 - i % 2)
+            yield 2 * i + i % 2, 2 * i + (1 - i % 2)
 
     tm_pb = ("tm", "pb")
 
-    def sent(piece, first):
-        def far(*parities):
-            return lax.ppermute(piece, tm_pb, list(far_pairs(parities)))
-
-        if not first:
-            alone = far(False, True)
-            return [alone], lax.ppermute(piece, tm_pb, list(near_pairs()))
-        alone = far(False)
+    def sent(piece):
         near = lax.ppermute(piece, tm_pb, list(near_pairs()))
-        return [alone, far(True)], near
+        return lax.ppermute(piece, tm_pb, list(far_pairs())), near
 
     unit = pixels // UNITS
     starts = [sum(SIZES[:index]) * unit for index in range(len(SIZES))]
     pieces = [lax.slice_in_dim(frames, 0, SIZES[0] * unit, axis=2), *later_pieces(frames, starts[1:])]
     own, third = own_part(annulus_label, pieces)
-    received = [sent(piece, index == 0) for index, piece in enumerate(pieces)]
+    received = [sent(piece) for piece in pieces]
     own, _ = lax.optimization_barrier((own, received[0]))
     own = own + lax.ppermute(own, "pix", [(0, 1), (1, 0)])
     factor = factors(own[2 * ROWS : 2 * ROWS + RADII, :ROWS], lag_width)
@@ -332,8 +317,7 @@
         before = states[-1] if states else None
         awaited = own
         if index == 0:
-            corner = lax.optimization_barrier(far[0][:, :8, :128])
-            awaited = corner + near[:, :8, :128]
+            awaited = far[:, :8, :128]
         result = chunk_part(piece, annulus_label, starts[index], far, near, before, awaited, last)
         states.append(result if last else result[0])
     state = states[-1]
@@ -348,7 +332,7 @@
     beside = lax.ppermute(here_other, "pix", [(0, 1), (1, 0)])
     after = [swapped(after_same, 0), swapped(after_other, 1)]
     here = here_same + beside
-    handed = lax.ppermute(here, tm_pb, [(2 * i + 1, 2 * i - 3) for i in range(2, devices)])
+    handed = lax.ppermute(here, tm_pb, [(source ^ 1, target ^ 1) for source, target in far_pairs()])
     return final_part(factor, own, here, [handed, *after])
 
 

time: 64.6 us -> 62.1 us (0.961)
  starting transfers between devices: 18.5 us -> 13.6 us
  waiting for transfers between devices: 17.1 us -> 20.1 us
    ppermute x9 -> x5, starting transfers between devices: 10.6 us -> 3.76 us  [the longest x1 2.03 us: shards(): lax.ppermute(here, tm_pb, [(source ^ 1, target ^ 1) for source, target in...]
    ppermute x1 -> x4, starting transfers between devices: 1.29 us -> 4.74 us  [sent(): near = lax.ppermute(piece, tm_pb, list(near_pairs()))]
    ppermute x9 -> x5, waiting for transfers between devices: 14.5 us -> 17.7 us  [the longest x4 17.1 us: sent(): return (lax.ppermute(piece, tm_pb, list(far_pairs())), near)]
    ppermute x1, starting transfers between devices: 3 us -> 1.49 us  [shards(): own = own + lax.ppermute(own, 'pix', [(0, 1), (1, 0)])]
  transfers between devices with their start and end apart: 14 -> 13, of which waited for: 6 -> 6; matrix products, arithmetic and copies ran while one was open for 0% -> 0% of each run, Pallas kernels for 34% -> 35%
where the time goes in v6:
time: 62.1 us; the launch traced here: 61.7 us
  Pallas kernels  23.8 us (38%)
  waiting for transfers between devices  20.1 us (32%)
  starting transfers between devices  13.6 us (22%)
  local copies, waits for them, and re-layouts  3.85 us (6%)
    ppermute x4, waiting for transfers between devices, sent(): return (lax.ppermute(piece, tm_pb, list(far_pairs())), near)  17.1 us
    pallas_call x4, Pallas kernels, chunk_part(): pl.pallas_call(functools.partial(chunk_kernel, start, before is None, las...  13.3 us
    pallas_call x1, Pallas kernels, own_part(): pl.pallas_call(own_kernel, in_specs=[vmem] * (1 + len(pieces)), out_specs...  5.98 us
    ppermute x4, starting transfers between devices, sent(): near = lax.ppermute(piece, tm_pb, list(near_pairs()))  4.74 us
    pallas_call x1, Pallas kernels, later_pieces(): pl.pallas_call(functools.partial(later_kernel, starts), in_specs=[pl.Bloc...  3.29 us
    unnamed x12, local copies, waits for them, and re-layouts  2.55 us
    ppermute x1, starting transfers between devices, shards(): lax.ppermute(here, tm_pb, [(source ^ 1, target ^ 1) for source, target in...  2.03 us
    ppermute x1, starting transfers between devices, shards(): beside = lax.ppermute(here_other, 'pix', [(0, 1), (1, 0)])  2 us
  transfers between devices with their start and end apart: 13, of which 6 were waited for; matrix products, arithmetic and copies ran while one was open for 0% of the time, Pallas kernels for 35%

profile of v6, /device:TPU:0, one launch (start us, length us, event | category | flops | bytes accessed | tf_op | source)
XLA Modules:
  0.0 61.7 jit_solution(12565189396637329582)
XLA Ops:
  0.0 1.3 %slice.21.refs_0_.own_ref = bf16[1,64,8192]{2,1,0:T(8,128)(2,1)S(1)} slice(bf16[1,64,32768]{2,1,0:T(8,128)(2,1)} %frames_ref.1), slice={[0:1], [0:64], [0:8192]} | slice | bytes 2097152 | tf_op jit(solution)/shard_map/slice | solution.py:306
  1.3 0.0 copy-start.4
  1.3 0.5 collective-permute-start
  1.8 2.1 %collective-permute-start.1 = (bf16[1,64,8192]{2,1,0:T(8,128)(2,1)S(1)}, bf16[1,64,8192]{2,1,0:T(8,128)(2,1)S(1)}, u32[]{:S(2)}, u32[]{:S(2)}) collective-permute-start(bf16[1,64,8192]{2,1,0:T(8,128)(2,1)S(1)} %slice.21.refs_0_.own_ref), channel_id=1, source_target_pairs={{1,5},{0,1},{4,0},{5,4},{9,13},{8,9},{12,8},{13,12},{17,21},{16,17... | collective-permute-start | bytes 3145736 | tf_op jit(solution)/shard_map/ppermute | solution.py:301
  3.9 3.3 %later_pieces.1 = (bf16[1,64,16384]{2,1,0:T(8,128)(2,1)}, bf16[1,64,6144]{2,1,0:T(8,128)(2,1)}, bf16[1,64,2048]{2,1,0:T(8,128)(2,1)}) custom-call(bf16[1,64,32768]{2,1,0:T(8,128)(2,1)} %frames_ref.1), custom_call_target="tpu_custom_call" | custom-call | tf_op jit(solution)/shard_map/later_pieces/pallas_call | solution.py:70
  7.2 1.3 %collective-permute-start.7 = (bf16[1,64,16384]{2,1,0:T(8,128)(2,1)}, bf16[1,64,16384]{2,1,0:T(8,128)(2,1)}, u32[]{:S(2)}, u32[]{:S(2)}) collective-permute-start(bf16[1,64,16384]{2,1,0:T(8,128)(2,1)} %get-tuple-element.15.refs_1_.own_ref), channel_id=1, source_target_pairs={{0,1},{1,9},{4,5},{5,13},{8,0},{9,17},{12,4},{13,21},{16,8},{17,25... | collective-permute-start | bytes 6291464 | tf_op jit(solution)/shard_map/ppermute | solution.py:302
  8.5 1.3 %collective-permute-start.8 = (bf16[1,64,16384]{2,1,0:T(8,128)(2,1)}, bf16[1,64,16384]{2,1,0:T(8,128)(2,1)}, u32[]{:S(2)}, u32[]{:S(2)}) collective-permute-start(bf16[1,64,16384]{2,1,0:T(8,128)(2,1)} %get-tuple-element.15.refs_1_.own_ref), channel_id=1, source_target_pairs={{1,5},{0,1},{4,0},{5,4},{9,13},{8,9},{12,8},{13,12},{17,21},{16,17... | collective-permute-start | bytes 6291464 | tf_op jit(solution)/shard_map/ppermute | solution.py:301
  9.8 0.0 collective-permute-start.5
  9.8 1.6 %copy-done = bf16[1,64,16384]{2,1,0:T(8,128)(2,1)S(1)} copy-done((bf16[1,64,16384]{2,1,0:T(8,128)(2,1)S(1)}, bf16[1,64,16384]{2,1,0:T(8,128)(2,1)}, u32[]{:S(2)}) %copy-start) | copy-done | bytes 2097176
  11.4 0.9 %copy-done.2 = bf16[1,64,2048]{2,1,0:T(8,128)(2,1)S(1)} copy-done((bf16[1,64,2048]{2,1,0:T(8,128)(2,1)S(1)}, bf16[1,64,2048]{2,1,0:T(8,128)(2,1)}, u32[]{:S(2)}) %copy-start.2) | copy-done | bytes 262168
  12.3 6.0 %own_tile_and_sums.1 = (f32[136,128]{1,0:T(8,128)S(1)}, bf16[1,64,6144]{2,1,0:T(8,128)(2,1)S(1)}) custom-call(s32[1,32768]{1,0:T(1,128)S(1)} %copy-done.4, bf16[1,64,8192]{2,1,0:T(8,128)(2,1)S(1)} %slice.21.refs_0_.own_ref, bf16[1,64,16384]{2,1,0:T(8,128)(2,1)S(1)} %copy-done, bf16[1,64,6144]{2,1,0:T(8,128)(2,1)} %get-tuple-element.16.refs_2_, ...), custom_call_target="tpu_custom_call" | custom-call | flops 8589934592 | bytes 16777216 | tf_op jit(solution)/shard_map/own_tile_and_sums/pallas_call | solution.py:109
  18.3 0.0 collective-permute-done.far_ref
  18.3 1.3 %collective-permute-start.6 = (bf16[1,64,6144]{2,1,0:T(8,128)(2,1)}, bf16[1,64,6144]{2,1,0:T(8,128)(2,1)S(1)}, u32[]{:S(2)}, u32[]{:S(2)}) collective-permute-start(bf16[1,64,6144]{2,1,0:T(8,128)(2,1)} %get-tuple-element.16.refs_2_), channel_id=1, source_target_pairs={{1,5},{0,1},{4,0},{5,4},{9,13},{8,9},{12,8},{13,12},{17,21},{16,17... | collective-permute-start | bytes 2359304 | tf_op jit(solution)/shard_map/ppermute | solution.py:301
  19.6 0.0 collective-permute-done.1.near_ref
  19.6 1.5 %collective-permute-start.2 = (f32[136,128]{1,0:T(8,128)S(1)}, f32[136,128]{1,0:T(8,128)S(1)}, u32[]{:S(2)}, u32[]{:S(2)}) collective-permute-start(f32[136,128]{1,0:T(8,128)S(1)} %get-tuple-element.19), channel_id=1, source_target_pairs={{0,2},{2,0},{1,3},{3,1},{4,6},{6,4},{5,7},{7,5},{8,10},{10,8},{9,1... | collective-permute-start | bytes 208904 | tf_op jit(solution)/shard_map/ppermute | solution.py:310
  21.1 2.4 %chunk_tiles.4.refs_0_ = f32[528,128]{1,0:T(8,128)S(1)} custom-call(bf16[1,64,8192]{2,1,0:T(8,128)(2,1)S(1)} %slice.21.refs_0_.own_ref, s32[1,32768]{1,0:T(1,128)S(1)} %copy-done.4, bf16[1,64,8192]{2,1,0:T(8,128)(2,1)S(1)} %collective-permute-done.far_ref, bf16[1,64,8192]{2,1,0:T(8,128)(2,1)S(1)} %collective-permute-done.1.near_ref, ...), custom_call_target="tpu_custom_call" | custom-call | flops 85899345920 | bytes 83886080 | tf_op jit(solution)/shard_map/chunk_tiles/pallas_call | solution.py:203
  23.5 0.4 collective-permute-done.2
  24.0 0.1 fusion.5
  24.1 15.6 %collective-permute-done.7.far_ref = bf16[1,64,16384]{2,1,0:T(8,128)(2,1)} collective-permute-done((bf16[1,64,16384]{2,1,0:T(8,128)(2,1)}, bf16[1,64,16384]{2,1,0:T(8,128)(2,1)}, u32[]{:S(2)}, u32[]{:S(2)}) %collective-permute-start.7) | collective-permute-done | bytes 2097184 | tf_op jit(solution)/shard_map/ppermute | solution.py:302
  39.7 6.9 %chunk_tiles.5.refs_0_ = f32[528,128]{1,0:T(8,128)S(1)} custom-call(bf16[1,64,16384]{2,1,0:T(8,128)(2,1)S(1)} %copy-done.1, s32[1,32768]{1,0:T(1,128)S(1)} %copy-done.4, bf16[1,64,16384]{2,1,0:T(8,128)(2,1)} %collective-permute-done.7.far_ref, bf16[1,64,16384]{2,1,0:T(8,128)(2,1)} %collective-permute-done.8.near_ref, f32[528,128]{1,0:T(8,128)S(1)} %chunk_tiles.4.refs_0_, ...), custom_call_target="tpu_custom_call" | custom-call | flops 8589934592 | bytes 8388608 | tf_op jit(solution)/shard_map/chunk_tiles/pallas_call | solution.py:203
  46.6 1.5 %collective-permute-done.5.far_ref = bf16[1,64,6144]{2,1,0:T(8,128)(2,1)} collective-permute-done((bf16[1,64,6144]{2,1,0:T(8,128)(2,1)}, bf16[1,64,6144]{2,1,0:T(8,128)(2,1)}, u32[]{:S(2)}, u32[]{:S(2)}) %collective-permute-start.5) | collective-permute-done | bytes 786464 | tf_op jit(solution)/shard_map/ppermute | solution.py:302
  48.1 3.0 %chunk_tiles.6.refs_0_ = f32[528,128]{1,0:T(8,128)S(1)} custom-call(bf16[1,64,6144]{2,1,0:T(8,128)(2,1)S(1)} %get-tuple-element.20.own_ref, s32[1,32768]{1,0:T(1,128)S(1)} %copy-done.4, bf16[1,64,6144]{2,1,0:T(8,128)(2,1)} %collective-permute-done.5.far_ref, bf16[1,64,6144]{2,1,0:T(8,128)(2,1)S(1)} %collective-permute-done.6.near_ref, ...), custom_call_target="tpu_custom_call" | custom-call | flops 3221225472 | bytes 3145728 | tf_op jit(solution)/shard_map/chunk_tiles/pallas_call | solution.py:203
  51.2 1.0 %chunk_tiles.7 = (f32[136,128]{1,0:T(8,128)S(1)}, f32[136,128]{1,0:T(8,128)S(1)}, f32[72,128]{1,0:T(8,128)S(1)}, f32[72,128]{1,0:T(8,128)S(1)}) custom-call(bf16[1,64,2048]{2,1,0:T(8,128)(2,1)S(1)} %copy-done.3, s32[1,32768]{1,0:T(1,128)S(1)} %copy-done.4, bf16[1,64,2048]{2,1,0:T(8,128)(2,1)S(1)} %collective-permute-done.3.far_ref, ...), custom_call_target="tpu_custom_call" | custom-call | flops 1073741824 | bytes 1048576 | tf_op jit(solution)/shard_map/chunk_tiles/pallas_call | solution.py:203
  52.2 2.0 %collective-permute-start.9 = (f32[136,128]{1,0:T(8,128)S(1)}, f32[136,128]{1,0:T(8,128)S(1)}, u32[]{:S(2)}, u32[]{:S(2)}) collective-permute-start(f32[136,128]{1,0:T(8,128)S(1)} %get-tuple-element.22), channel_id=1, source_target_pairs={{0,2},{2,0},{1,3},{3,1},{4,6},{6,4},{5,7},{7,5},{8,10},{10,8},{9,1... | collective-permute-start | bytes 208904 | tf_op jit(solution)/shard_map/ppermute | solution.py:332
  54.2 1.0 %collective-permute-start.11 = (f32[72,128]{1,0:T(8,128)S(1)}, f32[72,128]{1,0:T(8,128)S(1)}, u32[]{:S(2)}, u32[]{:S(2)}) collective-permute-start(f32[72,128]{1,0:T(8,128)S(1)} %get-tuple-element.23), channel_id=1, source_target_pairs={{0,4},{2,6},{4,0},{6,2},{8,12},{10,14},{12,8},{14,10},{16,20},{18,... | collective-permute-start | bytes 110600 | tf_op jit(solution)/shard_map/ppermute | solution.py:330
  55.1 0.7 %collective-permute-start.12 = (f32[72,128]{1,0:T(8,128)S(1)}, f32[72,128]{1,0:T(8,128)S(1)}, u32[]{:S(2)}, u32[]{:S(2)}) collective-permute-start(f32[72,128]{1,0:T(8,128)S(1)} %get-tuple-element.24), channel_id=1, source_target_pairs={{0,6},{2,4},{4,2},{6,0},{8,14},{10,12},{12,10},{14,8},{16,22},{18,... | collective-permute-start | bytes 110600 | tf_op jit(solution)/shard_map/ppermute | solution.py:330
  55.8 0.7 %collective-permute-done.9 = f32[136,128]{1,0:T(8,128)S(1)} collective-permute-done((f32[136,128]{1,0:T(8,128)S(1)}, f32[136,128]{1,0:T(8,128)S(1)}, u32[]{:S(2)}, u32[]{:S(2)}) %collective-permute-start.9) | collective-permute-done | bytes 69664 | tf_op jit(solution)/shard_map/ppermute | solution.py:332
  56.6 2.0 %collective-permute-start.10 = (f32[136,128]{1,0:T(8,128)S(1)}, f32[136,128]{1,0:T(8,128)S(1)}, u32[]{:S(2)}, u32[]{:S(2)}) collective-permute-start(f32[136,128]{1,0:T(8,128)S(1)} %add.36.kept_ref), channel_id=1, source_target_pairs={{1,0},{0,8},{5,4},{4,12},{9,1},{8,16},{13,5},{12,20},{17,9},{16,24... | collective-permute-start | bytes 208904 | tf_op jit(solution)/shard_map/ppermute | solution.py:335
  58.6 0.1 pad_maximum_fusion.factor_ref
  58.7 1.3 %collective-permute-done.12.other_ref = f32[72,128]{1,0:T(8,128)S(1)} collective-permute-done((f32[72,128]{1,0:T(8,128)S(1)}, f32[72,128]{1,0:T(8,128)S(1)}, u32[]{:S(2)}, u32[]{:S(2)}) %collective-permute-start.12) | collective-permute-done | bytes 36896 | tf_op jit(solution)/shard_map/ppermute | solution.py:330
  60.0 0.5 collective-permute-done.10.here_ref
  60.5 1.2 %normalise_and_skew.1 = f32[1,4,64,64]{3,2,1,0:T(8,128)} custom-call(f32[128,128]{1,0:T(8,128)S(1)} %pad_maximum_fusion.factor_ref, f32[136,128]{1,0:T(8,128)S(1)} %add.35.refs_1_.own_ref, f32[136,128]{1,0:T(8,128)S(1)} %add.36.kept_ref, f32[136,128]{1,0:T(8,128)S(1)} %collective-permute-done.10.here_ref, f32[72,128]{1,0:T(8,128)S(1)} %collective-permute-done.11.same_ref, ...), custom_call_target="tpu_custom_call" | custom-call | tf_op jit(solution)/shard_map/normalise_and_skew/pallas_call | solution.py:260
  (22 shorter events, 0.1 us)
Async XLA Ops:
  1.3 8.5 %copy-start.4 = (s32[1,32768]{1,0:T(1,128)S(1)}, s32[1,32768]{1,0:T(1,128)}, u32[]{:S(2)}) copy-start(s32[1,32768]{1,0:T(1,128)} %label_ref.9) | copy-start | bytes 393220
  1.3 17.0 %collective-permute-start = (bf16[1,64,8192]{2,1,0:T(8,128)(2,1)S(1)}, bf16[1,64,8192]{2,1,0:T(8,128)(2,1)S(1)}, u32[]{:S(2)}, u32[]{:S(2)}) collective-permute-start(bf16[1,64,8192]{2,1,0:T(8,128)(2,1)S(1)} %slice.21.refs_0_.own_ref), channel_id=1, source_target_pairs={{0,1},{1,9},{4,5},{5,13},{8,0},{9,17},{12,4},{13,21},{16,8},{17,25... | collective-permute-start | bytes 3145736 | tf_op jit(solution)/shard_map/ppermute | solution.py:302
  1.8 17.8 %collective-permute-start.1 = (bf16[1,64,8192]{2,1,0:T(8,128)(2,1)S(1)}, bf16[1,64,8192]{2,1,0:T(8,128)(2,1)S(1)}, u32[]{:S(2)}, u32[]{:S(2)}) collective-permute-start(bf16[1,64,8192]{2,1,0:T(8,128)(2,1)S(1)} %slice.21.refs_0_.own_ref), channel_id=1, source_target_pairs={{1,5},{0,1},{4,0},{5,4},{9,13},{8,9},{12,8},{13,12},{17,21},{16,17... | collective-permute-start | bytes 3145736 | tf_op jit(solution)/shard_map/ppermute | solution.py:301
  7.2 32.5 %collective-permute-start.7 = (bf16[1,64,16384]{2,1,0:T(8,128)(2,1)}, bf16[1,64,16384]{2,1,0:T(8,128)(2,1)}, u32[]{:S(2)}, u32[]{:S(2)}) collective-permute-start(bf16[1,64,16384]{2,1,0:T(8,128)(2,1)} %get-tuple-element.15.refs_1_.own_ref), channel_id=1, source_target_pairs={{0,1},{1,9},{4,5},{5,13},{8,0},{9,17},{12,4},{13,21},{16,8},{17,25... | collective-permute-start | bytes 6291464 | tf_op jit(solution)/shard_map/ppermute | solution.py:302
  8.5 31.3 %collective-permute-start.8 = (bf16[1,64,16384]{2,1,0:T(8,128)(2,1)}, bf16[1,64,16384]{2,1,0:T(8,128)(2,1)}, u32[]{:S(2)}, u32[]{:S(2)}) collective-permute-start(bf16[1,64,16384]{2,1,0:T(8,128)(2,1)} %get-tuple-element.15.refs_1_.own_ref), channel_id=1, source_target_pairs={{1,5},{0,1},{4,0},{5,4},{9,13},{8,9},{12,8},{13,12},{17,21},{16,17... | collective-permute-start | bytes 6291464 | tf_op jit(solution)/shard_map/ppermute | solution.py:301
  9.8 38.4 %collective-permute-start.5 = (bf16[1,64,6144]{2,1,0:T(8,128)(2,1)}, bf16[1,64,6144]{2,1,0:T(8,128)(2,1)}, u32[]{:S(2)}, u32[]{:S(2)}) collective-permute-start(bf16[1,64,6144]{2,1,0:T(8,128)(2,1)} %get-tuple-element.16.refs_2_), channel_id=1, source_target_pairs={{0,1},{1,9},{4,5},{5,13},{8,0},{9,17},{12,4},{13,21},{16,8},{17,25... | collective-permute-start | bytes 2359304 | tf_op jit(solution)/shard_map/ppermute | solution.py:302
  9.8 1.6 %copy-start = (bf16[1,64,16384]{2,1,0:T(8,128)(2,1)S(1)}, bf16[1,64,16384]{2,1,0:T(8,128)(2,1)}, u32[]{:S(2)}) copy-start(bf16[1,64,16384]{2,1,0:T(8,128)(2,1)} %get-tuple-element.15.refs_1_.own_ref) | copy-start | bytes 6291460
  11.4 0.9 %copy-start.2 = (bf16[1,64,2048]{2,1,0:T(8,128)(2,1)S(1)}, bf16[1,64,2048]{2,1,0:T(8,128)(2,1)}, u32[]{:S(2)}) copy-start(bf16[1,64,2048]{2,1,0:T(8,128)(2,1)} %get-tuple-element.17.refs_3_.own_ref) | copy-start | bytes 786436
  18.3 29.8 %collective-permute-start.6 = (bf16[1,64,6144]{2,1,0:T(8,128)(2,1)}, bf16[1,64,6144]{2,1,0:T(8,128)(2,1)S(1)}, u32[]{:S(2)}, u32[]{:S(2)}) collective-permute-start(bf16[1,64,6144]{2,1,0:T(8,128)(2,1)} %get-tuple-element.16.refs_2_), channel_id=1, source_target_pairs={{1,5},{0,1},{4,0},{5,4},{9,13},{8,9},{12,8},{13,12},{17,21},{16,17... | collective-permute-start | bytes 2359304 | tf_op jit(solution)/shard_map/ppermute | solution.py:301
  19.6 4.3 %collective-permute-start.2 = (f32[136,128]{1,0:T(8,128)S(1)}, f32[136,128]{1,0:T(8,128)S(1)}, u32[]{:S(2)}, u32[]{:S(2)}) collective-permute-start(f32[136,128]{1,0:T(8,128)S(1)} %get-tuple-element.19), channel_id=1, source_target_pairs={{0,2},{2,0},{1,3},{3,1},{4,6},{6,4},{5,7},{7,5},{8,10},{10,8},{9,1... | collective-permute-start | bytes 208904 | tf_op jit(solution)/shard_map/ppermute | solution.py:310
  21.1 2.8 %copy-start.3 = (bf16[1,64,2048]{2,1,0:T(8,128)(2,1)S(1)}, bf16[1,64,2048]{2,1,0:T(8,128)(2,1)}, u32[]{:S(2)}) copy-start(bf16[1,64,2048]{2,1,0:T(8,128)(2,1)} %get-tuple-element.17.refs_3_.own_ref) | copy-start | bytes 786436
  21.1 2.8 %copy-start.5 = (s32[1,4]{1,0:T(1,128)S(1)}, s32[1,4]{1,0:T(1,128)}, u32[]{:S(2)}) copy-start(s32[1,4]{1,0:T(1,128)} %param.5) | copy-start | bytes 52
  21.1 18.6 %copy-start.1 = (bf16[1,64,16384]{2,1,0:T(8,128)(2,1)S(1)}, bf16[1,64,16384]{2,1,0:T(8,128)(2,1)}, u32[]{:S(2)}) copy-start(bf16[1,64,16384]{2,1,0:T(8,128)(2,1)} %get-tuple-element.15.refs_1_.own_ref) | copy-start | bytes 6291460
  23.9 27.2 %collective-permute-start.3 = (bf16[1,64,2048]{2,1,0:T(8,128)(2,1)S(1)}, bf16[1,64,2048]{2,1,0:T(8,128)(2,1)S(1)}, u32[]{:S(2)}, u32[]{:S(2)}) collective-permute-start(bf16[1,64,2048]{2,1,0:T(8,128)(2,1)S(1)} %copy-done.3), channel_id=1, source_target_pairs={{0,1},{1,9},{4,5},{5,13},{8,0},{9,17},{12,4},{13,21},{16,8},{17,25... | collective-permute-start | bytes 786440 | tf_op jit(solution)/shard_map/ppermute | solution.py:302
  39.7 11.5 %collective-permute-start.4 = (bf16[1,64,2048]{2,1,0:T(8,128)(2,1)S(1)}, bf16[1,64,2048]{2,1,0:T(8,128)(2,1)S(1)}, u32[]{:S(2)}, u32[]{:S(2)}) collective-permute-start(bf16[1,64,2048]{2,1,0:T(8,128)(2,1)S(1)} %copy-done.3), channel_id=1, source_target_pairs={{1,5},{0,1},{4,0},{5,4},{9,13},{8,9},{12,8},{13,12},{17,21},{16,17... | collective-permute-start | bytes 786440 | tf_op jit(solution)/shard_map/ppermute | solution.py:301
  52.2 4.4 %collective-permute-start.9 = (f32[136,128]{1,0:T(8,128)S(1)}, f32[136,128]{1,0:T(8,128)S(1)}, u32[]{:S(2)}, u32[]{:S(2)}) collective-permute-start(f32[136,128]{1,0:T(8,128)S(1)} %get-tuple-element.22), channel_id=1, source_target_pairs={{0,2},{2,0},{1,3},{3,1},{4,6},{6,4},{5,7},{7,5},{8,10},{10,8},{9,1... | collective-permute-start | bytes 208904 | tf_op jit(solution)/shard_map/ppermute | solution.py:332
  54.2 4.5 %collective-permute-start.11 = (f32[72,128]{1,0:T(8,128)S(1)}, f32[72,128]{1,0:T(8,128)S(1)}, u32[]{:S(2)}, u32[]{:S(2)}) collective-permute-start(f32[72,128]{1,0:T(8,128)S(1)} %get-tuple-element.23), channel_id=1, source_target_pairs={{0,4},{2,6},{4,0},{6,2},{8,12},{10,14},{12,8},{14,10},{16,20},{18,... | collective-permute-start | bytes 110600 | tf_op jit(solution)/shard_map/ppermute | solution.py:330
  55.1 4.9 %collective-permute-start.12 = (f32[72,128]{1,0:T(8,128)S(1)}, f32[72,128]{1,0:T(8,128)S(1)}, u32[]{:S(2)}, u32[]{:S(2)}) collective-permute-start(f32[72,128]{1,0:T(8,128)S(1)} %get-tuple-element.24), channel_id=1, source_target_pairs={{0,6},{2,4},{4,2},{6,0},{8,14},{10,12},{12,10},{14,8},{16,22},{18,... | collective-permute-start | bytes 110600 | tf_op jit(solution)/shard_map/ppermute | solution.py:330
  56.6 4.0 %collective-permute-start.10 = (f32[136,128]{1,0:T(8,128)S(1)}, f32[136,128]{1,0:T(8,128)S(1)}, u32[]{:S(2)}, u32[]{:S(2)}) collective-permute-start(f32[136,128]{1,0:T(8,128)S(1)} %add.36.kept_ref), channel_id=1, source_target_pairs={{1,0},{0,8},{5,4},{4,12},{9,1},{8,16},{13,5},{12,20},{17,9},{16,24... | collective-permute-start | bytes 208904 | tf_op jit(solution)/shard_map/ppermute | solution.py:335

commit v7 on v6

--- a/solution.py
+++ b/solution.py
@@ -12,7 +12,7 @@
 RADII = 4
 ROWS = 64
 UNITS = 16
-SIZES = (4, 8, 3, 1)
+SIZES = (3, 9, 3, 1)
 STRIP = 2048
 NT = (((1,), (1,)), ((), ()))
 

time: 62.1 us -> 61.7 us (level)
  Pallas kernels: 23.8 us -> 23 us
    pallas_call x4, Pallas kernels: 13.3 us -> 12.3 us  [chunk_part(): pl.pallas_call(functools.partial(chunk_kernel, start, before is None, las...]
  transfers between devices with their start and end apart: 13 -> 13, of which waited for: 6 -> 7; matrix products, arithmetic and copies ran while one was open for 0% -> 0% of each run, Pallas kernels for 35% -> 34%
where the time goes in v7:
time: 61.7 us; the launch traced here: 61.3 us
  Pallas kernels  23 us (37%)
  waiting for transfers between devices  20.5 us (33%)
  starting transfers between devices  13.6 us (22%)
  local copies, waits for them, and re-layouts  3.82 us (6%)
    ppermute x4, waiting for transfers between devices, sent(): return (lax.ppermute(piece, tm_pb, list(far_pairs())), near)  17 us
    pallas_call x4, Pallas kernels, chunk_part(): pl.pallas_call(functools.partial(chunk_kernel, start, before is None, las...  12.3 us
    pallas_call x1, Pallas kernels, own_part(): pl.pallas_call(own_kernel, in_specs=[vmem] * (1 + len(pieces)), out_specs...  5.98 us
    ppermute x4, starting transfers between devices, sent(): near = lax.ppermute(piece, tm_pb, list(near_pairs()))  4.74 us
    pallas_call x1, Pallas kernels, later_pieces(): pl.pallas_call(functools.partial(later_kernel, starts), in_specs=[pl.Bloc...  3.48 us
    unnamed x12, local copies, waits for them, and re-layouts  2.63 us
    ppermute x1, starting transfers between devices, shards(): lax.ppermute(here, tm_pb, [(source ^ 1, target ^ 1) for source, target in...  2.07 us
    ppermute x1, starting transfers between devices, shards(): beside = lax.ppermute(here_other, 'pix', [(0, 1), (1, 0)])  2.03 us
  transfers between devices with their start and end apart: 13, of which 7 were waited for; matrix products, arithmetic and copies ran while one was open for 0% of the time, Pallas kernels for 34%

profile of v7, /device:TPU:0, one launch (start us, length us, event | category | flops | bytes accessed | tf_op | source)
XLA Modules:
  0.0 61.3 jit_solution(7085595492348712603)
XLA Ops:
  0.0 1.2 %slice.21.refs_0_.own_ref = bf16[1,64,6144]{2,1,0:T(8,128)(2,1)S(1)} slice(bf16[1,64,32768]{2,1,0:T(8,128)(2,1)} %frames_ref.1), slice={[0:1], [0:64], [0:6144]} | slice | bytes 1572864 | tf_op jit(solution)/shard_map/slice | solution.py:306
  1.2 0.0 copy-start.4
  1.2 0.5 collective-permute-start
  1.7 2.1 %collective-permute-start.1 = (bf16[1,64,6144]{2,1,0:T(8,128)(2,1)S(1)}, bf16[1,64,6144]{2,1,0:T(8,128)(2,1)S(1)}, u32[]{:S(2)}, u32[]{:S(2)}) collective-permute-start(bf16[1,64,6144]{2,1,0:T(8,128)(2,1)S(1)} %slice.21.refs_0_.own_ref), channel_id=1, source_target_pairs={{1,5},{0,1},{4,0},{5,4},{9,13},{8,9},{12,8},{13,12},{17,21},{16,17... | collective-permute-start | bytes 2359304 | tf_op jit(solution)/shard_map/ppermute | solution.py:301
  3.8 3.5 %later_pieces.1 = (bf16[1,64,18432]{2,1,0:T(8,128)(2,1)}, bf16[1,64,6144]{2,1,0:T(8,128)(2,1)}, bf16[1,64,2048]{2,1,0:T(8,128)(2,1)}) custom-call(bf16[1,64,32768]{2,1,0:T(8,128)(2,1)} %frames_ref.1), custom_call_target="tpu_custom_call" | custom-call | tf_op jit(solution)/shard_map/later_pieces/pallas_call | solution.py:70
  7.3 1.3 %collective-permute-start.7 = (bf16[1,64,18432]{2,1,0:T(8,128)(2,1)}, bf16[1,64,18432]{2,1,0:T(8,128)(2,1)}, u32[]{:S(2)}, u32[]{:S(2)}) collective-permute-start(bf16[1,64,18432]{2,1,0:T(8,128)(2,1)} %get-tuple-element.15.refs_1_.own_ref), channel_id=1, source_target_pairs={{0,1},{1,9},{4,5},{5,13},{8,0},{9,17},{12,4},{13,21},{16,8},{17,25... | collective-permute-start | bytes 7077896 | tf_op jit(solution)/shard_map/ppermute | solution.py:302
  8.5 1.3 %collective-permute-start.8 = (bf16[1,64,18432]{2,1,0:T(8,128)(2,1)}, bf16[1,64,18432]{2,1,0:T(8,128)(2,1)}, u32[]{:S(2)}, u32[]{:S(2)}) collective-permute-start(bf16[1,64,18432]{2,1,0:T(8,128)(2,1)} %get-tuple-element.15.refs_1_.own_ref), channel_id=1, source_target_pairs={{1,5},{0,1},{4,0},{5,4},{9,13},{8,9},{12,8},{13,12},{17,21},{16,17... | collective-permute-start | bytes 7077896 | tf_op jit(solution)/shard_map/ppermute | solution.py:301
  9.8 0.0 collective-permute-start.5
  9.9 1.7 %copy-done = bf16[1,64,18432]{2,1,0:T(8,128)(2,1)S(1)} copy-done((bf16[1,64,18432]{2,1,0:T(8,128)(2,1)S(1)}, bf16[1,64,18432]{2,1,0:T(8,128)(2,1)}, u32[]{:S(2)}) %copy-start) | copy-done | bytes 2359320
  11.5 0.9 %copy-done.2 = bf16[1,64,2048]{2,1,0:T(8,128)(2,1)S(1)} copy-done((bf16[1,64,2048]{2,1,0:T(8,128)(2,1)S(1)}, bf16[1,64,2048]{2,1,0:T(8,128)(2,1)}, u32[]{:S(2)}) %copy-start.2) | copy-done | bytes 262168
  12.5 6.0 %own_tile_and_sums.1 = (f32[136,128]{1,0:T(8,128)S(1)}, bf16[1,64,6144]{2,1,0:T(8,128)(2,1)S(1)}) custom-call(s32[1,32768]{1,0:T(1,128)S(1)} %copy-done.4, bf16[1,64,6144]{2,1,0:T(8,128)(2,1)S(1)} %slice.21.refs_0_.own_ref, bf16[1,64,18432]{2,1,0:T(8,128)(2,1)S(1)} %copy-done, bf16[1,64,6144]{2,1,0:T(8,128)(2,1)} %get-tuple-element.16.refs_2_, ...), custom_call_target="tpu_custom_call" | custom-call | flops 8589934592 | bytes 16777216 | tf_op jit(solution)/shard_map/own_tile_and_sums/pallas_call | solution.py:109
  18.5 1.3 %collective-permute-start.6 = (bf16[1,64,6144]{2,1,0:T(8,128)(2,1)}, bf16[1,64,6144]{2,1,0:T(8,128)(2,1)S(1)}, u32[]{:S(2)}, u32[]{:S(2)}) collective-permute-start(bf16[1,64,6144]{2,1,0:T(8,128)(2,1)} %get-tuple-element.16.refs_2_), channel_id=1, source_target_pairs={{1,5},{0,1},{4,0},{5,4},{9,13},{8,9},{12,8},{13,12},{17,21},{16,17... | collective-permute-start | bytes 2359304 | tf_op jit(solution)/shard_map/ppermute | solution.py:301
  19.8 1.5 %collective-permute-start.2 = (f32[136,128]{1,0:T(8,128)S(1)}, f32[136,128]{1,0:T(8,128)S(1)}, u32[]{:S(2)}, u32[]{:S(2)}) collective-permute-start(f32[136,128]{1,0:T(8,128)S(1)} %get-tuple-element.19), channel_id=1, source_target_pairs={{0,2},{2,0},{1,3},{3,1},{4,6},{6,4},{5,7},{7,5},{8,10},{10,8},{9,1... | collective-permute-start | bytes 208904 | tf_op jit(solution)/shard_map/ppermute | solution.py:310
  21.3 1.9 %chunk_tiles.4.refs_0_ = f32[528,128]{1,0:T(8,128)S(1)} custom-call(bf16[1,64,6144]{2,1,0:T(8,128)(2,1)S(1)} %slice.21.refs_0_.own_ref, s32[1,32768]{1,0:T(1,128)S(1)} %copy-done.4, bf16[1,64,6144]{2,1,0:T(8,128)(2,1)S(1)} %collective-permute-done.far_ref, bf16[1,64,6144]{2,1,0:T(8,128)(2,1)S(1)} %collective-permute-done.1.near_ref, ...), custom_call_target="tpu_custom_call" | custom-call | flops 64424509440 | bytes 62914560 | tf_op jit(solution)/shard_map/chunk_tiles/pallas_call | solution.py:203
  23.1 0.9 %collective-permute-done.2 = f32[136,128]{1,0:T(8,128)S(1)} collective-permute-done((f32[136,128]{1,0:T(8,128)S(1)}, f32[136,128]{1,0:T(8,128)S(1)}, u32[]{:S(2)}, u32[]{:S(2)}) %collective-permute-start.2) | collective-permute-done | bytes 69664 | tf_op jit(solution)/shard_map/ppermute | solution.py:310
  24.1 0.0 collective-permute-start.3
  24.1 0.1 fusion.5
  24.2 15.3 %collective-permute-done.7.far_ref = bf16[1,64,18432]{2,1,0:T(8,128)(2,1)} collective-permute-done((bf16[1,64,18432]{2,1,0:T(8,128)(2,1)}, bf16[1,64,18432]{2,1,0:T(8,128)(2,1)}, u32[]{:S(2)}, u32[]{:S(2)}) %collective-permute-start.7) | collective-permute-done | bytes 2359328 | tf_op jit(solution)/shard_map/ppermute | solution.py:302
  39.6 7.6 %chunk_tiles.5.refs_0_ = f32[528,128]{1,0:T(8,128)S(1)} custom-call(bf16[1,64,18432]{2,1,0:T(8,128)(2,1)S(1)} %copy-done.1, s32[1,32768]{1,0:T(1,128)S(1)} %copy-done.4, bf16[1,64,18432]{2,1,0:T(8,128)(2,1)} %collective-permute-done.7.far_ref, bf16[1,64,18432]{2,1,0:T(8,128)(2,1)} %collective-permute-done.8.near_ref, f32[528,128]{1,0:T(8,128)S(1)} %chunk_tiles.4.refs_0_, ...), custom_call_target="tpu_custom_call" | custom-call | flops 9663676416 | bytes 9437184 | tf_op jit(solution)/shard_map/chunk_tiles/pallas_call | solution.py:203
  47.2 0.7 %collective-permute-done.5.far_ref = bf16[1,64,6144]{2,1,0:T(8,128)(2,1)S(1)} collective-permute-done((bf16[1,64,6144]{2,1,0:T(8,128)(2,1)}, bf16[1,64,6144]{2,1,0:T(8,128)(2,1)S(1)}, u32[]{:S(2)}, u32[]{:S(2)}) %collective-permute-start.5) | collective-permute-done | bytes 786464 | tf_op jit(solution)/shard_map/ppermute | solution.py:302
  47.9 1.9 %chunk_tiles.6.refs_0_ = f32[528,128]{1,0:T(8,128)S(1)} custom-call(bf16[1,64,6144]{2,1,0:T(8,128)(2,1)S(1)} %get-tuple-element.20.own_ref, s32[1,32768]{1,0:T(1,128)S(1)} %copy-done.4, bf16[1,64,6144]{2,1,0:T(8,128)(2,1)S(1)} %collective-permute-done.5.far_ref, bf16[1,64,6144]{2,1,0:T(8,128)(2,1)S(1)} %collective-permute-done.6.near_ref, ...), custom_call_target="tpu_custom_call" | custom-call | flops 3221225472 | bytes 3145728 | tf_op jit(solution)/shard_map/chunk_tiles/pallas_call | solution.py:203
  49.8 0.9 %collective-permute-done.3.far_ref = bf16[1,64,2048]{2,1,0:T(8,128)(2,1)S(1)} collective-permute-done((bf16[1,64,2048]{2,1,0:T(8,128)(2,1)S(1)}, bf16[1,64,2048]{2,1,0:T(8,128)(2,1)S(1)}, u32[]{:S(2)}, u32[]{:S(2)}) %collective-permute-start.3) | collective-permute-done | bytes 262176 | tf_op jit(solution)/shard_map/ppermute | solution.py:302
  50.7 1.0 %chunk_tiles.7 = (f32[136,128]{1,0:T(8,128)S(1)}, f32[136,128]{1,0:T(8,128)S(1)}, f32[72,128]{1,0:T(8,128)S(1)}, f32[72,128]{1,0:T(8,128)S(1)}) custom-call(bf16[1,64,2048]{2,1,0:T(8,128)(2,1)S(1)} %copy-done.3, s32[1,32768]{1,0:T(1,128)S(1)} %copy-done.4, bf16[1,64,2048]{2,1,0:T(8,128)(2,1)S(1)} %collective-permute-done.3.far_ref, ...), custom_call_target="tpu_custom_call" | custom-call | flops 1073741824 | bytes 1048576 | tf_op jit(solution)/shard_map/chunk_tiles/pallas_call | solution.py:203
  51.7 2.0 %collective-permute-start.9 = (f32[136,128]{1,0:T(8,128)S(1)}, f32[136,128]{1,0:T(8,128)S(1)}, u32[]{:S(2)}, u32[]{:S(2)}) collective-permute-start(f32[136,128]{1,0:T(8,128)S(1)} %get-tuple-element.22), channel_id=1, source_target_pairs={{0,2},{2,0},{1,3},{3,1},{4,6},{6,4},{5,7},{7,5},{8,10},{10,8},{9,1... | collective-permute-start | bytes 208904 | tf_op jit(solution)/shard_map/ppermute | solution.py:332
  53.7 1.3 %collective-permute-start.11 = (f32[72,128]{1,0:T(8,128)S(1)}, f32[72,128]{1,0:T(8,128)S(1)}, u32[]{:S(2)}, u32[]{:S(2)}) collective-permute-start(f32[72,128]{1,0:T(8,128)S(1)} %get-tuple-element.23), channel_id=1, source_target_pairs={{0,4},{2,6},{4,0},{6,2},{8,12},{10,14},{12,8},{14,10},{16,20},{18,... | collective-permute-start | bytes 110600 | tf_op jit(solution)/shard_map/ppermute | solution.py:330
  55.0 0.3 collective-permute-start.12
  55.3 0.7 %collective-permute-done.9 = f32[136,128]{1,0:T(8,128)S(1)} collective-permute-done((f32[136,128]{1,0:T(8,128)S(1)}, f32[136,128]{1,0:T(8,128)S(1)}, u32[]{:S(2)}, u32[]{:S(2)}) %collective-permute-start.9) | collective-permute-done | bytes 69664 | tf_op jit(solution)/shard_map/ppermute | solution.py:332
  56.1 2.1 %collective-permute-start.10 = (f32[136,128]{1,0:T(8,128)S(1)}, f32[136,128]{1,0:T(8,128)S(1)}, u32[]{:S(2)}, u32[]{:S(2)}) collective-permute-start(f32[136,128]{1,0:T(8,128)S(1)} %add.36.kept_ref), channel_id=1, source_target_pairs={{1,0},{0,8},{5,4},{4,12},{9,1},{8,16},{13,5},{12,20},{17,9},{16,24... | collective-permute-start | bytes 208904 | tf_op jit(solution)/shard_map/ppermute | solution.py:335
  58.2 0.1 pad_maximum_fusion.factor_ref
  58.3 1.6 %collective-permute-done.12.other_ref = f32[72,128]{1,0:T(8,128)S(1)} collective-permute-done((f32[72,128]{1,0:T(8,128)S(1)}, f32[72,128]{1,0:T(8,128)S(1)}, u32[]{:S(2)}, u32[]{:S(2)}) %collective-permute-start.12) | collective-permute-done | bytes 36896 | tf_op jit(solution)/shard_map/ppermute | solution.py:330
  59.9 0.2 collective-permute-done.10.here_ref
  60.1 1.2 %normalise_and_skew.1 = f32[1,4,64,64]{3,2,1,0:T(8,128)} custom-call(f32[128,128]{1,0:T(8,128)S(1)} %pad_maximum_fusion.factor_ref, f32[136,128]{1,0:T(8,128)S(1)} %add.35.refs_1_.own_ref, f32[136,128]{1,0:T(8,128)S(1)} %add.36.kept_ref, f32[136,128]{1,0:T(8,128)S(1)} %collective-permute-done.10.here_ref, f32[72,128]{1,0:T(8,128)S(1)} %collective-permute-done.11.same_ref, ...), custom_call_target="tpu_custom_call" | custom-call | tf_op jit(solution)/shard_map/normalise_and_skew/pallas_call | solution.py:260
  (22 shorter events, 0.1 us)
Async XLA Ops:
  1.2 8.7 %copy-start.4 = (s32[1,32768]{1,0:T(1,128)S(1)}, s32[1,32768]{1,0:T(1,128)}, u32[]{:S(2)}) copy-start(s32[1,32768]{1,0:T(1,128)} %label_ref.9) | copy-start | bytes 393220
  1.2 17.3 %collective-permute-start = (bf16[1,64,6144]{2,1,0:T(8,128)(2,1)S(1)}, bf16[1,64,6144]{2,1,0:T(8,128)(2,1)S(1)}, u32[]{:S(2)}, u32[]{:S(2)}) collective-permute-start(bf16[1,64,6144]{2,1,0:T(8,128)(2,1)S(1)} %slice.21.refs_0_.own_ref), channel_id=1, source_target_pairs={{0,1},{1,9},{4,5},{5,13},{8,0},{9,17},{12,4},{13,21},{16,8},{17,25... | collective-permute-start | bytes 2359304 | tf_op jit(solution)/shard_map/ppermute | solution.py:302
  1.7 18.1 %collective-permute-start.1 = (bf16[1,64,6144]{2,1,0:T(8,128)(2,1)S(1)}, bf16[1,64,6144]{2,1,0:T(8,128)(2,1)S(1)}, u32[]{:S(2)}, u32[]{:S(2)}) collective-permute-start(bf16[1,64,6144]{2,1,0:T(8,128)(2,1)S(1)} %slice.21.refs_0_.own_ref), channel_id=1, source_target_pairs={{1,5},{0,1},{4,0},{5,4},{9,13},{8,9},{12,8},{13,12},{17,21},{16,17... | collective-permute-start | bytes 2359304 | tf_op jit(solution)/shard_map/ppermute | solution.py:301
  7.3 32.3 %collective-permute-start.7 = (bf16[1,64,18432]{2,1,0:T(8,128)(2,1)}, bf16[1,64,18432]{2,1,0:T(8,128)(2,1)}, u32[]{:S(2)}, u32[]{:S(2)}) collective-permute-start(bf16[1,64,18432]{2,1,0:T(8,128)(2,1)} %get-tuple-element.15.refs_1_.own_ref), channel_id=1, source_target_pairs={{0,1},{1,9},{4,5},{5,13},{8,0},{9,17},{12,4},{13,21},{16,8},{17,25... | collective-permute-start | bytes 7077896 | tf_op jit(solution)/shard_map/ppermute | solution.py:302
  8.5 31.1 %collective-permute-start.8 = (bf16[1,64,18432]{2,1,0:T(8,128)(2,1)}, bf16[1,64,18432]{2,1,0:T(8,128)(2,1)}, u32[]{:S(2)}, u32[]{:S(2)}) collective-permute-start(bf16[1,64,18432]{2,1,0:T(8,128)(2,1)} %get-tuple-element.15.refs_1_.own_ref), channel_id=1, source_target_pairs={{1,5},{0,1},{4,0},{5,4},{9,13},{8,9},{12,8},{13,12},{17,21},{16,17... | collective-permute-start | bytes 7077896 | tf_op jit(solution)/shard_map/ppermute | solution.py:301
  9.8 38.1 %collective-permute-start.5 = (bf16[1,64,6144]{2,1,0:T(8,128)(2,1)}, bf16[1,64,6144]{2,1,0:T(8,128)(2,1)S(1)}, u32[]{:S(2)}, u32[]{:S(2)}) collective-permute-start(bf16[1,64,6144]{2,1,0:T(8,128)(2,1)} %get-tuple-element.16.refs_2_), channel_id=1, source_target_pairs={{0,1},{1,9},{4,5},{5,13},{8,0},{9,17},{12,4},{13,21},{16,8},{17,25... | collective-permute-start | bytes 2359304 | tf_op jit(solution)/shard_map/ppermute | solution.py:302
  9.8 1.7 %copy-start = (bf16[1,64,18432]{2,1,0:T(8,128)(2,1)S(1)}, bf16[1,64,18432]{2,1,0:T(8,128)(2,1)}, u32[]{:S(2)}) copy-start(bf16[1,64,18432]{2,1,0:T(8,128)(2,1)} %get-tuple-element.15.refs_1_.own_ref) | copy-start | bytes 7077892
  11.5 0.9 %copy-start.2 = (bf16[1,64,2048]{2,1,0:T(8,128)(2,1)S(1)}, bf16[1,64,2048]{2,1,0:T(8,128)(2,1)}, u32[]{:S(2)}) copy-start(bf16[1,64,2048]{2,1,0:T(8,128)(2,1)} %get-tuple-element.17.refs_3_.own_ref) | copy-start | bytes 786436
  18.5 29.5 %collective-permute-start.6 = (bf16[1,64,6144]{2,1,0:T(8,128)(2,1)}, bf16[1,64,6144]{2,1,0:T(8,128)(2,1)S(1)}, u32[]{:S(2)}, u32[]{:S(2)}) collective-permute-start(bf16[1,64,6144]{2,1,0:T(8,128)(2,1)} %get-tuple-element.16.refs_2_), channel_id=1, source_target_pairs={{1,5},{0,1},{4,0},{5,4},{9,13},{8,9},{12,8},{13,12},{17,21},{16,17... | collective-permute-start | bytes 2359304 | tf_op jit(solution)/shard_map/ppermute | solution.py:301
  19.8 4.3 %collective-permute-start.2 = (f32[136,128]{1,0:T(8,128)S(1)}, f32[136,128]{1,0:T(8,128)S(1)}, u32[]{:S(2)}, u32[]{:S(2)}) collective-permute-start(f32[136,128]{1,0:T(8,128)S(1)} %get-tuple-element.19), channel_id=1, source_target_pairs={{0,2},{2,0},{1,3},{3,1},{4,6},{6,4},{5,7},{7,5},{8,10},{10,8},{9,1... | collective-permute-start | bytes 208904 | tf_op jit(solution)/shard_map/ppermute | solution.py:310
  21.3 2.8 %copy-start.3 = (bf16[1,64,2048]{2,1,0:T(8,128)(2,1)S(1)}, bf16[1,64,2048]{2,1,0:T(8,128)(2,1)}, u32[]{:S(2)}) copy-start(bf16[1,64,2048]{2,1,0:T(8,128)(2,1)} %get-tuple-element.17.refs_3_.own_ref) | copy-start | bytes 786436
  21.3 2.8 %copy-start.5 = (s32[1,4]{1,0:T(1,128)S(1)}, s32[1,4]{1,0:T(1,128)}, u32[]{:S(2)}) copy-start(s32[1,4]{1,0:T(1,128)} %param.5) | copy-start | bytes 52
  21.3 18.3 %copy-start.1 = (bf16[1,64,18432]{2,1,0:T(8,128)(2,1)S(1)}, bf16[1,64,18432]{2,1,0:T(8,128)(2,1)}, u32[]{:S(2)}) copy-start(bf16[1,64,18432]{2,1,0:T(8,128)(2,1)} %get-tuple-element.15.refs_1_.own_ref) | copy-start | bytes 7077892
  24.1 26.6 %collective-permute-start.3 = (bf16[1,64,2048]{2,1,0:T(8,128)(2,1)S(1)}, bf16[1,64,2048]{2,1,0:T(8,128)(2,1)S(1)}, u32[]{:S(2)}, u32[]{:S(2)}) collective-permute-start(bf16[1,64,2048]{2,1,0:T(8,128)(2,1)S(1)} %copy-done.3), channel_id=1, source_target_pairs={{0,1},{1,9},{4,5},{5,13},{8,0},{9,17},{12,4},{13,21},{16,8},{17,25... | collective-permute-start | bytes 786440 | tf_op jit(solution)/shard_map/ppermute | solution.py:302
  39.6 11.1 %collective-permute-start.4 = (bf16[1,64,2048]{2,1,0:T(8,128)(2,1)S(1)}, bf16[1,64,2048]{2,1,0:T(8,128)(2,1)S(1)}, u32[]{:S(2)}, u32[]{:S(2)}) collective-permute-start(bf16[1,64,2048]{2,1,0:T(8,128)(2,1)S(1)} %copy-done.3), channel_id=1, source_target_pairs={{1,5},{0,1},{4,0},{5,4},{9,13},{8,9},{12,8},{13,12},{17,21},{16,17... | collective-permute-start | bytes 786440 | tf_op jit(solution)/shard_map/ppermute | solution.py:301
  51.7 4.4 %collective-permute-start.9 = (f32[136,128]{1,0:T(8,128)S(1)}, f32[136,128]{1,0:T(8,128)S(1)}, u32[]{:S(2)}, u32[]{:S(2)}) collective-permute-start(f32[136,128]{1,0:T(8,128)S(1)} %get-tuple-element.22), channel_id=1, source_target_pairs={{0,2},{2,0},{1,3},{3,1},{4,6},{6,4},{5,7},{7,5},{8,10},{10,8},{9,1... | collective-permute-start | bytes 208904 | tf_op jit(solution)/shard_map/ppermute | solution.py:332
  53.7 4.5 %collective-permute-start.11 = (f32[72,128]{1,0:T(8,128)S(1)}, f32[72,128]{1,0:T(8,128)S(1)}, u32[]{:S(2)}, u32[]{:S(2)}) collective-permute-start(f32[72,128]{1,0:T(8,128)S(1)} %get-tuple-element.23), channel_id=1, source_target_pairs={{0,4},{2,6},{4,0},{6,2},{8,12},{10,14},{12,8},{14,10},{16,20},{18,... | collective-permute-start | bytes 110600 | tf_op jit(solution)/shard_map/ppermute | solution.py:330
  55.0 4.9 %collective-permute-start.12 = (f32[72,128]{1,0:T(8,128)S(1)}, f32[72,128]{1,0:T(8,128)S(1)}, u32[]{:S(2)}, u32[]{:S(2)}) collective-permute-start(f32[72,128]{1,0:T(8,128)S(1)} %get-tuple-element.24), channel_id=1, source_target_pairs={{0,6},{2,4},{4,2},{6,0},{8,14},{10,12},{12,10},{14,8},{16,22},{18,... | collective-permute-start | bytes 110600 | tf_op jit(solution)/shard_map/ppermute | solution.py:330
  56.1 4.0 %collective-permute-start.10 = (f32[136,128]{1,0:T(8,128)S(1)}, f32[136,128]{1,0:T(8,128)S(1)}, u32[]{:S(2)}, u32[]{:S(2)}) collective-permute-start(f32[136,128]{1,0:T(8,128)S(1)} %add.36.kept_ref), channel_id=1, source_target_pairs={{1,0},{0,8},{5,4},{4,12},{9,1},{8,16},{13,5},{12,20},{17,9},{16,24... | collective-permute-start | bytes 208904 | tf_op jit(solution)/shard_map/ppermute | solution.py:335

commit v8 on v7

--- a/solution.py
+++ b/solution.py
@@ -317,7 +317,7 @@
         before = states[-1] if states else None
         awaited = own
         if index == 0:
-            awaited = far[:, :8, :128]
+            awaited = near[:, :8, :128]
         result = chunk_part(piece, annulus_label, starts[index], far, near, before, awaited, last)
         states.append(result if last else result[0])
     state = states[-1]

time: 61.7 us -> 61.8 us (level)
  starting transfers between devices: 13.6 us -> 14.4 us
    ppermute x4, starting transfers between devices: 1.73 us -> 4.06 us  [sent(): return (lax.ppermute(piece, tm_pb, list(far_pairs())), near)]
    ppermute x4, starting transfers between devices: 4.74 us -> 3.08 us  [sent(): near = lax.ppermute(piece, tm_pb, list(near_pairs()))]
    ppermute x4, waiting for transfers between devices: 17 us -> 16.3 us  [sent(): return (lax.ppermute(piece, tm_pb, list(far_pairs())), near)]
  transfers between devices with their start and end apart: 13 -> 13, of which waited for: 7 -> 6; matrix products, arithmetic and copies ran while one was open for 0% -> 0% of each run, Pallas kernels for 34% -> 34%
where the time goes in v8:
time: 61.8 us; the launch traced here: 61.6 us
  Pallas kernels  23 us (37%)
  waiting for transfers between devices  20 us (32%)
  starting transfers between devices  14.4 us (23%)
  local copies, waits for them, and re-layouts  3.83 us (6%)
    ppermute x4, waiting for transfers between devices, sent(): return (lax.ppermute(piece, tm_pb, list(far_pairs())), near)  16.3 us
    pallas_call x4, Pallas kernels, chunk_part(): pl.pallas_call(functools.partial(chunk_kernel, start, before is None, las...  12.3 us
    pallas_call x1, Pallas kernels, own_part(): pl.pallas_call(own_kernel, in_specs=[vmem] * (1 + len(pieces)), out_specs...  5.98 us
    ppermute x4, starting transfers between devices, sent(): return (lax.ppermute(piece, tm_pb, list(far_pairs())), near)  4.06 us
    pallas_call x1, Pallas kernels, later_pieces(): pl.pallas_call(functools.partial(later_kernel, starts), in_specs=[pl.Bloc...  3.48 us
    ppermute x4, starting transfers between devices, sent(): near = lax.ppermute(piece, tm_pb, list(near_pairs()))  3.08 us
    unnamed x12, local copies, waits for them, and re-layouts  2.63 us
    ppermute x2, waiting for transfers between devices, swapped(): return lax.ppermute(message, ('tm', 'pix'), pairs)  2.14 us
  transfers between devices with their start and end apart: 13, of which 6 were waited for; matrix products, arithmetic and copies ran while one was open for 0% of the time, Pallas kernels for 34%

profile of v8, /device:TPU:0, one launch (start us, length us, event | category | flops | bytes accessed | tf_op | source)
XLA Modules:
  0.0 61.6 jit_solution(9796367935758686863)
XLA Ops:
  0.0 1.2 %slice.21.refs_0_.own_ref = bf16[1,64,6144]{2,1,0:T(8,128)(2,1)S(1)} slice(bf16[1,64,32768]{2,1,0:T(8,128)(2,1)} %frames_ref.1), slice={[0:1], [0:64], [0:6144]} | slice | bytes 1572864 | tf_op jit(solution)/shard_map/slice | solution.py:306
  1.2 0.0 copy-start.4
  1.2 0.5 collective-permute-start.1
  1.7 2.1 %collective-permute-start = (bf16[1,64,6144]{2,1,0:T(8,128)(2,1)S(1)}, bf16[1,64,6144]{2,1,0:T(8,128)(2,1)S(1)}, u32[]{:S(2)}, u32[]{:S(2)}) collective-permute-start(bf16[1,64,6144]{2,1,0:T(8,128)(2,1)S(1)} %slice.21.refs_0_.own_ref), channel_id=1, source_target_pairs={{0,1},{1,9},{4,5},{5,13},{8,0},{9,17},{12,4},{13,21},{16,8},{17,25... | collective-permute-start | bytes 2359304 | tf_op jit(solution)/shard_map/ppermute | solution.py:302
  3.7 3.5 %later_pieces.1 = (bf16[1,64,18432]{2,1,0:T(8,128)(2,1)}, bf16[1,64,6144]{2,1,0:T(8,128)(2,1)}, bf16[1,64,2048]{2,1,0:T(8,128)(2,1)}) custom-call(bf16[1,64,32768]{2,1,0:T(8,128)(2,1)} %frames_ref.1), custom_call_target="tpu_custom_call" | custom-call | tf_op jit(solution)/shard_map/later_pieces/pallas_call | solution.py:70
  7.2 1.3 %collective-permute-start.7 = (bf16[1,64,18432]{2,1,0:T(8,128)(2,1)}, bf16[1,64,18432]{2,1,0:T(8,128)(2,1)}, u32[]{:S(2)}, u32[]{:S(2)}) collective-permute-start(bf16[1,64,18432]{2,1,0:T(8,128)(2,1)} %get-tuple-element.15.refs_1_.own_ref), channel_id=1, source_target_pairs={{0,1},{1,9},{4,5},{5,13},{8,0},{9,17},{12,4},{13,21},{16,8},{17,25... | collective-permute-start | bytes 7077896 | tf_op jit(solution)/shard_map/ppermute | solution.py:302
  8.5 1.3 %collective-permute-start.8 = (bf16[1,64,18432]{2,1,0:T(8,128)(2,1)}, bf16[1,64,18432]{2,1,0:T(8,128)(2,1)}, u32[]{:S(2)}, u32[]{:S(2)}) collective-permute-start(bf16[1,64,18432]{2,1,0:T(8,128)(2,1)} %get-tuple-element.15.refs_1_.own_ref), channel_id=1, source_target_pairs={{1,5},{0,1},{4,0},{5,4},{9,13},{8,9},{12,8},{13,12},{17,21},{16,17... | collective-permute-start | bytes 7077896 | tf_op jit(solution)/shard_map/ppermute | solution.py:301
  9.8 0.7 %collective-permute-start.5 = (bf16[1,64,6144]{2,1,0:T(8,128)(2,1)}, bf16[1,64,6144]{2,1,0:T(8,128)(2,1)S(1)}, u32[]{:S(2)}, u32[]{:S(2)}) collective-permute-start(bf16[1,64,6144]{2,1,0:T(8,128)(2,1)} %get-tuple-element.16.refs_2_), channel_id=1, source_target_pairs={{0,1},{1,9},{4,5},{5,13},{8,0},{9,17},{12,4},{13,21},{16,8},{17,25... | collective-permute-start | bytes 2359304 | tf_op jit(solution)/shard_map/ppermute | solution.py:302
  10.5 1.7 %copy-done = bf16[1,64,18432]{2,1,0:T(8,128)(2,1)S(1)} copy-done((bf16[1,64,18432]{2,1,0:T(8,128)(2,1)S(1)}, bf16[1,64,18432]{2,1,0:T(8,128)(2,1)}, u32[]{:S(2)}) %copy-start) | copy-done | bytes 2359320
  12.2 0.9 %copy-done.2 = bf16[1,64,2048]{2,1,0:T(8,128)(2,1)S(1)} copy-done((bf16[1,64,2048]{2,1,0:T(8,128)(2,1)S(1)}, bf16[1,64,2048]{2,1,0:T(8,128)(2,1)}, u32[]{:S(2)}) %copy-start.2) | copy-done | bytes 262168
  13.1 6.0 %own_tile_and_sums.1 = (f32[136,128]{1,0:T(8,128)S(1)}, bf16[1,64,6144]{2,1,0:T(8,128)(2,1)S(1)}) custom-call(s32[1,32768]{1,0:T(1,128)S(1)} %copy-done.4, bf16[1,64,6144]{2,1,0:T(8,128)(2,1)S(1)} %slice.21.refs_0_.own_ref, bf16[1,64,18432]{2,1,0:T(8,128)(2,1)S(1)} %copy-done, bf16[1,64,6144]{2,1,0:T(8,128)(2,1)} %get-tuple-element.16.refs_2_, ...), custom_call_target="tpu_custom_call" | custom-call | flops 8589934592 | bytes 16777216 | tf_op jit(solution)/shard_map/own_tile_and_sums/pallas_call | solution.py:109
  19.1 0.0 collective-permute-done.1.near_ref
  19.1 1.3 %collective-permute-start.6 = (bf16[1,64,6144]{2,1,0:T(8,128)(2,1)}, bf16[1,64,6144]{2,1,0:T(8,128)(2,1)S(1)}, u32[]{:S(2)}, u32[]{:S(2)}) collective-permute-start(bf16[1,64,6144]{2,1,0:T(8,128)(2,1)} %get-tuple-element.16.refs_2_), channel_id=1, source_target_pairs={{1,5},{0,1},{4,0},{5,4},{9,13},{8,9},{12,8},{13,12},{17,21},{16,17... | collective-permute-start | bytes 2359304 | tf_op jit(solution)/shard_map/ppermute | solution.py:301
  20.4 0.0 collective-permute-done.far_ref
  20.4 1.5 %collective-permute-start.2 = (f32[136,128]{1,0:T(8,128)S(1)}, f32[136,128]{1,0:T(8,128)S(1)}, u32[]{:S(2)}, u32[]{:S(2)}) collective-permute-start(f32[136,128]{1,0:T(8,128)S(1)} %get-tuple-element.19), channel_id=1, source_target_pairs={{0,2},{2,0},{1,3},{3,1},{4,6},{6,4},{5,7},{7,5},{8,10},{10,8},{9,1... | collective-permute-start | bytes 208904 | tf_op jit(solution)/shard_map/ppermute | solution.py:310
  21.9 1.9 %chunk_tiles.4.refs_0_ = f32[528,128]{1,0:T(8,128)S(1)} custom-call(bf16[1,64,6144]{2,1,0:T(8,128)(2,1)S(1)} %slice.21.refs_0_.own_ref, s32[1,32768]{1,0:T(1,128)S(1)} %copy-done.4, bf16[1,64,6144]{2,1,0:T(8,128)(2,1)S(1)} %collective-permute-done.far_ref, bf16[1,64,6144]{2,1,0:T(8,128)(2,1)S(1)} %collective-permute-done.1.near_ref, ...), custom_call_target="tpu_custom_call" | custom-call | flops 64424509440 | bytes 62914560 | tf_op jit(solution)/shard_map/chunk_tiles/pallas_call | solution.py:203
  23.8 0.9 %collective-permute-done.2 = f32[136,128]{1,0:T(8,128)S(1)} collective-permute-done((f32[136,128]{1,0:T(8,128)S(1)}, f32[136,128]{1,0:T(8,128)S(1)}, u32[]{:S(2)}, u32[]{:S(2)}) %collective-permute-start.2) | collective-permute-done | bytes 69664 | tf_op jit(solution)/shard_map/ppermute | solution.py:310
  24.8 0.1 fusion.5
  24.9 14.7 %collective-permute-done.7.far_ref = bf16[1,64,18432]{2,1,0:T(8,128)(2,1)} collective-permute-done((bf16[1,64,18432]{2,1,0:T(8,128)(2,1)}, bf16[1,64,18432]{2,1,0:T(8,128)(2,1)}, u32[]{:S(2)}, u32[]{:S(2)}) %collective-permute-start.7) | collective-permute-done | bytes 2359328 | tf_op jit(solution)/shard_map/ppermute | solution.py:302
  39.6 0.0 collective-permute-done.8.near_ref
  39.6 7.6 %chunk_tiles.5.refs_0_ = f32[528,128]{1,0:T(8,128)S(1)} custom-call(bf16[1,64,18432]{2,1,0:T(8,128)(2,1)S(1)} %copy-done.1, s32[1,32768]{1,0:T(1,128)S(1)} %copy-done.4, bf16[1,64,18432]{2,1,0:T(8,128)(2,1)} %collective-permute-done.7.far_ref, bf16[1,64,18432]{2,1,0:T(8,128)(2,1)} %collective-permute-done.8.near_ref, f32[528,128]{1,0:T(8,128)S(1)} %chunk_tiles.4.refs_0_, ...), custom_call_target="tpu_custom_call" | custom-call | flops 9663676416 | bytes 9437184 | tf_op jit(solution)/shard_map/chunk_tiles/pallas_call | solution.py:203
  47.3 0.7 %collective-permute-done.5.far_ref = bf16[1,64,6144]{2,1,0:T(8,128)(2,1)S(1)} collective-permute-done((bf16[1,64,6144]{2,1,0:T(8,128)(2,1)}, bf16[1,64,6144]{2,1,0:T(8,128)(2,1)S(1)}, u32[]{:S(2)}, u32[]{:S(2)}) %collective-permute-start.5) | collective-permute-done | bytes 786464 | tf_op jit(solution)/shard_map/ppermute | solution.py:302
  47.9 1.9 %chunk_tiles.6.refs_0_ = f32[528,128]{1,0:T(8,128)S(1)} custom-call(bf16[1,64,6144]{2,1,0:T(8,128)(2,1)S(1)} %get-tuple-element.20.own_ref, s32[1,32768]{1,0:T(1,128)S(1)} %copy-done.4, bf16[1,64,6144]{2,1,0:T(8,128)(2,1)S(1)} %collective-permute-done.5.far_ref, bf16[1,64,6144]{2,1,0:T(8,128)(2,1)S(1)} %collective-permute-done.6.near_ref, ...), custom_call_target="tpu_custom_call" | custom-call | flops 3221225472 | bytes 3145728 | tf_op jit(solution)/shard_map/chunk_tiles/pallas_call | solution.py:203
  49.8 0.9 %collective-permute-done.3.far_ref = bf16[1,64,2048]{2,1,0:T(8,128)(2,1)S(1)} collective-permute-done((bf16[1,64,2048]{2,1,0:T(8,128)(2,1)S(1)}, bf16[1,64,2048]{2,1,0:T(8,128)(2,1)S(1)}, u32[]{:S(2)}, u32[]{:S(2)}) %collective-permute-start.3) | collective-permute-done | bytes 262176 | tf_op jit(solution)/shard_map/ppermute | solution.py:302
  50.8 1.0 %chunk_tiles.7 = (f32[136,128]{1,0:T(8,128)S(1)}, f32[136,128]{1,0:T(8,128)S(1)}, f32[72,128]{1,0:T(8,128)S(1)}, f32[72,128]{1,0:T(8,128)S(1)}) custom-call(bf16[1,64,2048]{2,1,0:T(8,128)(2,1)S(1)} %copy-done.3, s32[1,32768]{1,0:T(1,128)S(1)} %copy-done.4, bf16[1,64,2048]{2,1,0:T(8,128)(2,1)S(1)} %collective-permute-done.3.far_ref, ...), custom_call_target="tpu_custom_call" | custom-call | flops 1073741824 | bytes 1048576 | tf_op jit(solution)/shard_map/chunk_tiles/pallas_call | solution.py:203
  51.7 2.0 %collective-permute-start.9 = (f32[136,128]{1,0:T(8,128)S(1)}, f32[136,128]{1,0:T(8,128)S(1)}, u32[]{:S(2)}, u32[]{:S(2)}) collective-permute-start(f32[136,128]{1,0:T(8,128)S(1)} %get-tuple-element.22), channel_id=1, source_target_pairs={{0,2},{2,0},{1,3},{3,1},{4,6},{6,4},{5,7},{7,5},{8,10},{10,8},{9,1... | collective-permute-start | bytes 208904 | tf_op jit(solution)/shard_map/ppermute | solution.py:332
  53.8 1.8 %collective-permute-start.11 = (f32[72,128]{1,0:T(8,128)S(1)}, f32[72,128]{1,0:T(8,128)S(1)}, u32[]{:S(2)}, u32[]{:S(2)}) collective-permute-start(f32[72,128]{1,0:T(8,128)S(1)} %get-tuple-element.23), channel_id=1, source_target_pairs={{0,4},{2,6},{4,0},{6,2},{8,12},{10,14},{12,8},{14,10},{16,20},{18,... | collective-permute-start | bytes 110600 | tf_op jit(solution)/shard_map/ppermute | solution.py:330
  55.5 0.6 collective-permute-done.9
  56.1 2.0 %collective-permute-start.10 = (f32[136,128]{1,0:T(8,128)S(1)}, f32[136,128]{1,0:T(8,128)S(1)}, u32[]{:S(2)}, u32[]{:S(2)}) collective-permute-start(f32[136,128]{1,0:T(8,128)S(1)} %add.36.kept_ref), channel_id=1, source_target_pairs={{1,0},{0,8},{5,4},{4,12},{9,1},{8,16},{13,5},{12,20},{17,9},{16,24... | collective-permute-start | bytes 208904 | tf_op jit(solution)/shard_map/ppermute | solution.py:335
  58.2 0.1 pad_maximum_fusion.factor_ref
  58.3 2.1 %collective-permute-done.12.other_ref = f32[72,128]{1,0:T(8,128)S(1)} collective-permute-done((f32[72,128]{1,0:T(8,128)S(1)}, f32[72,128]{1,0:T(8,128)S(1)}, u32[]{:S(2)}, u32[]{:S(2)}) %collective-permute-start.12) | collective-permute-done | bytes 36896 | tf_op jit(solution)/shard_map/ppermute | solution.py:330
  60.4 1.2 %normalise_and_skew.1 = f32[1,4,64,64]{3,2,1,0:T(8,128)} custom-call(f32[128,128]{1,0:T(8,128)S(1)} %pad_maximum_fusion.factor_ref, f32[136,128]{1,0:T(8,128)S(1)} %add.35.refs_1_.own_ref, f32[136,128]{1,0:T(8,128)S(1)} %add.36.kept_ref, f32[136,128]{1,0:T(8,128)S(1)} %collective-permute-done.10.here_ref, f32[72,128]{1,0:T(8,128)S(1)} %collective-permute-done.11.same_ref, ...), custom_call_target="tpu_custom_call" | custom-call | tf_op jit(solution)/shard_map/normalise_and_skew/pallas_call | solution.py:260
  (22 shorter events, 0.1 us)
Async XLA Ops:
  1.2 9.3 %copy-start.4 = (s32[1,32768]{1,0:T(1,128)S(1)}, s32[1,32768]{1,0:T(1,128)}, u32[]{:S(2)}) copy-start(s32[1,32768]{1,0:T(1,128)} %label_ref.9) | copy-start | bytes 393220
  1.2 17.9 %collective-permute-start.1 = (bf16[1,64,6144]{2,1,0:T(8,128)(2,1)S(1)}, bf16[1,64,6144]{2,1,0:T(8,128)(2,1)S(1)}, u32[]{:S(2)}, u32[]{:S(2)}) collective-permute-start(bf16[1,64,6144]{2,1,0:T(8,128)(2,1)S(1)} %slice.21.refs_0_.own_ref), channel_id=1, source_target_pairs={{1,5},{0,1},{4,0},{5,4},{9,13},{8,9},{12,8},{13,12},{17,21},{16,17... | collective-permute-start | bytes 2359304 | tf_op jit(solution)/shard_map/ppermute | solution.py:301
  1.7 18.8 %collective-permute-start = (bf16[1,64,6144]{2,1,0:T(8,128)(2,1)S(1)}, bf16[1,64,6144]{2,1,0:T(8,128)(2,1)S(1)}, u32[]{:S(2)}, u32[]{:S(2)}) collective-permute-start(bf16[1,64,6144]{2,1,0:T(8,128)(2,1)S(1)} %slice.21.refs_0_.own_ref), channel_id=1, source_target_pairs={{0,1},{1,9},{4,5},{5,13},{8,0},{9,17},{12,4},{13,21},{16,8},{17,25... | collective-permute-start | bytes 2359304 | tf_op jit(solution)/shard_map/ppermute | solution.py:302
  7.2 32.4 %collective-permute-start.7 = (bf16[1,64,18432]{2,1,0:T(8,128)(2,1)}, bf16[1,64,18432]{2,1,0:T(8,128)(2,1)}, u32[]{:S(2)}, u32[]{:S(2)}) collective-permute-start(bf16[1,64,18432]{2,1,0:T(8,128)(2,1)} %get-tuple-element.15.refs_1_.own_ref), channel_id=1, source_target_pairs={{0,1},{1,9},{4,5},{5,13},{8,0},{9,17},{12,4},{13,21},{16,8},{17,25... | collective-permute-start | bytes 7077896 | tf_op jit(solution)/shard_map/ppermute | solution.py:302
  8.5 31.1 %collective-permute-start.8 = (bf16[1,64,18432]{2,1,0:T(8,128)(2,1)}, bf16[1,64,18432]{2,1,0:T(8,128)(2,1)}, u32[]{:S(2)}, u32[]{:S(2)}) collective-permute-start(bf16[1,64,18432]{2,1,0:T(8,128)(2,1)} %get-tuple-element.15.refs_1_.own_ref), channel_id=1, source_target_pairs={{1,5},{0,1},{4,0},{5,4},{9,13},{8,9},{12,8},{13,12},{17,21},{16,17... | collective-permute-start | bytes 7077896 | tf_op jit(solution)/shard_map/ppermute | solution.py:301
  9.8 38.1 %collective-permute-start.5 = (bf16[1,64,6144]{2,1,0:T(8,128)(2,1)}, bf16[1,64,6144]{2,1,0:T(8,128)(2,1)S(1)}, u32[]{:S(2)}, u32[]{:S(2)}) collective-permute-start(bf16[1,64,6144]{2,1,0:T(8,128)(2,1)} %get-tuple-element.16.refs_2_), channel_id=1, source_target_pairs={{0,1},{1,9},{4,5},{5,13},{8,0},{9,17},{12,4},{13,21},{16,8},{17,25... | collective-permute-start | bytes 2359304 | tf_op jit(solution)/shard_map/ppermute | solution.py:302
  10.5 1.7 %copy-start = (bf16[1,64,18432]{2,1,0:T(8,128)(2,1)S(1)}, bf16[1,64,18432]{2,1,0:T(8,128)(2,1)}, u32[]{:S(2)}) copy-start(bf16[1,64,18432]{2,1,0:T(8,128)(2,1)} %get-tuple-element.15.refs_1_.own_ref) | copy-start | bytes 7077892
  12.2 0.9 %copy-start.2 = (bf16[1,64,2048]{2,1,0:T(8,128)(2,1)S(1)}, bf16[1,64,2048]{2,1,0:T(8,128)(2,1)}, u32[]{:S(2)}) copy-start(bf16[1,64,2048]{2,1,0:T(8,128)(2,1)} %get-tuple-element.17.refs_3_.own_ref) | copy-start | bytes 786436
  19.1 28.8 %collective-permute-start.6 = (bf16[1,64,6144]{2,1,0:T(8,128)(2,1)}, bf16[1,64,6144]{2,1,0:T(8,128)(2,1)S(1)}, u32[]{:S(2)}, u32[]{:S(2)}) collective-permute-start(bf16[1,64,6144]{2,1,0:T(8,128)(2,1)} %get-tuple-element.16.refs_2_), channel_id=1, source_target_pairs={{1,5},{0,1},{4,0},{5,4},{9,13},{8,9},{12,8},{13,12},{17,21},{16,17... | collective-permute-start | bytes 2359304 | tf_op jit(solution)/shard_map/ppermute | solution.py:301
  20.4 4.3 %collective-permute-start.2 = (f32[136,128]{1,0:T(8,128)S(1)}, f32[136,128]{1,0:T(8,128)S(1)}, u32[]{:S(2)}, u32[]{:S(2)}) collective-permute-start(f32[136,128]{1,0:T(8,128)S(1)} %get-tuple-element.19), channel_id=1, source_target_pairs={{0,2},{2,0},{1,3},{3,1},{4,6},{6,4},{5,7},{7,5},{8,10},{10,8},{9,1... | collective-permute-start | bytes 208904 | tf_op jit(solution)/shard_map/ppermute | solution.py:310
  21.9 2.8 %copy-start.3 = (bf16[1,64,2048]{2,1,0:T(8,128)(2,1)S(1)}, bf16[1,64,2048]{2,1,0:T(8,128)(2,1)}, u32[]{:S(2)}) copy-start(bf16[1,64,2048]{2,1,0:T(8,128)(2,1)} %get-tuple-element.17.refs_3_.own_ref) | copy-start | bytes 786436
  21.9 2.8 %copy-start.5 = (s32[1,4]{1,0:T(1,128)S(1)}, s32[1,4]{1,0:T(1,128)}, u32[]{:S(2)}) copy-start(s32[1,4]{1,0:T(1,128)} %param.5) | copy-start | bytes 52
  21.9 17.7 %copy-start.1 = (bf16[1,64,18432]{2,1,0:T(8,128)(2,1)S(1)}, bf16[1,64,18432]{2,1,0:T(8,128)(2,1)}, u32[]{:S(2)}) copy-start(bf16[1,64,18432]{2,1,0:T(8,128)(2,1)} %get-tuple-element.15.refs_1_.own_ref) | copy-start | bytes 7077892
  24.8 26.0 %collective-permute-start.3 = (bf16[1,64,2048]{2,1,0:T(8,128)(2,1)S(1)}, bf16[1,64,2048]{2,1,0:T(8,128)(2,1)S(1)}, u32[]{:S(2)}, u32[]{:S(2)}) collective-permute-start(bf16[1,64,2048]{2,1,0:T(8,128)(2,1)S(1)} %copy-done.3), channel_id=1, source_target_pairs={{0,1},{1,9},{4,5},{5,13},{8,0},{9,17},{12,4},{13,21},{16,8},{17,25... | collective-permute-start | bytes 786440 | tf_op jit(solution)/shard_map/ppermute | solution.py:302
  39.6 11.1 %collective-permute-start.4 = (bf16[1,64,2048]{2,1,0:T(8,128)(2,1)S(1)}, bf16[1,64,2048]{2,1,0:T(8,128)(2,1)S(1)}, u32[]{:S(2)}, u32[]{:S(2)}) collective-permute-start(bf16[1,64,2048]{2,1,0:T(8,128)(2,1)S(1)} %copy-done.3), channel_id=1, source_target_pairs={{1,5},{0,1},{4,0},{5,4},{9,13},{8,9},{12,8},{13,12},{17,21},{16,17... | collective-permute-start | bytes 786440 | tf_op jit(solution)/shard_map/ppermute | solution.py:301
  51.7 4.4 %collective-permute-start.9 = (f32[136,128]{1,0:T(8,128)S(1)}, f32[136,128]{1,0:T(8,128)S(1)}, u32[]{:S(2)}, u32[]{:S(2)}) collective-permute-start(f32[136,128]{1,0:T(8,128)S(1)} %get-tuple-element.22), channel_id=1, source_target_pairs={{0,2},{2,0},{1,3},{3,1},{4,6},{6,4},{5,7},{7,5},{8,10},{10,8},{9,1... | collective-permute-start | bytes 208904 | tf_op jit(solution)/shard_map/ppermute | solution.py:332
  53.8 4.5 %collective-permute-start.11 = (f32[72,128]{1,0:T(8,128)S(1)}, f32[72,128]{1,0:T(8,128)S(1)}, u32[]{:S(2)}, u32[]{:S(2)}) collective-permute-start(f32[72,128]{1,0:T(8,128)S(1)} %get-tuple-element.23), channel_id=1, source_target_pairs={{0,4},{2,6},{4,0},{6,2},{8,12},{10,14},{12,8},{14,10},{16,20},{18,... | collective-permute-start | bytes 110600 | tf_op jit(solution)/shard_map/ppermute | solution.py:330
  55.5 4.9 %collective-permute-start.12 = (f32[72,128]{1,0:T(8,128)S(1)}, f32[72,128]{1,0:T(8,128)S(1)}, u32[]{:S(2)}, u32[]{:S(2)}) collective-permute-start(f32[72,128]{1,0:T(8,128)S(1)} %get-tuple-element.24), channel_id=1, source_target_pairs={{0,6},{2,4},{4,2},{6,0},{8,14},{10,12},{12,10},{14,8},{16,22},{18,... | collective-permute-start | bytes 110600 | tf_op jit(solution)/shard_map/ppermute | solution.py:330
  56.1 4.3 %collective-permute-start.10 = (f32[136,128]{1,0:T(8,128)S(1)}, f32[136,128]{1,0:T(8,128)S(1)}, u32[]{:S(2)}, u32[]{:S(2)}) collective-permute-start(f32[136,128]{1,0:T(8,128)S(1)} %add.36.kept_ref), channel_id=1, source_target_pairs={{1,0},{0,8},{5,4},{4,12},{9,1},{8,16},{13,5},{12,20},{17,9},{16,24... | collective-permute-start | bytes 208904 | tf_op jit(solution)/shard_map/ppermute | solution.py:335

commit v9 on v7

--- a/solution.py
+++ b/solution.py
@@ -13,7 +13,7 @@
 ROWS = 64
 UNITS = 16
 SIZES = (3, 9, 3, 1)
-STRIP = 2048
+STRIP = 1024
 NT = (((1,), (1,)), ((), ()))
 
 

time: 61.7 us -> 61.7 us (level)
  no operation moved by 1% of the time
where the time goes in v9:
time: 61.7 us; the launch traced here: 61.3 us
  Pallas kernels  23 us (37%)
  waiting for transfers between devices  20.5 us (33%)
  starting transfers between devices  13.6 us (22%)
  local copies, waits for them, and re-layouts  3.82 us (6%)
    ppermute x4, waiting for transfers between devices, sent(): return (lax.ppermute(piece, tm_pb, list(far_pairs())), near)  17 us
    pallas_call x4, Pallas kernels, chunk_part(): pl.pallas_call(functools.partial(chunk_kernel, start, before is None, las...  12.3 us
    pallas_call x1, Pallas kernels, own_part(): pl.pallas_call(own_kernel, in_specs=[vmem] * (1 + len(pieces)), out_specs...  5.98 us
    ppermute x4, starting transfers between devices, sent(): near = lax.ppermute(piece, tm_pb, list(near_pairs()))  4.74 us
    pallas_call x1, Pallas kernels, later_pieces(): pl.pallas_call(functools.partial(later_kernel, starts), in_specs=[pl.Bloc...  3.48 us
    unnamed x12, local copies, waits for them, and re-layouts  2.63 us
    ppermute x1, starting transfers between devices, shards(): lax.ppermute(here, tm_pb, [(source ^ 1, target ^ 1) for source, target in...  2.06 us
    ppermute x1, starting transfers between devices, shards(): beside = lax.ppermute(here_other, 'pix', [(0, 1), (1, 0)])  2.03 us
  transfers between devices with their start and end apart: 13, of which 7 were waited for; matrix products, arithmetic and copies ran while one was open for 0% of the time, Pallas kernels for 34%

profile of v9, /device:TPU:0, one launch (start us, length us, event | category | flops | bytes accessed | tf_op | source)
XLA Modules:
  0.0 61.3 jit_solution(14263624280925006523)
XLA Ops:
  0.0 1.2 %slice.21.refs_0_.own_ref = bf16[1,64,6144]{2,1,0:T(8,128)(2,1)S(1)} slice(bf16[1,64,32768]{2,1,0:T(8,128)(2,1)} %frames_ref.1), slice={[0:1], [0:64], [0:6144]} | slice | bytes 1572864 | tf_op jit(solution)/shard_map/slice | solution.py:306
  1.2 0.0 copy-start.4
  1.2 0.5 collective-permute-start
  1.7 2.1 %collective-permute-start.1 = (bf16[1,64,6144]{2,1,0:T(8,128)(2,1)S(1)}, bf16[1,64,6144]{2,1,0:T(8,128)(2,1)S(1)}, u32[]{:S(2)}, u32[]{:S(2)}) collective-permute-start(bf16[1,64,6144]{2,1,0:T(8,128)(2,1)S(1)} %slice.21.refs_0_.own_ref), channel_id=1, source_target_pairs={{1,5},{0,1},{4,0},{5,4},{9,13},{8,9},{12,8},{13,12},{17,21},{16,17... | collective-permute-start | bytes 2359304 | tf_op jit(solution)/shard_map/ppermute | solution.py:301
  3.8 3.5 %later_pieces.1 = (bf16[1,64,18432]{2,1,0:T(8,128)(2,1)}, bf16[1,64,6144]{2,1,0:T(8,128)(2,1)}, bf16[1,64,2048]{2,1,0:T(8,128)(2,1)}) custom-call(bf16[1,64,32768]{2,1,0:T(8,128)(2,1)} %frames_ref.1), custom_call_target="tpu_custom_call" | custom-call | tf_op jit(solution)/shard_map/later_pieces/pallas_call | solution.py:70
  7.3 1.3 %collective-permute-start.7 = (bf16[1,64,18432]{2,1,0:T(8,128)(2,1)}, bf16[1,64,18432]{2,1,0:T(8,128)(2,1)}, u32[]{:S(2)}, u32[]{:S(2)}) collective-permute-start(bf16[1,64,18432]{2,1,0:T(8,128)(2,1)} %get-tuple-element.15.refs_1_.own_ref), channel_id=1, source_target_pairs={{0,1},{1,9},{4,5},{5,13},{8,0},{9,17},{12,4},{13,21},{16,8},{17,25... | collective-permute-start | bytes 7077896 | tf_op jit(solution)/shard_map/ppermute | solution.py:302
  8.5 1.3 %collective-permute-start.8 = (bf16[1,64,18432]{2,1,0:T(8,128)(2,1)}, bf16[1,64,18432]{2,1,0:T(8,128)(2,1)}, u32[]{:S(2)}, u32[]{:S(2)}) collective-permute-start(bf16[1,64,18432]{2,1,0:T(8,128)(2,1)} %get-tuple-element.15.refs_1_.own_ref), channel_id=1, source_target_pairs={{1,5},{0,1},{4,0},{5,4},{9,13},{8,9},{12,8},{13,12},{17,21},{16,17... | collective-permute-start | bytes 7077896 | tf_op jit(solution)/shard_map/ppermute | solution.py:301
  9.8 0.0 collective-permute-start.5
  9.9 1.7 %copy-done = bf16[1,64,18432]{2,1,0:T(8,128)(2,1)S(1)} copy-done((bf16[1,64,18432]{2,1,0:T(8,128)(2,1)S(1)}, bf16[1,64,18432]{2,1,0:T(8,128)(2,1)}, u32[]{:S(2)}) %copy-start) | copy-done | bytes 2359320
  11.5 0.9 %copy-done.2 = bf16[1,64,2048]{2,1,0:T(8,128)(2,1)S(1)} copy-done((bf16[1,64,2048]{2,1,0:T(8,128)(2,1)S(1)}, bf16[1,64,2048]{2,1,0:T(8,128)(2,1)}, u32[]{:S(2)}) %copy-start.2) | copy-done | bytes 262168
  12.5 6.0 %own_tile_and_sums.1 = (f32[136,128]{1,0:T(8,128)S(1)}, bf16[1,64,6144]{2,1,0:T(8,128)(2,1)S(1)}) custom-call(s32[1,32768]{1,0:T(1,128)S(1)} %copy-done.4, bf16[1,64,6144]{2,1,0:T(8,128)(2,1)S(1)} %slice.21.refs_0_.own_ref, bf16[1,64,18432]{2,1,0:T(8,128)(2,1)S(1)} %copy-done, bf16[1,64,6144]{2,1,0:T(8,128)(2,1)} %get-tuple-element.16.refs_2_, ...), custom_call_target="tpu_custom_call" | custom-call | flops 8589934592 | bytes 16777216 | tf_op jit(solution)/shard_map/own_tile_and_sums/pallas_call | solution.py:109
  18.5 1.3 %collective-permute-start.6 = (bf16[1,64,6144]{2,1,0:T(8,128)(2,1)}, bf16[1,64,6144]{2,1,0:T(8,128)(2,1)S(1)}, u32[]{:S(2)}, u32[]{:S(2)}) collective-permute-start(bf16[1,64,6144]{2,1,0:T(8,128)(2,1)} %get-tuple-element.16.refs_2_), channel_id=1, source_target_pairs={{1,5},{0,1},{4,0},{5,4},{9,13},{8,9},{12,8},{13,12},{17,21},{16,17... | collective-permute-start | bytes 2359304 | tf_op jit(solution)/shard_map/ppermute | solution.py:301
  19.8 1.5 %collective-permute-start.2 = (f32[136,128]{1,0:T(8,128)S(1)}, f32[136,128]{1,0:T(8,128)S(1)}, u32[]{:S(2)}, u32[]{:S(2)}) collective-permute-start(f32[136,128]{1,0:T(8,128)S(1)} %get-tuple-element.19), channel_id=1, source_target_pairs={{0,2},{2,0},{1,3},{3,1},{4,6},{6,4},{5,7},{7,5},{8,10},{10,8},{9,1... | collective-permute-start | bytes 208904 | tf_op jit(solution)/shard_map/ppermute | solution.py:310
  21.3 1.9 %chunk_tiles.4.refs_0_ = f32[528,128]{1,0:T(8,128)S(1)} custom-call(bf16[1,64,6144]{2,1,0:T(8,128)(2,1)S(1)} %slice.21.refs_0_.own_ref, s32[1,32768]{1,0:T(1,128)S(1)} %copy-done.4, bf16[1,64,6144]{2,1,0:T(8,128)(2,1)S(1)} %collective-permute-done.far_ref, bf16[1,64,6144]{2,1,0:T(8,128)(2,1)S(1)} %collective-permute-done.1.near_ref, ...), custom_call_target="tpu_custom_call" | custom-call | flops 64424509440 | bytes 62914560 | tf_op jit(solution)/shard_map/chunk_tiles/pallas_call | solution.py:203
  23.1 0.9 %collective-permute-done.2 = f32[136,128]{1,0:T(8,128)S(1)} collective-permute-done((f32[136,128]{1,0:T(8,128)S(1)}, f32[136,128]{1,0:T(8,128)S(1)}, u32[]{:S(2)}, u32[]{:S(2)}) %collective-permute-start.2) | collective-permute-done | bytes 69664 | tf_op jit(solution)/shard_map/ppermute | solution.py:310
  24.1 0.0 collective-permute-start.3
  24.1 0.1 fusion.5
  24.2 15.3 %collective-permute-done.7.far_ref = bf16[1,64,18432]{2,1,0:T(8,128)(2,1)} collective-permute-done((bf16[1,64,18432]{2,1,0:T(8,128)(2,1)}, bf16[1,64,18432]{2,1,0:T(8,128)(2,1)}, u32[]{:S(2)}, u32[]{:S(2)}) %collective-permute-start.7) | collective-permute-done | bytes 2359328 | tf_op jit(solution)/shard_map/ppermute | solution.py:302
  39.6 7.6 %chunk_tiles.5.refs_0_ = f32[528,128]{1,0:T(8,128)S(1)} custom-call(bf16[1,64,18432]{2,1,0:T(8,128)(2,1)S(1)} %copy-done.1, s32[1,32768]{1,0:T(1,128)S(1)} %copy-done.4, bf16[1,64,18432]{2,1,0:T(8,128)(2,1)} %collective-permute-done.7.far_ref, bf16[1,64,18432]{2,1,0:T(8,128)(2,1)} %collective-permute-done.8.near_ref, f32[528,128]{1,0:T(8,128)S(1)} %chunk_tiles.4.refs_0_, ...), custom_call_target="tpu_custom_call" | custom-call | flops 9663676416 | bytes 9437184 | tf_op jit(solution)/shard_map/chunk_tiles/pallas_call | solution.py:203
  47.2 0.7 %collective-permute-done.5.far_ref = bf16[1,64,6144]{2,1,0:T(8,128)(2,1)S(1)} collective-permute-done((bf16[1,64,6144]{2,1,0:T(8,128)(2,1)}, bf16[1,64,6144]{2,1,0:T(8,128)(2,1)S(1)}, u32[]{:S(2)}, u32[]{:S(2)}) %collective-permute-start.5) | collective-permute-done | bytes 786464 | tf_op jit(solution)/shard_map/ppermute | solution.py:302
  47.9 1.9 %chunk_tiles.6.refs_0_ = f32[528,128]{1,0:T(8,128)S(1)} custom-call(bf16[1,64,6144]{2,1,0:T(8,128)(2,1)S(1)} %get-tuple-element.20.own_ref, s32[1,32768]{1,0:T(1,128)S(1)} %copy-done.4, bf16[1,64,6144]{2,1,0:T(8,128)(2,1)S(1)} %collective-permute-done.5.far_ref, bf16[1,64,6144]{2,1,0:T(8,128)(2,1)S(1)} %collective-permute-done.6.near_ref, ...), custom_call_target="tpu_custom_call" | custom-call | flops 3221225472 | bytes 3145728 | tf_op jit(solution)/shard_map/chunk_tiles/pallas_call | solution.py:203
  49.8 0.9 %collective-permute-done.3.far_ref = bf16[1,64,2048]{2,1,0:T(8,128)(2,1)S(1)} collective-permute-done((bf16[1,64,2048]{2,1,0:T(8,128)(2,1)S(1)}, bf16[1,64,2048]{2,1,0:T(8,128)(2,1)S(1)}, u32[]{:S(2)}, u32[]{:S(2)}) %collective-permute-start.3) | collective-permute-done | bytes 262176 | tf_op jit(solution)/shard_map/ppermute | solution.py:302
  50.7 1.0 %chunk_tiles.7 = (f32[136,128]{1,0:T(8,128)S(1)}, f32[136,128]{1,0:T(8,128)S(1)}, f32[72,128]{1,0:T(8,128)S(1)}, f32[72,128]{1,0:T(8,128)S(1)}) custom-call(bf16[1,64,2048]{2,1,0:T(8,128)(2,1)S(1)} %copy-done.3, s32[1,32768]{1,0:T(1,128)S(1)} %copy-done.4, bf16[1,64,2048]{2,1,0:T(8,128)(2,1)S(1)} %collective-permute-done.3.far_ref, ...), custom_call_target="tpu_custom_call" | custom-call | flops 1073741824 | bytes 1048576 | tf_op jit(solution)/shard_map/chunk_tiles/pallas_call | solution.py:203
  51.7 2.0 %collective-permute-start.9 = (f32[136,128]{1,0:T(8,128)S(1)}, f32[136,128]{1,0:T(8,128)S(1)}, u32[]{:S(2)}, u32[]{:S(2)}) collective-permute-start(f32[136,128]{1,0:T(8,128)S(1)} %get-tuple-element.22), channel_id=1, source_target_pairs={{0,2},{2,0},{1,3},{3,1},{4,6},{6,4},{5,7},{7,5},{8,10},{10,8},{9,1... | collective-permute-start | bytes 208904 | tf_op jit(solution)/shard_map/ppermute | solution.py:332
  53.8 1.3 %collective-permute-start.11 = (f32[72,128]{1,0:T(8,128)S(1)}, f32[72,128]{1,0:T(8,128)S(1)}, u32[]{:S(2)}, u32[]{:S(2)}) collective-permute-start(f32[72,128]{1,0:T(8,128)S(1)} %get-tuple-element.23), channel_id=1, source_target_pairs={{0,4},{2,6},{4,0},{6,2},{8,12},{10,14},{12,8},{14,10},{16,20},{18,... | collective-permute-start | bytes 110600 | tf_op jit(solution)/shard_map/ppermute | solution.py:330
  55.1 0.3 collective-permute-start.12
  55.3 0.7 %collective-permute-done.9 = f32[136,128]{1,0:T(8,128)S(1)} collective-permute-done((f32[136,128]{1,0:T(8,128)S(1)}, f32[136,128]{1,0:T(8,128)S(1)}, u32[]{:S(2)}, u32[]{:S(2)}) %collective-permute-start.9) | collective-permute-done | bytes 69664 | tf_op jit(solution)/shard_map/ppermute | solution.py:332
  56.1 2.1 %collective-permute-start.10 = (f32[136,128]{1,0:T(8,128)S(1)}, f32[136,128]{1,0:T(8,128)S(1)}, u32[]{:S(2)}, u32[]{:S(2)}) collective-permute-start(f32[136,128]{1,0:T(8,128)S(1)} %add.36.kept_ref), channel_id=1, source_target_pairs={{1,0},{0,8},{5,4},{4,12},{9,1},{8,16},{13,5},{12,20},{17,9},{16,24... | collective-permute-start | bytes 208904 | tf_op jit(solution)/shard_map/ppermute | solution.py:335
  58.2 0.1 pad_maximum_fusion.factor_ref
  58.3 1.7 %collective-permute-done.12.other_ref = f32[72,128]{1,0:T(8,128)S(1)} collective-permute-done((f32[72,128]{1,0:T(8,128)S(1)}, f32[72,128]{1,0:T(8,128)S(1)}, u32[]{:S(2)}, u32[]{:S(2)}) %collective-permute-start.12) | collective-permute-done | bytes 36896 | tf_op jit(solution)/shard_map/ppermute | solution.py:330
  59.9 0.2 collective-permute-done.10.here_ref
  60.1 1.2 %normalise_and_skew.1 = f32[1,4,64,64]{3,2,1,0:T(8,128)} custom-call(f32[128,128]{1,0:T(8,128)S(1)} %pad_maximum_fusion.factor_ref, f32[136,128]{1,0:T(8,128)S(1)} %add.35.refs_1_.own_ref, f32[136,128]{1,0:T(8,128)S(1)} %add.36.kept_ref, f32[136,128]{1,0:T(8,128)S(1)} %collective-permute-done.10.here_ref, f32[72,128]{1,0:T(8,128)S(1)} %collective-permute-done.11.same_ref, ...), custom_call_target="tpu_custom_call" | custom-call | tf_op jit(solution)/shard_map/normalise_and_skew/pallas_call | solution.py:260
  (22 shorter events, 0.1 us)
Async XLA Ops:
  1.2 8.7 %copy-start.4 = (s32[1,32768]{1,0:T(1,128)S(1)}, s32[1,32768]{1,0:T(1,128)}, u32[]{:S(2)}) copy-start(s32[1,32768]{1,0:T(1,128)} %label_ref.9) | copy-start | bytes 393220
  1.2 17.3 %collective-permute-start = (bf16[1,64,6144]{2,1,0:T(8,128)(2,1)S(1)}, bf16[1,64,6144]{2,1,0:T(8,128)(2,1)S(1)}, u32[]{:S(2)}, u32[]{:S(2)}) collective-permute-start(bf16[1,64,6144]{2,1,0:T(8,128)(2,1)S(1)} %slice.21.refs_0_.own_ref), channel_id=1, source_target_pairs={{0,1},{1,9},{4,5},{5,13},{8,0},{9,17},{12,4},{13,21},{16,8},{17,25... | collective-permute-start | bytes 2359304 | tf_op jit(solution)/shard_map/ppermute | solution.py:302
  1.7 18.1 %collective-permute-start.1 = (bf16[1,64,6144]{2,1,0:T(8,128)(2,1)S(1)}, bf16[1,64,6144]{2,1,0:T(8,128)(2,1)S(1)}, u32[]{:S(2)}, u32[]{:S(2)}) collective-permute-start(bf16[1,64,6144]{2,1,0:T(8,128)(2,1)S(1)} %slice.21.refs_0_.own_ref), channel_id=1, source_target_pairs={{1,5},{0,1},{4,0},{5,4},{9,13},{8,9},{12,8},{13,12},{17,21},{16,17... | collective-permute-start | bytes 2359304 | tf_op jit(solution)/shard_map/ppermute | solution.py:301
  7.3 32.3 %collective-permute-start.7 = (bf16[1,64,18432]{2,1,0:T(8,128)(2,1)}, bf16[1,64,18432]{2,1,0:T(8,128)(2,1)}, u32[]{:S(2)}, u32[]{:S(2)}) collective-permute-start(bf16[1,64,18432]{2,1,0:T(8,128)(2,1)} %get-tuple-element.15.refs_1_.own_ref), channel_id=1, source_target_pairs={{0,1},{1,9},{4,5},{5,13},{8,0},{9,17},{12,4},{13,21},{16,8},{17,25... | collective-permute-start | bytes 7077896 | tf_op jit(solution)/shard_map/ppermute | solution.py:302
  8.5 31.1 %collective-permute-start.8 = (bf16[1,64,18432]{2,1,0:T(8,128)(2,1)}, bf16[1,64,18432]{2,1,0:T(8,128)(2,1)}, u32[]{:S(2)}, u32[]{:S(2)}) collective-permute-start(bf16[1,64,18432]{2,1,0:T(8,128)(2,1)} %get-tuple-element.15.refs_1_.own_ref), channel_id=1, source_target_pairs={{1,5},{0,1},{4,0},{5,4},{9,13},{8,9},{12,8},{13,12},{17,21},{16,17... | collective-permute-start | bytes 7077896 | tf_op jit(solution)/shard_map/ppermute | solution.py:301
  9.8 38.1 %collective-permute-start.5 = (bf16[1,64,6144]{2,1,0:T(8,128)(2,1)}, bf16[1,64,6144]{2,1,0:T(8,128)(2,1)S(1)}, u32[]{:S(2)}, u32[]{:S(2)}) collective-permute-start(bf16[1,64,6144]{2,1,0:T(8,128)(2,1)} %get-tuple-element.16.refs_2_), channel_id=1, source_target_pairs={{0,1},{1,9},{4,5},{5,13},{8,0},{9,17},{12,4},{13,21},{16,8},{17,25... | collective-permute-start | bytes 2359304 | tf_op jit(solution)/shard_map/ppermute | solution.py:302
  9.8 1.7 %copy-start = (bf16[1,64,18432]{2,1,0:T(8,128)(2,1)S(1)}, bf16[1,64,18432]{2,1,0:T(8,128)(2,1)}, u32[]{:S(2)}) copy-start(bf16[1,64,18432]{2,1,0:T(8,128)(2,1)} %get-tuple-element.15.refs_1_.own_ref) | copy-start | bytes 7077892
  11.5 0.9 %copy-start.2 = (bf16[1,64,2048]{2,1,0:T(8,128)(2,1)S(1)}, bf16[1,64,2048]{2,1,0:T(8,128)(2,1)}, u32[]{:S(2)}) copy-start(bf16[1,64,2048]{2,1,0:T(8,128)(2,1)} %get-tuple-element.17.refs_3_.own_ref) | copy-start | bytes 786436
  18.5 29.5 %collective-permute-start.6 = (bf16[1,64,6144]{2,1,0:T(8,128)(2,1)}, bf16[1,64,6144]{2,1,0:T(8,128)(2,1)S(1)}, u32[]{:S(2)}, u32[]{:S(2)}) collective-permute-start(bf16[1,64,6144]{2,1,0:T(8,128)(2,1)} %get-tuple-element.16.refs_2_), channel_id=1, source_target_pairs={{1,5},{0,1},{4,0},{5,4},{9,13},{8,9},{12,8},{13,12},{17,21},{16,17... | collective-permute-start | bytes 2359304 | tf_op jit(solution)/shard_map/ppermute | solution.py:301
  19.8 4.3 %collective-permute-start.2 = (f32[136,128]{1,0:T(8,128)S(1)}, f32[136,128]{1,0:T(8,128)S(1)}, u32[]{:S(2)}, u32[]{:S(2)}) collective-permute-start(f32[136,128]{1,0:T(8,128)S(1)} %get-tuple-element.19), channel_id=1, source_target_pairs={{0,2},{2,0},{1,3},{3,1},{4,6},{6,4},{5,7},{7,5},{8,10},{10,8},{9,1... | collective-permute-start | bytes 208904 | tf_op jit(solution)/shard_map/ppermute | solution.py:310
  21.3 2.8 %copy-start.3 = (bf16[1,64,2048]{2,1,0:T(8,128)(2,1)S(1)}, bf16[1,64,2048]{2,1,0:T(8,128)(2,1)}, u32[]{:S(2)}) copy-start(bf16[1,64,2048]{2,1,0:T(8,128)(2,1)} %get-tuple-element.17.refs_3_.own_ref) | copy-start | bytes 786436
  21.3 2.8 %copy-start.5 = (s32[1,4]{1,0:T(1,128)S(1)}, s32[1,4]{1,0:T(1,128)}, u32[]{:S(2)}) copy-start(s32[1,4]{1,0:T(1,128)} %param.5) | copy-start | bytes 52
  21.3 18.3 %copy-start.1 = (bf16[1,64,18432]{2,1,0:T(8,128)(2,1)S(1)}, bf16[1,64,18432]{2,1,0:T(8,128)(2,1)}, u32[]{:S(2)}) copy-start(bf16[1,64,18432]{2,1,0:T(8,128)(2,1)} %get-tuple-element.15.refs_1_.own_ref) | copy-start | bytes 7077892
  24.1 26.6 %collective-permute-start.3 = (bf16[1,64,2048]{2,1,0:T(8,128)(2,1)S(1)}, bf16[1,64,2048]{2,1,0:T(8,128)(2,1)S(1)}, u32[]{:S(2)}, u32[]{:S(2)}) collective-permute-start(bf16[1,64,2048]{2,1,0:T(8,128)(2,1)S(1)} %copy-done.3), channel_id=1, source_target_pairs={{0,1},{1,9},{4,5},{5,13},{8,0},{9,17},{12,4},{13,21},{16,8},{17,25... | collective-permute-start | bytes 786440 | tf_op jit(solution)/shard_map/ppermute | solution.py:302
  39.6 11.1 %collective-permute-start.4 = (bf16[1,64,2048]{2,1,0:T(8,128)(2,1)S(1)}, bf16[1,64,2048]{2,1,0:T(8,128)(2,1)S(1)}, u32[]{:S(2)}, u32[]{:S(2)}) collective-permute-start(bf16[1,64,2048]{2,1,0:T(8,128)(2,1)S(1)} %copy-done.3), channel_id=1, source_target_pairs={{1,5},{0,1},{4,0},{5,4},{9,13},{8,9},{12,8},{13,12},{17,21},{16,17... | collective-permute-start | bytes 786440 | tf_op jit(solution)/shard_map/ppermute | solution.py:301
  51.7 4.4 %collective-permute-start.9 = (f32[136,128]{1,0:T(8,128)S(1)}, f32[136,128]{1,0:T(8,128)S(1)}, u32[]{:S(2)}, u32[]{:S(2)}) collective-permute-start(f32[136,128]{1,0:T(8,128)S(1)} %get-tuple-element.22), channel_id=1, source_target_pairs={{0,2},{2,0},{1,3},{3,1},{4,6},{6,4},{5,7},{7,5},{8,10},{10,8},{9,1... | collective-permute-start | bytes 208904 | tf_op jit(solution)/shard_map/ppermute | solution.py:332
  53.8 4.5 %collective-permute-start.11 = (f32[72,128]{1,0:T(8,128)S(1)}, f32[72,128]{1,0:T(8,128)S(1)}, u32[]{:S(2)}, u32[]{:S(2)}) collective-permute-start(f32[72,128]{1,0:T(8,128)S(1)} %get-tuple-element.23), channel_id=1, source_target_pairs={{0,4},{2,6},{4,0},{6,2},{8,12},{10,14},{12,8},{14,10},{16,20},{18,... | collective-permute-start | bytes 110600 | tf_op jit(solution)/shard_map/ppermute | solution.py:330
  55.1 4.9 %collective-permute-start.12 = (f32[72,128]{1,0:T(8,128)S(1)}, f32[72,128]{1,0:T(8,128)S(1)}, u32[]{:S(2)}, u32[]{:S(2)}) collective-permute-start(f32[72,128]{1,0:T(8,128)S(1)} %get-tuple-element.24), channel_id=1, source_target_pairs={{0,6},{2,4},{4,2},{6,0},{8,14},{10,12},{12,10},{14,8},{16,22},{18,... | collective-permute-start | bytes 110600 | tf_op jit(solution)/shard_map/ppermute | solution.py:330
  56.1 4.0 %collective-permute-start.10 = (f32[136,128]{1,0:T(8,128)S(1)}, f32[136,128]{1,0:T(8,128)S(1)}, u32[]{:S(2)}, u32[]{:S(2)}) collective-permute-start(f32[136,128]{1,0:T(8,128)S(1)} %add.36.kept_ref), channel_id=1, source_target_pairs={{1,0},{0,8},{5,4},{4,12},{9,1},{8,16},{13,5},{12,20},{17,9},{16,24... | collective-permute-start | bytes 208904 | tf_op jit(solution)/shard_map/ppermute | solution.py:335
